TPU v7x, 32 devices: a whole 2x2x4 slice. The times are simulated.
32 devices in a mesh: pack: 4 (over y, x), blk: 4 (over z), head: 2 (over core).
Axes of the slice: x: 2, y: 2, z: 4, core: 2. Of those that a mesh axis runs over, the one named last changes fastest.
Arguments:
- tokens_full: bfloat16 [4, 3072, 1152], P('pack', 'blk'), may hold values from -6 to 6
- condition: bfloat16 [4, 9, 1152], P('pack'), may hold values from -6 to 6
- kept_index: int32 [4, 1536], P('pack', 'blk'), may hold values from 0 to 3071, as said below
- segment_ids: int32 [4, 1536], P('pack'), may hold values from 0 to 8, as said below
- cotangent: bfloat16 [4, 3072, 1152], P('pack', 'blk'), may hold values from -6 to 6
- qkv_weight: bfloat16 [1152, 3, 1152], P(None, None, 'head'), may hold values from -0.1875 to 0.1875
- query_value_bias: bfloat16 [2, 1152], P(None, 'head'), may hold values from -3 to 3
- output_weight: bfloat16 [1152, 1152], P('head'), may hold values from -2 to 2
- output_bias: bfloat16 [1152], replicated, may hold values from -2 to 2
- hidden_weight: bfloat16 [1152, 4608], P(None, 'head'), may hold values from -0.1875 to 0.1875
- hidden_bias: bfloat16 [4608], P('head'), may hold values from -2 to 2
- down_weight: bfloat16 [4608, 1152], P('head'), may hold values from -0.09375 to 0.09375
- down_bias: bfloat16 [1152], replicated, may hold values from -2 to 2
- modulation_weight: bfloat16 [1152, 6, 1152], P(None, None, 'head'), may hold values from -0.1875 to 0.1875
- modulation_bias: bfloat16 [6, 1152], P(None, 'head'), may hold values from -2 to 2
Outputs:
- block_output: bfloat16 [4, 3072, 1152], P('pack', 'blk')
- tokens_grad: bfloat16 [4, 3072, 1152], P('pack', 'blk')
- condition_grad: float32 [4, 9, 1152], P('pack')
- qkv_weight_grad: float32 [1152, 3, 1152], P('blk', None, 'head')
- query_value_bias_grad: float32 [2, 1152], P(None, 'head')
- output_weight_grad: float32 [1152, 1152], P('head', 'blk')
- output_bias_grad: float32 [1152], replicated
- hidden_weight_grad: float32 [1152, 4608], P('blk', 'head')
- hidden_bias_grad: float32 [4608], P('head')
- down_weight_grad: float32 [4608, 1152], P('head', 'blk')
- down_bias_grad: float32 [1152], replicated
- modulation_weight_grad: float32 [1152, 6, 1152], P('blk', None, 'head')
- modulation_bias_grad: float32 [6, 1152], P(None, 'head')
Inputs may be any that keep to these rules, and one draw needn't show every extreme that they name: `kept_index`: within a pack, the kept tokens j * 384 to (j + 1) * 384 - 1 hold distinct positions from 2 * j * 384 to 2 * (j + 1) * 384 - 1; the first block keeps position 0 and the last keeps the pack's last position. `segment_ids`: each pack is 1 latents of 512 kept tokens and the others of 128, in an order drawn per pack; the ids never fall along a pack, and each id from 0 to 8 names one latent.
All inputs are finite; a program needn't handle non-finite values.
Results may differ from a plain program's by a relative error of at most 0.015.
The roundings to bfloat16 on the way count: a program that leaves them out, or rounds other values in their place, can miss the bound.
Values may be sent and summed in bfloat16 or wider, within the bound.
No kernel may reach another device: no remote copies, remote signals or barrier semaphores. Data moves between devices by JAX's collectives and lax.ppermute only.
A program may use at most 320 MiB of HBM per device.

v0:
```python
import math

import jax
import jax.numpy as jnp
from jax import lax
from jax.experimental import pallas as pl
from jax.experimental.pallas import tpu as pltpu
from jax.sharding import PartitionSpec as P

HEAD_DIM = 72
SHORT = 128
LONG = 4 * SHORT
LANES = 128
EPSILON = 1e-06
FACTOR = 1.0 / math.sqrt(HEAD_DIM)
FACTOR_LOG2 = FACTOR * math.log2(math.e)
GELU_SLOPE = math.sqrt(2.0 / math.pi)
GELU_CUBE = 0.044715
F32 = jnp.float32
BF16 = jnp.bfloat16
ROWS_BY_ROWS = (((1,), (1,)), ((), ()))
COLUMNS_BY_COLUMNS = (((0,), (0,)), ((), ()))
VMEM = pl.BlockSpec(memory_space=pltpu.VMEM)
SMEM = pl.BlockSpec(memory_space=pltpu.SMEM)


def bf_dot(operand_a, operand_b):
    return jnp.dot(operand_a, operand_b, preferred_element_type=F32)


def dot_by(dims, operand_a, operand_b):
    return lax.dot_general(operand_a, operand_b, dims, preferred_element_type=F32)


def array(shape, kind):
    return jax.ShapeDtypeStruct(shape, kind)


SLOW = 1000


def kernel_call(
    body, name, outs, args, flops, grid=(), in_specs=None, out_specs=None, scratch=(), vmem=56
):
    moved = sum(math.prod(a.shape) * a.dtype.itemsize for a in (*args, *outs))
    return pl.pallas_call(
        body,
        name=name,
        out_shape=tuple(outs),
        grid=grid,
        in_specs=in_specs or [VMEM] * len(args),
        out_specs=out_specs or (VMEM,) * len(outs),
        scratch_shapes=scratch,
        compiler_params=pltpu.CompilerParams(vmem_limit_bytes=vmem << 20),
        cost_estimate=pl.CostEstimate(
            flops=int(flops) // SLOW, bytes_accessed=int(moved) // SLOW, transcendentals=0
        ),
    )(*args)


def aligned(index, to=LANES):
    return pl.multiple_of(index, to)


def layer_norm(values):
    center = values - jnp.mean(values, axis=-1, keepdims=True)
    spread = jnp.mean(center * center, axis=-1, keepdims=True)
    inverse = lax.rsqrt(spread + EPSILON)
    return (center * inverse, inverse)


def norm_back(upstream, normed, inverse):
    mean_grad = jnp.mean(upstream, axis=-1, keepdims=True)
    mean_cross = jnp.mean(upstream * normed, axis=-1, keepdims=True)
    return inverse * (upstream - mean_grad - normed * mean_cross)


def gelu_pair(value):
    square = value * value
    bent = jnp.tanh(GELU_SLOPE * (value + GELU_CUBE * (value * square)))
    half = 0.5 * (1.0 + bent)
    slope = GELU_SLOPE * (1.0 + (3.0 * GELU_CUBE) * square)
    return value * half, half + 0.5 * value * (1.0 - bent * bent) * slope


def plan_body(longs, packs, starts, place_ref, segments, out_ref):
    core, blk, pack, blocks = (place_ref[number] for number in range(4))
    places = 3
    out_ref[0] = core
    out_ref[1] = blk
    for entry in range(packs):
        window = jnp.bitwise_xor(pack, entry)
        start = jnp.int32(0)
        for number in range(packs):
            start = jnp.where(window == number, starts[number], start)
        out_ref[2 + entry] = start
    out_ref[2 + packs] = pack
    near = []
    for number in range(3 * places):
        index = (blk - 1) * places + number
        inside = jnp.logical_and(index >= 0, index < blocks * places)
        found = segments[jnp.clip(index, 0, blocks * places - 1) * SHORT]
        near.append(jnp.where(inside, found, -1))
    reaches_low = near[places - 1] == near[places]
    reaches_high = near[2 * places - 1] == near[2 * places]
    base = 3 + packs
    firsts, lengths = [], []
    for place in range(places):
        own = near[places + place]
        first = jnp.int32(0)
        length = jnp.int32(0)
        for number in reversed(range(3 * places)):
            same = near[number] == own
            first = jnp.where(same, number, first)
            length = length + same.astype(jnp.int32)
        firsts.append(first)
        lengths.append((length > 1).astype(jnp.int32))
    out_ref[base] = jnp.where(reaches_low, 0, 2 * places * SHORT)
    out_ref[base + 1] = jnp.where(reaches_low, firsts[0], -1)
    out_ref[base + 2] = jnp.where(reaches_high, firsts[-1], -1)
    for place in range(places):
        out_ref[base + 3 + place] = firsts[place]
        out_ref[base + 3 + places + place] = lengths[place]
        out_ref[base + 3 + 2 * places + place] = near[places + place]
    beside = near[:places] + near[2 * places :]
    if longs == 1:
        beside = [
            jnp.where(reaches_low, low, high)
            for low, high in zip(near[:places], near[2 * places :])
        ]
    for number, segment in enumerate(beside):
        out_ref[base + 3 + 3 * places + number] = jnp.maximum(segment, 0)
    out_ref[base + 3 + 3 * places + len(beside)] = reaches_low.astype(jnp.int32)


def plan(longs, packs, starts, place, segments):
    beside = 3 if longs == 1 else 6
    size = 3 + packs + 3 + 9 + beside + 1
    return kernel_call(
        lambda *refs: plan_body(longs, packs, starts, *refs),
        "plan",
        [array((size,), jnp.int32)],
        [place, segments],
        0,
        in_specs=[SMEM, SMEM],
        out_specs=(SMEM,),
    )[0]


def pick_body(first, scalars, own_ref, other_ref, out_ref):
    half = own_ref.shape[2]
    core = scalars[0]
    for place in range(out_ref.shape[0]):
        segment = scalars[first + place]

        def write(low, high):
            out_ref[place, :, :half] = low[segment]
            out_ref[place, :, half:] = high[segment]

        pl.when(core == 0)(lambda: write(own_ref, other_ref))
        pl.when(core == 1)(lambda: write(other_ref, own_ref))


def pick(scalars, first, own, other, count):
    shape = (count, own.shape[1], 2 * own.shape[2])
    return kernel_call(
        lambda *refs: pick_body(first, *refs),
        "pick",
        [array(shape, F32)],
        [scalars, own, other],
        0,
        in_specs=[SMEM, VMEM, VMEM],
    )[0]


def norm_body(scalars, own_ref, near_ref, up_ref, mod_ref, hidden_ref, down_in_ref, shares_ref):
    step = pl.program_id(0)
    places = 3
    half = shares_ref.shape[1] // 2
    shift, scale = mod_ref[0, 0:1], mod_ref[0, 1:2]

    def write(rows):
        normed, _ = layer_norm(rows.astype(F32))
        hidden_ref[...] = (normed * (1.0 + scale) + shift).astype(BF16)

    @pl.when(step < places)
    def _():
        write(own_ref[...])
        down_in_ref[...] = (mod_ref[0, 5:6] * up_ref[...].astype(F32)).astype(BF16)
        start = aligned(scalars[0] * (hidden_ref.shape[1] - half))
        shares_ref[:, :half] = down_in_ref[:, pl.ds(start, half)]
        shares_ref[:, half:] = hidden_ref[:, pl.ds(start, half)]

    pl.when(step >= places)(lambda: write(near_ref[...]))


def norm(scalars, own, near, upstream, mod_places):
    count, width = own.shape
    places = count // SHORT
    total = count + near.shape[0]
    share = 2 * half_width(width)

    def own_place(i):
        return (jnp.minimum(i, places - 1), 0)

    return kernel_call(
        norm_body,
        "norm",
        [array((total, width), BF16), array((count, width), BF16), array((count, share), BF16)],
        [scalars, own, near, upstream, mod_places],
        0,
        grid=(total // SHORT,),
        in_specs=[
            SMEM,
            pl.BlockSpec((SHORT, width), own_place),
            pl.BlockSpec((SHORT, width), lambda i: (jnp.maximum(i - places, 0), 0)),
            pl.BlockSpec((SHORT, width), own_place),
            pl.BlockSpec((1, *mod_places.shape[1:]), lambda i: (i, 0, 0)),
        ],
        out_specs=(
            pl.BlockSpec((SHORT, width), lambda i: (i, 0)),
            pl.BlockSpec((SHORT, width), own_place),
            pl.BlockSpec((SHORT, share), own_place),
        ),
    )


def lay_beside(buffer, own, beside, table):
    count = own.shape[0]
    buffer[count : 2 * count] = own
    if beside.shape[0] == count:
        buffer[pl.ds(aligned(table[0], SHORT), count)] = beside
    else:
        buffer[:count] = beside[:count]
        buffer[2 * count :] = beside[count:]


def attend_body(base, scalars, rows_ref, weight_ref, attended_ref, branch_ref, keys, values, turned):
    count, own_width = attended_ref.shape
    places = count // SHORT
    table = [scalars[base + number] for number in range(3)]
    lay_beside(keys, rows_ref[1, :count], rows_ref[1, count:], table)
    lay_beside(values, rows_ref[2, :count], rows_ref[2, count:], table)

    def attend(place, size):
        near = pl.ds(aligned(scalars[base + 3 + place] * SHORT, SHORT), size)
        rows = pl.ds(aligned(place * SHORT, SHORT), SHORT)
        for head in range(own_width // HEAD_DIM):
            columns = pl.ds(head * HEAD_DIM, HEAD_DIM)
            scores = dot_by(ROWS_BY_ROWS, keys[near, columns], rows_ref[0, rows, columns])
            peak = jnp.max(scores, axis=0, keepdims=True)
            exponent = jnp.exp2((scores - peak) * FACTOR_LOG2)
            total = jnp.sum(exponent, axis=0, keepdims=True)
            probs = (exponent * (1.0 / total)).astype(BF16)
            turned[columns] = dot_by(COLUMNS_BY_COLUMNS, values[near, columns], probs)
        attended_ref[rows] = turned[...].T.astype(BF16)

    def one_place(place, carry):
        is_long = scalars[base + 3 + places + place]
        pl.when(is_long == 1)(lambda: attend(place, LONG))
        pl.when(is_long == 0)(lambda: attend(place, SHORT))
        return carry

    lax.fori_loop(0, places, one_place, 0)
    branch_ref[...] = bf_dot(attended_ref[...], weight_ref[...])


def attend(base, scalars, rows, weight, count):
    own_width, width = weight.shape
    return kernel_call(
        lambda *refs: attend_body(base, *refs),
        "attend",
        [array((count, own_width), BF16), array((count, width), F32)],
        [scalars, rows, weight],
        2 * count * own_width * (width + 2 * LONG),
        in_specs=[SMEM, VMEM, VMEM],
        scratch=[
            pltpu.VMEM((3 * count, own_width), BF16),
            pltpu.VMEM((3 * count, own_width), BF16),
            pltpu.VMEM((own_width, SHORT), F32),
        ],
    )


def attend_back_body(base, scalars, rows_ref, grad_ref, near_grad_ref, weight_ref, *rest):
    hidden_grad_ref, bias_ref, pieces = rest[0], rest[1], rest[2:-3]
    held, grads, split = rest[-3:]
    count, own_width = grad_ref.shape
    places = count // SHORT
    table = [scalars[base + number] for number in range(3)]
    for number in range(3):
        lay_beside(held.at[number], rows_ref[number, :count], rows_ref[number, count:], table)
    lay_beside(held.at[3], grad_ref[...], near_grad_ref[...], table)

    def attend_back(first, size):
        rows = pl.ds(aligned(first * SHORT, SHORT), size)
        for head in range(own_width // HEAD_DIM):
            columns = pl.ds(head * HEAD_DIM, HEAD_DIM)
            query, key, value, grad = (held[number, rows, columns] for number in range(4))
            scores = dot_by(ROWS_BY_ROWS, key, query)
            peak = jnp.max(scores, axis=0, keepdims=True)
            exponent = jnp.exp2((scores - peak) * FACTOR_LOG2)
            probs = exponent * (1.0 / jnp.sum(exponent, axis=0, keepdims=True))
            probs_grad = dot_by(ROWS_BY_ROWS, value, grad)
            row_dot = jnp.sum(probs * probs_grad, axis=0, keepdims=True)
            score_grad = (probs * (probs_grad - row_dot)).astype(BF16)
            query_grad = dot_by(COLUMNS_BY_COLUMNS, score_grad, key) * FACTOR
            grads[0, rows, columns] = query_grad.astype(BF16)
            grads[1, rows, columns] = (bf_dot(score_grad, query) * FACTOR).astype(BF16)
            grads[2, rows, columns] = bf_dot(probs.astype(BF16), grad).astype(BF16)

    def short_latent(place, carry):
        is_long = scalars[base + 3 + places + place]
        pl.when(is_long == 0)(lambda: attend_back(places + place, SHORT))
        return carry

    lax.fori_loop(0, places, short_latent, 0)

    def long_latent(number, carry):
        first = scalars[base + 1 + number]
        pl.when(first >= 0)(lambda: attend_back(first, LONG))
        return carry

    lax.fori_loop(0, 2, long_latent, 0)
    own_grads = [grads[number, count : 2 * count] for number in range(3)]
    total = bf_dot(own_grads[0], weight_ref[0])
    for number in range(1, 3):
        total = total + bf_dot(own_grads[number], weight_ref[number])
    hidden_grad_ref[...] = total.astype(BF16)
    for number, grad in enumerate((own_grads[0], own_grads[2])):
        bias_ref[number : number + 1] = jnp.sum(grad.astype(F32), axis=0, keepdims=True)
    share = own_width // len(pieces)
    for number in range(len(pieces)):
        for part in range(3):
            split[number, :, part * share : (part + 1) * share] = own_grads[part][
                :, number * share : (number + 1) * share
            ]
    for entry, piece in enumerate(pieces):
        piece[...] = split[jnp.bitwise_xor(scalars[base - 1], entry)]


def attend_back(base, scalars, rows, grad, near_grad, weight, packs):
    count, own_width = grad.shape
    width = weight.shape[2]
    share = 3 * own_width // packs
    outs = kernel_call(
        lambda *refs: attend_back_body(base, *refs),
        "attend_back",
        [array((count, width), BF16), array((2, own_width), F32)]
        + [array((count, share), BF16)] * packs,
        [scalars, rows, grad, near_grad, weight],
        6 * count * own_width * width + 10 * own_width * LONG * LONG,
        in_specs=[SMEM] + [VMEM] * 4,
        scratch=[
            pltpu.VMEM((4, 3 * count, own_width), BF16),
            pltpu.VMEM((3, 3 * count, own_width), BF16),
            pltpu.VMEM((packs, count, share), BF16),
        ],
    )
    return outs[0], outs[1], list(outs[2:])


def whole(shape):
    return pl.BlockSpec(shape, lambda i: (0,) * len(shape))


def feed_up_body(scalars, kept_ref, term_ref, other_ref, bias_ref, mod_ref, *rest):
    weight_ref, hidden_bias_ref, branch_ref, hidden_ref, share_ref, slope_ref = rest[:6]
    gelu_ref, pieces = rest[6], rest[7:]
    step = pl.program_id(0)
    size = weight_ref.shape[1]

    @pl.when(step == 0)
    def _():
        def place(number, carry):
            rows = pl.ds(aligned(number * SHORT, SHORT), SHORT)
            branch = (term_ref[rows] + other_ref[rows]) + bias_ref[...]
            branch_ref[rows] = branch
            middle = kept_ref[rows].astype(F32) + mod_ref[number, 2:3] * branch
            normed, _ = layer_norm(middle)
            shift, scale = mod_ref[number, 3:4], mod_ref[number, 4:5]
            hidden_ref[rows] = (normed * (1.0 + scale) + shift).astype(BF16)
            return carry

        lax.fori_loop(0, kept_ref.shape[0] // SHORT, place, 0)
        start = aligned(scalars[0] * (hidden_ref.shape[1] - share_ref.shape[1]))
        share_ref[...] = hidden_ref[:, pl.ds(start, share_ref.shape[1])]

    gelu, slope = gelu_pair(bf_dot(hidden_ref[...], weight_ref[...]) + hidden_bias_ref[...])
    slope_ref[...] = slope
    gelu_ref[:, pl.ds(aligned(step * size), size)] = gelu.astype(BF16)

    @pl.when(step == pl.num_programs(0) - 1)
    def _():
        for entry, piece in enumerate(pieces):
            piece[...] = gelu_ref[:, pl.ds(aligned(scalars[2 + entry]), piece.shape[1])]


def feed_up(scalars, kept, term, other, bias, mod_places, weight, hidden_bias, packs):
    count, width = kept.shape
    hidden = weight.shape[1]
    size = hidden // 3
    window = windows(hidden, packs)[1]
    outs = [
        array((count, width), F32),
        array((count, width), BF16),
        array((count, half_width(width)), BF16),
        array((count, hidden), F32),
        array((count, hidden), BF16),
    ] + [array((count, window), BF16)] * packs
    out_specs = [whole(out.shape) for out in outs]
    out_specs[3] = pl.BlockSpec((count, size), lambda i: (0, i))
    result = kernel_call(
        feed_up_body,
        "feed_up",
        outs,
        [scalars, kept, term, other, bias, mod_places, weight, hidden_bias],
        2 * count * width * hidden,
        grid=(hidden // size,),
        in_specs=[
            SMEM,
            *[whole(a.shape) for a in (kept, term, other, bias, mod_places)],
            pl.BlockSpec((width, size), lambda i: (0, i)),
            pl.BlockSpec((1, size), lambda i: (0, i)),
        ],
        out_specs=tuple(out_specs),
    )
    return *result[:5], list(result[5:])


def feed_back_body(scalars, down_in_ref, down_ref, slope_ref, weight_ref, *rest):
    back_ref, sums_ref, pieces, pre_rows = rest[0], rest[1], rest[2:-1], rest[-1]
    step = pl.program_id(0)
    size = weight_ref.shape[1]
    pre_grad = dot_by(ROWS_BY_ROWS, down_in_ref[...], down_ref[...]) * slope_ref[...]
    pre_grad = pre_grad.astype(BF16)
    pre_rows[:, pl.ds(aligned(step * size), size)] = pre_grad
    sums_ref[...] = jnp.sum(pre_grad.astype(F32), axis=0, keepdims=True)
    back = dot_by(ROWS_BY_ROWS, pre_grad, weight_ref[...])

    @pl.when(step == 0)
    def _():
        back_ref[...] = back

    @pl.when(step > 0)
    def _():
        back_ref[...] += back

    @pl.when(step == pl.num_programs(0) - 1)
    def _():
        for entry, piece in enumerate(pieces):
            piece[...] = pre_rows[:, pl.ds(aligned(scalars[2 + entry]), piece.shape[1])]


def feed_back(scalars, down_in, down, slope, weight, packs):
    count, width = down_in.shape
    hidden = weight.shape[1]
    size = hidden // 3
    window = windows(hidden, packs)[1]
    outs = [array((count, width), F32), array((1, hidden), F32)]
    outs += [array((count, window), BF16)] * packs
    out_specs = [whole(out.shape) for out in outs]
    out_specs[1] = pl.BlockSpec((1, size), lambda i: (0, i))
    result = kernel_call(
        feed_back_body,
        "feed_back",
        outs,
        [scalars, down_in, down, slope, weight],
        4 * count * width * hidden,
        grid=(hidden // size,),
        in_specs=[
            SMEM,
            whole(down_in.shape),
            pl.BlockSpec((size, width), lambda i: (i, 0)),
            pl.BlockSpec((count, size), lambda i: (0, i)),
            pl.BlockSpec((width, size), lambda i: (0, i)),
        ],
        out_specs=tuple(out_specs),
        scratch=[pltpu.VMEM((count, hidden), BF16)],
    )
    return result[0], result[1], list(result[2:])


def middle_back_body(term_ref, other_ref, branch_ref, kept_ref, up_ref, mod_ref, *rest):
    weight_ref, middle_grad_ref, branch_grad_ref, attended_ref, sums_ref, bias_ref = rest
    hidden_grad = term_ref[...] + other_ref[...]
    branch = branch_ref[...]
    gate = mod_ref[0, 2:3]
    normed, inverse = layer_norm(kept_ref[...].astype(F32) + gate * branch)
    middle_grad = up_ref[...].astype(F32) + norm_back(
        hidden_grad * (1.0 + mod_ref[0, 4:5]), normed, inverse
    )
    middle_grad_ref[...] = middle_grad
    branch_grad = (gate * middle_grad).astype(BF16)
    branch_grad_ref[...] = branch_grad
    attended_ref[...] = dot_by(ROWS_BY_ROWS, branch_grad, weight_ref[...]).astype(BF16)
    bias_ref[0] = jnp.sum(branch_grad.astype(F32), axis=0, keepdims=True)
    sums_ref[0, 0:1] = jnp.sum(middle_grad * branch, axis=0, keepdims=True)
    sums_ref[0, 1:2] = jnp.sum(hidden_grad, axis=0, keepdims=True)
    sums_ref[0, 2:3] = jnp.sum(hidden_grad * normed, axis=0, keepdims=True)


def by_place(body, name, outs, args, flops):
    places = args[0].shape[0] // SHORT

    def spec(a):
        if a.shape[0] == places * SHORT and len(a.shape) == 2:
            return pl.BlockSpec((SHORT, a.shape[1]), lambda i: (i, 0))
        if a.shape[0] == places and len(a.shape) == 3:
            return pl.BlockSpec((1, *a.shape[1:]), lambda i: (i, 0, 0))
        return pl.BlockSpec(a.shape, lambda i: (0,) * len(a.shape))

    return kernel_call(
        body,
        name,
        outs,
        args,
        flops,
        grid=(places,),
        in_specs=[spec(a) for a in args],
        out_specs=tuple(spec(a) for a in outs),
    )


def middle_back(term, other, branch, kept, upstream, mod_places, weight):
    count, width = kept.shape
    places = count // SHORT
    return by_place(
        middle_back_body,
        "middle_back",
        [
            array((count, width), F32),
            array((count, width), BF16),
            array((count, weight.shape[0]), BF16),
            array((places, 3, width), F32),
            array((places, 1, width), F32),
        ],
        [term, other, branch, kept, upstream, mod_places, weight],
        2 * count * width * weight.shape[0],
    )


def input_back_body(term_ref, other_ref, middle_grad_ref, kept_ref, mod_ref, grad_ref, sums_ref):
    hidden_grad = term_ref[...].astype(F32) + other_ref[...].astype(F32)
    normed, inverse = layer_norm(kept_ref[...].astype(F32))
    grad = middle_grad_ref[...] + norm_back(hidden_grad * (1.0 + mod_ref[0, 1:2]), normed, inverse)
    grad_ref[...] = grad.astype(BF16)
    sums_ref[0, 0:1] = jnp.sum(hidden_grad, axis=0, keepdims=True)
    sums_ref[0, 1:2] = jnp.sum(hidden_grad * normed, axis=0, keepdims=True)


def input_back(term, other, middle_grad, kept, mod_places):
    count, width = kept.shape
    return by_place(
        input_back_body,
        "input_back",
        [array((count, width), BF16), array((count // SHORT, 2, width), F32)],
        [term, other, middle_grad, kept, mod_places],
        0,
    )


def result_body(term_ref, other_ref, bias_ref, branch_ref, kept_ref, up_ref, mod_ref, *rest):
    result_ref, sums_ref, bias_grad_ref = rest
    branch_two = term_ref[...].astype(F32) + other_ref[...].astype(F32) + bias_ref[...]
    middle = kept_ref[...].astype(F32) + mod_ref[0, 2:3] * branch_ref[...]
    gate = mod_ref[0, 5:6]
    upstream = up_ref[...].astype(F32)
    result_ref[...] = (middle + gate * branch_two).astype(BF16)
    sums_ref[0, 0:1] = jnp.sum(upstream * branch_two, axis=0, keepdims=True)
    down_in = (gate * upstream).astype(BF16).astype(F32)
    bias_grad_ref[0] = jnp.sum(down_in, axis=0, keepdims=True)


def result(term, other, bias, branch, kept, upstream, mod_places):
    count, width = kept.shape
    places = count // SHORT
    return by_place(
        result_body,
        "result",
        [
            array((count, width), BF16),
            array((places, 1, width), F32),
            array((places, 1, width), F32),
        ],
        [term, other, bias, branch, kept, upstream, mod_places],
        0,
    )


def weight_grad_body(packs, offset, count_shares, scalars, *refs):
    shares, refs = refs[:count_shares], refs[count_shares:]
    columns, refs = refs[:packs], refs[packs:]
    outs, (rows_all, columns_all, total) = refs[:-3], refs[-3:]
    count, wide = columns[0].shape
    width = rows_all.shape[1]
    half = half_width(width)
    for entry in range(packs):
        rows = pl.ds(entry * count, count)
        columns_all[rows] = columns[entry][...]
        if count_shares == 1:
            source = jnp.bitwise_xor(scalars[2 + packs], entry) * (2 * count)
            low = pl.ds(aligned(source, SHORT), count)
            high = pl.ds(aligned(source + count, SHORT), count)
            rows_all[rows, :half] = shares[0][low, offset : offset + half]
            rows_all[rows, half:] = shares[0][high, offset + 2 * half - width : offset + half]
        elif entry == 0:
            rows_all[rows] = shares[0][...]
        else:
            skip = width - half
            place = pl.ds(aligned(scalars[0] * skip), half)
            rows_all[rows, place] = shares[1][(entry - 1) * count : entry * count]
            place = pl.ds(aligned((1 - scalars[0]) * skip), half)
            rows_all[rows, place] = shares[2][(entry - 1) * count : entry * count]
    if len(outs) == 1:
        outs[0][...] = dot_by(COLUMNS_BY_COLUMNS, rows_all[...], columns_all[...]).astype(BF16)
        return
    total[...] = dot_by(COLUMNS_BY_COLUMNS, rows_all[...], columns_all[...])
    cut_by_blk(scalars, total, outs)


def cut_by_blk(scalars, total, outs):
    blocks = len(outs)
    size = total.shape[0] // blocks
    for step in range(blocks):
        target = lax.rem(scalars[1] + step, blocks)
        piece = total[pl.ds(aligned(target * size, 8), size)]
        outs[step][...] = piece.astype(outs[step].dtype)


def cut_shapes(width, wide, blocks):
    size = width // blocks
    return [array((size, wide), F32)] + [array((size, wide), BF16)] * (blocks - 1)


def weight_grad(scalars, width, offset, shares, columns, blocks=1):
    packs = len(columns)
    count, wide = columns[0].shape
    outs = [array((width, wide), BF16)]
    if blocks > 1:
        outs = cut_shapes(width, wide, blocks)
    return kernel_call(
        lambda *refs: weight_grad_body(packs, offset, len(shares), *refs),
        "weight_grad",
        outs,
        [scalars, *shares, *columns],
        2 * packs * count * width * wide,
        in_specs=[SMEM] + [VMEM] * (packs + len(shares)),
        scratch=[
            pltpu.VMEM((packs * count, width), BF16),
            pltpu.VMEM((packs * count, wide), BF16),
            pltpu.VMEM((width, wide), F32),
        ],
    )


def own_weight_grad_body(rows_ref, columns_ref, out_ref):
    out_ref[...] = dot_by(COLUMNS_BY_COLUMNS, rows_ref[...], columns_ref[...]).astype(BF16)


def own_weight_grad(rows, columns):
    shape = (rows.shape[1], columns.shape[1])
    return kernel_call(
        own_weight_grad_body,
        "own_weight_grad",
        [array(shape, BF16)],
        [rows, columns],
        2 * rows.shape[0] * math.prod(shape),
    )[0]


def join_body(kind, starts, packs, scalars, *refs):
    entries, outs, held = refs[:-2], refs[-2:-1], refs[-1]
    size = entries[0].shape[0] // (packs if len(entries) == 1 else 1)
    if len(entries) > 1:
        for entry in range(packs):
            held[entry] = entries[entry][...]
    if kind == "output":
        total = held[scalars[2 + packs]].astype(F32)
        for number in range(1, packs):
            total = total + held[jnp.bitwise_xor(scalars[2 + packs], number)].astype(F32)
        outs[0][...] = total
        return
    for number in range(packs):
        if len(entries) > 1:
            piece = held[jnp.bitwise_xor(scalars[2 + packs], number)].astype(F32)
        else:
            piece = entries[0][number * size : (number + 1) * size].astype(F32)
        if kind == "qkv":
            share = piece.shape[1] // 3
            for part in range(3):
                columns = pl.ds(number * share, share)
                outs[0][part, :, columns] = piece[:, part * share : (part + 1) * share]
        else:
            end = [*starts[1:], outs[0].shape[1]][number]
            outs[0][:, starts[number] : end] = piece[:, : end - starts[number]]


def join(kind, scalars, entries, packs, shapes, starts=()):
    held = (len(entries), *entries[0].shape) if len(entries) > 1 else (16, LANES)
    return kernel_call(
        lambda *refs: join_body(kind, starts, packs, *refs),
        "join_" + kind,
        [array(shape, F32) for shape in shapes],
        [scalars, *entries],
        0,
        in_specs=[SMEM] + [VMEM] * len(entries),
        scratch=[pltpu.VMEM(held, BF16)],
    )


def collect_body(first, scalars, input_ref, middle_ref, two_ref, active_ref, *refs):
    qkv_ref, output_ref, hidden_ref, down_ref, out_ref, held = refs
    places, _, width = middle_ref.shape
    half = width // 2
    row = 0

    def put(value):
        nonlocal row
        held[row : row + 1] = value
        row += 1

    def put_twice(value):
        high = value.astype(BF16).astype(F32)
        put(high)
        put(value - high)

    def put_sums(start):
        nonlocal row
        row = 0
        for place in range(places):
            for source in (input_ref, middle_ref, two_ref):
                for number in range(source.shape[1]):
                    put(source[place, number : number + 1, start : start + half])

    held[...] = jnp.zeros_like(held)
    pl.when(scalars[0] == 0)(lambda: put_sums(0))
    pl.when(scalars[0] == 1)(lambda: put_sums(half))
    for place in range(places):
        active = active_ref[pl.ds(scalars[first + place], 1)]
        put(active[:, :half])
        put(active[:, half:])
    put_twice(qkv_ref[0:1])
    put_twice(qkv_ref[1:2])
    for number in range(hidden_ref.shape[1] // half):
        put_twice(hidden_ref[:, number * half : (number + 1) * half])
    for source in (output_ref, down_ref):
        total = jnp.sum(source[...], axis=0)
        put_twice(total[:, :half])
        put_twice(total[:, half:])
    out_ref[...] = held[...].astype(BF16)


def collect(first, scalars, *args):
    places, _, width = args[0].shape
    hidden = args[6].shape[1]
    used = places * 8 + 2 * (2 + 2 * hidden // width + 4)
    size = -(-used // 16) * 16
    return kernel_call(
        lambda *refs: collect_body(first, *refs),
        "collect",
        [array((size, width // 2), BF16)],
        [scalars, *args],
        0,
        in_specs=[SMEM] + [VMEM] * len(args),
        scratch=[pltpu.VMEM((size, width // 2), F32)],
    )[0]


def spread_body(packs, blocks, places, size, scalars, segments, *refs):
    entries = refs[:packs]
    weight_ref, bias_ref, biases_ref, grad_ref, held, rows_all, active, sums = refs[packs:]
    half = weight_ref.shape[2]
    rows = weight_ref.shape[1]
    pack = scalars[2 + packs]
    for entry in range(packs):
        held[entry] = entries[entry][...].reshape(blocks, size, half)
    for number in range(packs):
        for block in range(blocks):
            source = held[
                jnp.bitwise_xor(pack, number), jnp.bitwise_xor(scalars[1], block)
            ]
            rows_all[number * blocks + block] = source.astype(F32)
    cut = 6 * places
    devices = packs * blocks

    def take_active(block):
        start = block * rows
        for device in range(devices):
            for place in range(places):
                row = cut + 2 * place
                whole_row = jnp.concatenate(
                    [rows_all[device, row : row + 1], rows_all[device, row + 1 : row + 2]], axis=1
                )
                number = device * places + place
                active[number : number + 1] = whole_row[:, start : start + rows]

    for block in range(blocks):
        pl.when(scalars[1] == block)(lambda: take_active(block))
    own_active = active[...].astype(BF16)
    for group in range(6):
        for device in range(devices):
            for place in range(places):
                number = device * places + place
                row = place * 6 + group
                sums[number : number + 1] = rows_all[device, row : row + 1]
        values = sums[...]
        bias_ref[group : group + 1] = jnp.sum(values, axis=0, keepdims=True)
        weight_ref[group] = dot_by(COLUMNS_BY_COLUMNS, own_active, values.astype(BF16))
    first = cut + 2 * places
    total = rows_all[0, first:]
    for device in range(1, devices):
        total = total + rows_all[device, first:]
    biases_ref[...] = total
    grad_ref[...] = jnp.zeros_like(grad_ref)
    for block in range(blocks):
        for place in range(places):
            segment = segments[(block * places + place) * SHORT]
            own = rows_all[pack * blocks + block, place * 6 : place * 6 + 6]
            grad_ref[segment] = grad_ref[segment] + own


def spread(scalars, segments, entries, packs, blocks, places, seg_count, width):
    size = entries[0].shape[0] // blocks
    half = entries[0].shape[1]
    devices = packs * blocks
    return kernel_call(
        lambda *refs: spread_body(packs, blocks, places, size, *refs),
        "spread",
        [
            array((6, width // blocks, half), F32),
            array((6, half), F32),
            array((size - 8 * places, half), F32),
            array((seg_count, 6, half), F32),
        ],
        [scalars, segments, *entries],
        0,
        in_specs=[SMEM, SMEM] + [VMEM] * packs,
        scratch=[
            pltpu.VMEM((packs, blocks, size, half), BF16),
            pltpu.VMEM((devices, size, half), F32),
            pltpu.VMEM((devices * places, width // blocks), F32),
            pltpu.VMEM((devices * places, half), F32),
        ],
    )


def xor_permute(block, axis, bits):
    return lax.ppermute(block, axis, [(i, i ^ bits) for i in range(lax.axis_size(axis))])


def swap(block):
    return xor_permute(block, "head", 1)


def move(block, step):
    count = lax.axis_size("blk")
    pairs = [(i, i + step) for i in range(count) if 0 <= i + step < count]
    return lax.ppermute(block, "blk", pairs)


def gather_xor(block, axis, turned=False):
    bits = [1 << b for b in range((lax.axis_size(axis) - 1).bit_length())]
    held = {0: block}
    for bit in bits[::-1] if turned else bits:
        for entry in list(held):
            held[entry ^ bit] = xor_permute(held[entry], axis, bit)
    return [held[entry] for entry in range(lax.axis_size(axis))]


def in_order(entries, axis):
    order = jnp.arange(len(entries), dtype=jnp.int32) ^ lax.axis_index(axis)
    return jnp.take(jnp.stack(entries), order, axis=0)


def trade(pieces, axis, entries):
    return {r: xor_permute(pieces[r], axis, r) for r in entries}


def windows(width, parts):
    tiles = width // LANES
    size = -(-tiles // parts)
    return [LANES * (q * (tiles - size) // (parts - 1)) for q in range(parts)], size * LANES


def half_width(width):
    return -(-width // (2 * LANES)) * LANES


def share_of(block):
    half = half_width(block.shape[1])
    first, last = block[:, :half], block[:, block.shape[1] - half :]
    return jnp.where(lax.axis_index("head") == 0, first, last)


def gather_shares(share):
    return lax.all_gather(share, ("pack", "head"), axis=0, tiled=True)


def hold(values, *after):
    flat, tree = jax.tree.flatten(values)
    held = lax.optimization_barrier((*flat, *after))
    return jax.tree.unflatten(tree, held[: len(flat)])


def sum_blk(pieces):
    count = len(pieces)
    total = pieces[0]
    for step in range(1, count):
        pairs = [(i, (i + step) % count) for i in range(count)]
        total = total + lax.ppermute(pieces[step], "blk", pairs).astype(F32)
    return total.astype(BF16)


def local(
    tokens_full,
    condition,
    kept_index,
    segment_ids,
    cotangent,
    qkv_weight,
    query_value_bias,
    output_weight,
    output_bias,
    hidden_weight,
    hidden_bias,
    down_weight,
    down_bias,
    modulation_weight,
    modulation_bias,
):
    width = tokens_full.shape[2]
    own_width = qkv_weight.shape[2]
    hidden = hidden_weight.shape[1]
    count = kept_index.shape[1]
    seg_count = condition.shape[1]
    places = count // SHORT
    longs = (segment_ids.shape[1] - SHORT * seg_count) // (LONG - SHORT)
    packs = lax.axis_size("pack")
    blocks = lax.axis_size("blk")
    blk = lax.axis_index("blk")
    core = lax.axis_index("head")
    pack = lax.axis_index("pack")

    local_index = kept_index[0] - blk * (2 * count)
    full_rows = tokens_full[0]
    cot_rows = cotangent[0]
    picker = (
        local_index[:, None] == jnp.arange(full_rows.shape[0], dtype=jnp.int32)[None, :]
    ).astype(BF16)
    kept_rows = bf_dot(picker, full_rows).astype(BF16)
    upstream = bf_dot(picker, cot_rows).astype(BF16)

    starts, window = windows(hidden, packs)
    place = jnp.stack([core, blk, pack, jnp.int32(blocks)]).astype(jnp.int32)
    scalars = plan(longs, packs, starts, place, segment_ids[0])
    base = 3 + packs
    reaches_low = scalars[-1] == 1

    def beside(block):
        low, high = move(block, 1), move(block, -1)
        if longs == 1:
            return jnp.where(reaches_low, low, high)
        return jnp.concatenate([low, high], axis=0)

    half = count // 2
    near_half = beside(lax.dynamic_slice_in_dim(kept_rows, core * half, half, 0))
    other_half = swap(near_half)
    first = jnp.where(core == 0, near_half, other_half).reshape(-1, half, width)
    second = jnp.where(core == 0, other_half, near_half).reshape(-1, half, width)
    near_rows = jnp.concatenate([first, second], axis=1).reshape(-1, width)

    cond_rows = condition[0].astype(F32)
    active = jax.nn.silu(cond_rows).astype(BF16)
    mod_own = (
        jnp.einsum("sd,dgf->sgf", active, modulation_weight, preferred_element_type=F32)
        + modulation_bias.astype(F32)[None]
    )
    mod_near = pick(
        scalars,
        base + 3 + 2 * places,
        mod_own,
        swap(mod_own),
        places + near_rows.shape[0] // SHORT,
    )
    mod_places = mod_near[:places]
    wide_bias = query_value_bias.astype(F32)
    qkv_bias = jnp.stack([wide_bias[0], jnp.zeros_like(wide_bias[0]), wide_bias[1]])[:, None]
    hidden_rows, down_in, share = norm(scalars, kept_rows, near_rows, upstream, mod_near)
    early_shares = gather_shares(share)
    qkv_turned = jnp.transpose(qkv_weight, (1, 2, 0))
    projected = jnp.einsum("td,gfd->gtf", hidden_rows, qkv_turned, preferred_element_type=F32)
    qkv_rows = (projected + qkv_bias).astype(BF16)

    attended, branch_term = attend(base, scalars, qkv_rows, output_weight, count)
    branch_one, hidden_two, hidden_two_share, slope, gelu, gelu_pieces = feed_up(
        scalars,
        kept_rows,
        branch_term,
        swap(branch_term),
        output_bias.astype(F32)[None],
        mod_places,
        hidden_weight,
        hidden_bias.astype(F32)[None],
        packs,
    )
    one_step = [r for r in range(1, packs) if r & (r - 1) == 0]
    further = [r for r in range(1, packs) if r & (r - 1)]

    def by_entry(pieces, *parts):
        found = {0: pieces[0]}
        for part in parts:
            found.update(part)
        return [found[r] for r in range(packs)]

    gelu_first = trade(gelu_pieces, "pack", one_step)
    hidden_two_shares = gather_shares(hidden_two_share)
    back_term, hidden_sums, pre_pieces = feed_back(
        scalars, down_in, down_weight, slope, hidden_weight, packs
    )
    back_term, gelu_first, gelu_pieces, pre_pieces = hold(
        (back_term, gelu_first, gelu_pieces, pre_pieces)
    )
    gelu_last = trade(gelu_pieces, "pack", further)
    middle_grad, branch_grad, attended_grad, middle_sums, output_sums = middle_back(
        back_term, swap(back_term), branch_one, kept_rows, upstream, mod_places, output_weight
    )
    attended_grad, gelu_last, early_shares, pre_pieces, gelu = hold(
        (attended_grad, gelu_last, early_shares, pre_pieces, gelu)
    )
    near_grad = beside(attended_grad)

    pre_first = trade(pre_pieces, "pack", range(1, packs))
    gelu_all = by_entry(gelu_pieces, gelu_first, gelu_last)
    down_raw = weight_grad(scalars, width, 0, [early_shares], gelu_all)[0]
    two_term = bf_dot(gelu, down_weight).astype(BF16)
    output_raw = own_weight_grad(branch_grad, attended)
    near_grad, down_raw, output_raw, two_term, pre_first = hold(
        (near_grad, down_raw, output_raw, two_term, pre_first)
    )
    half = half_width(width)
    rows = width // blocks
    down_term = lax.psum_scatter(down_raw, "blk", scatter_dimension=0, tiled=True)
    output_term = lax.psum_scatter(output_raw, "blk", scatter_dimension=0, tiled=True)
    hidden_term, qkv_sums, qkv_pieces = attend_back(
        base, scalars, qkv_rows, attended_grad, near_grad, qkv_turned, packs
    )
    hidden_term, qkv_pieces, two_term = hold((hidden_term, qkv_pieces, two_term))
    qkv_all = by_entry(qkv_pieces, trade(qkv_pieces, "pack", range(1, packs)))

    def put_rows(base, rows):
        spread = dot_by(COLUMNS_BY_COLUMNS, picker, rows)
        kept = jnp.max(picker, axis=0)[:, None] > 0
        return jnp.where(kept, spread.astype(BF16), base)[None]

    input_grad, input_sums = input_back(
        hidden_term, swap(hidden_term), middle_grad, kept_rows, mod_places
    )
    tokens_grad = put_rows(cot_rows, input_grad)
    pre_all = by_entry(pre_pieces, pre_first)
    hidden_raw = weight_grad(scalars, width, 0, [hidden_two_shares], pre_all)[0]
    result_rows, two_sums, down_sums = result(
        two_term,
        swap(two_term),
        down_bias.astype(F32)[None],
        branch_one,
        kept_rows,
        upstream,
        mod_places,
    )
    sent = collect(
        base + 3 + 2 * places,
        scalars,
        input_sums,
        middle_sums,
        two_sums,
        active.astype(F32),
        qkv_sums,
        output_sums,
        hidden_sums,
        down_sums,
    )
    qkv_all, tokens_grad, hidden_raw, result_rows, sent = hold(
        (qkv_all, tokens_grad, hidden_raw, result_rows, sent)
    )
    hidden_term = lax.psum_scatter(hidden_raw, "blk", scatter_dimension=0, tiled=True)
    by_blk = gather_xor(sent, "blk")
    qkv_terms = weight_grad(scalars, width, half, [early_shares], qkv_all, blocks)
    qkv_terms, result_rows, by_blk = hold((qkv_terms, result_rows, by_blk))
    entries = gather_xor(jnp.concatenate(by_blk, axis=0), "pack")
    block_output = put_rows(full_rows, result_rows)
    down_entries = gather_xor(down_term, "pack")
    qkv_share, entries, block_output, down_entries = hold(
        (sum_blk(qkv_terms), entries, block_output, down_entries)
    )
    qkv_entries = gather_xor(qkv_share, "pack")
    modulation_weight_grad, modulation_bias_grad, biases, mod_grad = spread(
        scalars, segment_ids[0], entries, packs, blocks, places, seg_count, width
    )
    down_weight_grad = join("down", scalars, down_entries, packs, [(rows, hidden)], starts)[0].T
    qkv_entries, output_term, hidden_term, modulation_weight_grad = hold(
        (qkv_entries, output_term, hidden_term, modulation_weight_grad)
    )
    hidden_weight_grad = join(
        "hidden", scalars, gather_xor(hidden_term, "pack", True), packs, [(rows, hidden)], starts
    )[0]
    output_weight_grad = join(
        "output", scalars, gather_xor(output_term, "pack"), packs, [(rows, own_width)]
    )[0].T
    qkv_weight_grad = join("qkv", scalars, qkv_entries, packs, [(3, rows, own_width)])[0]
    qkv_weight_grad = jnp.swapaxes(qkv_weight_grad, 0, 1)
    modulation_weight_grad = jnp.swapaxes(modulation_weight_grad, 0, 1)
    mod_high = mod_grad.astype(BF16)
    mod_low = (mod_grad - mod_high.astype(F32)).astype(BF16)
    cond_terms = jnp.einsum(
        "sgf,dgf->sd",
        jnp.concatenate([mod_high, mod_low], axis=0),
        modulation_weight,
        preferred_element_type=F32,
    )
    cond_term = cond_terms[:seg_count] + cond_terms[seg_count:]
    cond_total = cond_term + swap(cond_term)
    squashed = jax.nn.sigmoid(cond_rows)
    condition_grad = (cond_total * squashed * (1.0 + cond_rows * (1.0 - squashed)))[None]

    def bias_rows(first, number):
        pairs = biases[2 * first : 2 * (first + number)].reshape(number, 2, own_width)
        return (pairs[:, 0] + pairs[:, 1]).reshape(-1)

    value_bias = bias_rows(0, 2).reshape(2, own_width)
    hidden_rows_count = hidden // own_width
    return (
        block_output,
        tokens_grad,
        condition_grad,
        qkv_weight_grad,
        value_bias,
        output_weight_grad,
        bias_rows(2 + hidden_rows_count, 2),
        hidden_weight_grad,
        bias_rows(2, hidden_rows_count),
        down_weight_grad,
        bias_rows(4 + hidden_rows_count, 2),
        modulation_weight_grad,
        modulation_bias_grad,
    )


def solution(mesh):
    in_specs = (
        P("pack", "blk", None),
        P("pack", None, None),
        P("pack", "blk"),
        P("pack", None),
        P("pack", "blk", None),
        P(None, None, "head"),
        P(None, "head"),
        P("head", None),
        P(),
        P(None, "head"),
        P("head"),
        P("head", None),
        P(),
        P(None, None, "head"),
        P(None, "head"),
    )
    out_specs = (
        P("pack", "blk", None),
        P("pack", "blk", None),
        P("pack", None, None),
        P("blk", None, "head"),
        P(None, "head"),
        P("head", "blk"),
        P(),
        P("blk", "head"),
        P("head"),
        P("head", "blk"),
        P(),
        P("blk", None, "head"),
        P(None, "head"),
    )
    return jax.shard_map(local, mesh=mesh, in_specs=in_specs, out_specs=out_specs, check_vma=False)
```

profile of v0, /device:TPU:0, one launch (start us, length us, event | category | flops | bytes accessed | tf_op | source)
XLA Modules:
  0.0 339.1 jit_solution(3135859920424034653)
XLA Ops:
  8.0 2.5 convolution_convert_fusion.4.own_ref.kept_ref
  10.5 5.0 %collective-permute-start = (bf16[192,1152]{1,0:T(8,128)(2,1)S(1)}, bf16[192,1152]{1,0:T(8,128)(2,1)S(1)}, u32[]{:S(2)}, u32[]{:S(2)}) collective-permute-start(bf16[192,1152]{1,0:T(8,128)(2,1)S(1)} %constant_dynamic-slice_fusion), channel_id=1, source_target_pairs={{0,2},{2,4},{4,6},{1,3},{3,5},{5,7},{8,10},{10,12},{12,14},{9,11},... | collective-permute-start | bytes 1327112 | tf_op jit(solution)/shard_map/ppermute | solution.py:859
  18.0 1.4 plan.1.refs_0_.scalars
  21.2 5.6 %fusion.22 = f32[9,6,576]{2,0,1:T(8,128)S(1)} fusion(bf16[1152,6,576]{0,2,1:T(8,128)(2,1)} %param.28, bf16[1,9,1152]{2,1,0:T(8,128)(2,1)S(1)} %copy-done.30), kind=kOutput, calls=%fused_computation.43 | convolution fusion | flops 71725824 | bytes 8107776 | tf_op jit(solution)/shard_map/sd,dgf->sgf/dot_general | solution.py:976
  26.8 2.2 collective-permute-done.1
  29.8 1.9 convolution_convert_fusion.3.up_ref
  32.4 2.2 pick.1.mod_ref
  35.6 6.4 %norm.1 = (bf16[768,1152]{1,0:T(8,128)(2,1)}, bf16[384,1152]{1,0:T(8,128)(2,1)}, bf16[384,1280]{1,0:T(8,128)(2,1)}) custom-call(s32[23]{0:T(128)} %plan.1.refs_0_.scalars, bf16[384,1152]{1,0:T(8,128)(2,1)} %copy-done, bf16[384,1152]{1,0:T(8,128)(2,1)} %maximum_bitcast_fusion.near_ref, bf16[384,1152]{1,0:T(8,128)(2,1)} %convolution_convert_fusion.3.up_ref, ...), custom_call_target="tpu_custom_call" | custom-call | bytes 6457 | tf_op jit(solution)/shard_map/norm/pallas_call | solution.py:46
  42.5 8.4 %fusion.4.refs_1_ = bf16[3,768,576]{2,1,0:T(8,128)(2,1)} fusion(f32[3,576]{1,0:T(4,128)S(1)} %pad_maximum_fusion.1, bf16[768,1152]{1,0:T(8,128)(2,1)} %get-tuple-element.121, bf16[1152,3,576]{0,2,1:T(8,128)(2,1)} %param.20), kind=kOutput, calls=%fused_computation.7 | convolution fusion | flops 3060301824 | bytes 8411904 | tf_op jit(solution)/shard_map/td,gfd->gtf/dot_general | solution.py:992
  50.9 11.1 %attend.1 = (bf16[384,576]{1,0:T(8,128)(2,1)}, f32[384,1152]{1,0:T(8,128)}) custom-call(s32[23]{0:T(128)} %plan.1.refs_0_.scalars, bf16[3,768,576]{2,1,0:T(8,128)(2,1)} %fusion.4.refs_1_, bf16[576,1152]{1,0:T(8,128)(2,1)} %rest_0_.3), custom_call_target="tpu_custom_call" | custom-call | flops 962592 | bytes 6193 | tf_op jit(solution)/shard_map/attend/pallas_call | solution.py:46
  64.0 1.9 collective-permute-done.4.other_ref
  67.1 12.0 %feed_up.1 = (f32[384,1152]{1,0:T(8,128)}, bf16[384,1152]{1,0:T(8,128)(2,1)}, bf16[384,640]{1,0:T(8,128)(2,1)}, f32[384,2304]{1,0:T(8,128)}, bf16[384,2304]{1,0:...) custom-call(s32[23]{0:T(128)} %plan.1.refs_0_.scalars, ...), custom_call_target="tpu_custom_call" | custom-call | flops 2038431 | bytes 20249 | tf_op jit(solution)/shard_map/feed_up/pallas_call | solution.py:46
  79.8 2.6 collective-permute-start.5
  82.3 1.6 collective-permute-start.6
  83.9 11.4 %feed_back.1 = (f32[384,1152]{1,0:T(8,128)}, f32[1,2304]{1,0:T(1,128)}, bf16[384,640]{1,0:T(8,128)(2,1)}, bf16[384,640]{1,0:T(8,128)(2,1)}, bf16[384,640]{1,0:T(8,128)(2,1)}, /*index=5*/bf16[384,640]{1,0:T(8,128)(2,1)}) custom-call(s32[23]{0:T(128)} %plan.1.refs_0_.scalars, bf16[384,1152]{1,0:T(8,128)(2,1)} %get-tuple-element.120.down_in_ref, ...), custom_call_target="tpu_custom_call" | custom-call | flops 4076863 | bytes 18785 | tf_op jit(solution)/shard_map/feed_back/pallas_call | solution.py:46
  95.3 8.5 %collective-permute-done.5.refs_3_ = bf16[384,640]{1,0:T(8,128)(2,1)S(1)} collective-permute-done((bf16[384,640]{1,0:T(8,128)(2,1)}, bf16[384,640]{1,0:T(8,128)(2,1)S(1)}, u32[]{:S(2)}, u32[]{:S(2)}) %collective-permute-start.5) | collective-permute-done | bytes 491552 | tf_op jit(solution)/shard_map/ppermute | solution.py:849
  104.8 1.5 collective-permute-start.8
  106.3 2.4 collective-permute-done.7.other_ref
  109.9 7.6 %middle_back.1 = (f32[384,1152]{1,0:T(8,128)}, bf16[384,1152]{1,0:T(8,128)(2,1)}, bf16[384,576]{1,0:T(8,128)(2,1)}, f32[3,3,1152]{2,1,0:T(4,128)}, f32[3,1,1152]{2,1,0:T(1,128)}) custom-call(f32[384,1152]{1,0:T(8,128)} %get-tuple-element.133.term_ref, f32[384,1152]{1,0:T(8,128)} %copy-done.2, f32[384,1152]{1,0:T(8,128)} %get-tuple-element.134.branch_ref, ...), custom_call_target="tpu_custom_call" | custom-call | flops 509607 | bytes 11639 | tf_op jit(solution)/shard_map/middle_back/pallas_call | solution.py:46
  117.5 3.6 %own_weight_grad.1 = bf16[1152,576]{1,0:T(8,128)(2,1)} custom-call(bf16[384,1152]{1,0:T(8,128)(2,1)} %get-tuple-element.149.rows_ref, bf16[384,576]{1,0:T(8,128)(2,1)} %get-tuple-element.150.columns_ref), custom_call_target="tpu_custom_call" | custom-call | flops 509607 | bytes 2654 | tf_op jit(solution)/shard_map/own_weight_grad/pallas_call | solution.py:46
  122.9 5.3 %collective-permute-start.9 = (bf16[384,576]{1,0:T(8,128)(2,1)S(1)}, bf16[384,576]{1,0:T(8,128)(2,1)}, u32[]{:S(2)}, u32[]{:S(2)}) collective-permute-start(bf16[384,576]{1,0:T(8,128)(2,1)S(1)} %copy-done.11), channel_id=1, source_target_pairs={{0,2},{2,4},{4,6},{1,3},{3,5},{5,7},{8,10},{10,12},{12,14},{9,11},... | collective-permute-start | bytes 1327112 | tf_op jit(solution)/shard_map/ppermute | solution.py:859
  128.2 2.1 collective-permute-start.11
  132.1 5.5 %convolution_convert_fusion.2.term_ref = bf16[384,1152]{1,0:T(8,128)(2,1)S(1)} fusion(bf16[384,2304]{1,0:T(8,128)(2,1)} %get-tuple-element.151, bf16[2304,1152]{1,0:T(8,128)(2,1)} %down_ref.1), kind=kOutput, calls=%fused_computation.8 | convolution fusion | flops 2038874112 | bytes 7962624 | tf_op jit(solution)/shard_map/dot_general | solution.py:28
  137.7 8.2 %weight_grad.3 = bf16[1152,640]{1,0:T(8,128)(2,1)} custom-call(s32[23]{0:T(128)} %plan.1.refs_0_.scalars, bf16[3072,1280]{1,0:T(8,128)(2,1)} %all-gather.3.cloned.1.call-done.refs_1_, bf16[384,640]{1,0:T(8,128)(2,1)} %get-tuple-element.145.refs_2_, bf16[384,640]{1,0:T(8,128)(2,1)} %copy-done.13, bf16[384,640]{1,0:T(8,128)(2,1)} %copy-done.14, ...), custom_call_target="tpu_custom_call" | custom-call | flops 2264924 | bytes 11305 | tf_op jit(solution)/shard_map/weight_grad/pallas_call | solution.py:46
  145.9 1.9 broadcast_select_fusion.refs_3_
  147.7 5.2 %collective-permute-done.11.refs_3_ = bf16[384,640]{1,0:T(8,128)(2,1)S(1)} collective-permute-done((bf16[384,640]{1,0:T(8,128)(2,1)}, bf16[384,640]{1,0:T(8,128)(2,1)S(1)}, u32[]{:S(2)}, u32[]{:S(2)}) %collective-permute-start.11) | collective-permute-done | bytes 491552 | tf_op jit(solution)/shard_map/ppermute | solution.py:849
  152.9 8.3 %collective-permute-done.12.refs_4_ = bf16[384,640]{1,0:T(8,128)(2,1)S(1)} collective-permute-done((bf16[384,640]{1,0:T(8,128)(2,1)S(1)}, bf16[384,640]{1,0:T(8,128)(2,1)S(1)}, u32[]{:S(2)}, u32[]{:S(2)}) %collective-permute-start.12) | collective-permute-done | bytes 491552 | tf_op jit(solution)/shard_map/ppermute | solution.py:849
  161.3 1.7 collective-permute-done.13.refs_5_
  163.8 14.3 %attend_back.1 = (bf16[384,1152]{1,0:T(8,128)(2,1)}, f32[2,576]{1,0:T(2,128)}, bf16[384,432]{1,0:T(8,128)(2,1)}, bf16[384,432]{1,0:T(8,128)(2,1)}, bf16[384,432]{1,0:T(8,128)(2,1)}, /*index=5*/bf16[384,432]{1,0:T(8,128)(2,1)}) custom-call(s32[23]{0:T(128)} %plan.1.refs_0_.scalars, bf16[3,768,576]{2,1,0:T(8,128)(2,1)} %fusion.4.refs_1_, ...), custom_call_target="tpu_custom_call" | custom-call | flops 3038773 | bytes 9736 | tf_op jit(solution)/shard_map/attend_back/pallas_call | solution.py:46
  179.5 7.1 %collective-permute-start.14 = (bf16[384,432]{1,0:T(8,128)(2,1)}, bf16[384,432]{1,0:T(8,128)(2,1)S(1)}, u32[]{:S(2)}, u32[]{:S(2)}) collective-permute-start(bf16[384,432]{1,0:T(8,128)(2,1)} %get-tuple-element.163), channel_id=1, source_target_pairs={{0,8},{8,0},{16,24},{24,16},{1,9},{9,1},{17,25},{25,17},{2,10},{10... | collective-permute-start | bytes 995336 | tf_op jit(solution)/shard_map/ppermute | solution.py:849
  186.7 1.5 collective-permute-start.16
  188.8 6.8 %weight_grad.4 = bf16[1152,640]{1,0:T(8,128)(2,1)} custom-call(s32[23]{0:T(128)} %plan.1.refs_0_.scalars, bf16[3072,640]{1,0:T(8,128)(2,1)} %all-gather.5.cloned.1.call-done.refs_1_, bf16[384,640]{1,0:T(8,128)(2,1)} %get-tuple-element.170.refs_2_, bf16[384,640]{1,0:T(8,128)(2,1)} %copy-done.10, bf16[384,640]{1,0:T(8,128)(2,1)} %copy-done.12, ...), custom_call_target="tpu_custom_call" | custom-call | flops 2264924 | bytes 7372 | tf_op jit(solution)/shard_map/weight_grad/pallas_call | solution.py:46
  196.5 4.6 %result.1 = (bf16[384,1152]{1,0:T(8,128)(2,1)}, f32[3,1,1152]{2,1,0:T(1,128)}, f32[3,1,1152]{2,1,0:T(1,128)}) custom-call(bf16[384,1152]{1,0:T(8,128)(2,1)} %copy-done.6, bf16[384,1152]{1,0:T(8,128)(2,1)} %copy-done.7, f32[1,1152]{1,0:T(1,128)} %reshape.87.bias_ref, f32[384,1152]{1,0:T(8,128)} %get-tuple-element.134.branch_ref, bf16[384,1152]{1,0:T(8,128)(2,1)} %copy-done, ...), custom_call_target="tpu_custom_call" | custom-call | bytes 6308 | tf_op jit(solution)/shard_map/result/pallas_call | solution.py:46
  202.0 4.7 %input_back.1 = (bf16[384,1152]{1,0:T(8,128)(2,1)}, f32[3,2,1152]{2,1,0:T(2,128)}) custom-call(bf16[384,1152]{1,0:T(8,128)(2,1)} %get-tuple-element.166.term_ref, bf16[384,1152]{1,0:T(8,128)(2,1)} %copy-done.5, f32[384,1152]{1,0:T(8,128)} %get-tuple-element.167.middle_grad_ref, bf16[384,1152]{1,0:T(8,128)(2,1)} %copy-done, f32[3,6,1152]{2,1,0:T(8,128)} %slice.74.mod_ref), custom_call_target="tpu_custom_call" | custom-call | bytes 5419 | tf_op jit(solution)/shard_map/input_back/pallas_call | solution.py:46
  206.7 1.7 collect.1
  208.4 3.8 %fusion.3 = bf16[1,768,1152]{2,1,0:T(8,128)(2,1)} fusion(bf16[384,1152]{1,0:T(8,128)(2,1)} %get-tuple-element.168, bf16[1,768,1152]{2,1,0:T(8,128)(2,1)S(1)} %copy-done.46, pred[768]{0:T(1024)(128)(4,1)S(1)} %broadcast_compare_fusion, s32[384]{0:T(512)S(1)} %subtract_reduce_fusion), kind=kOutput, calls=%fused_computation.6 | convolution fusion | flops 681541632 | bytes 4425984 | tf_op jit(solution)/shard_map/dot_general | solution.py:32
  212.3 3.7 %collective-permute-start.20 = (bf16[48,576]{1,0:T(8,128)(2,1)S(1)}, bf16[48,576]{1,0:T(8,128)(2,1)S(1)}, u32[]{:S(2)}, u32[]{:S(2)}) collective-permute-start(bf16[48,576]{1,0:T(8,128)(2,1)S(1)} %copy-done.37), channel_id=1, source_target_pairs={{0,4},{2,6},{4,0},{6,2},{1,5},{3,7},{5,1},{7,3},{8,12},{10,14},{12... | collective-permute-start | bytes 165896 | tf_op jit(solution)/shard_map/ppermute | solution.py:849
  216.1 5.5 %collective-permute-done.19 = bf16[48,576]{1,0:T(8,128)(2,1)S(1)} collective-permute-done((bf16[48,576]{1,0:T(8,128)(2,1)S(1)}, bf16[48,576]{1,0:T(8,128)(2,1)S(1)}, u32[]{:S(2)}, u32[]{:S(2)}) %collective-permute-start.19) | collective-permute-done | bytes 55328 | tf_op jit(solution)/shard_map/ppermute | solution.py:849
  222.2 7.1 %weight_grad.5 = (f32[288,432]{1,0:T(8,128)}, bf16[288,432]{1,0:T(8,128)(2,1)}, bf16[288,432]{1,0:T(8,128)(2,1)}, bf16[288,432]{1,0:T(8,128)(2,1)}) custom-call(s32[23]{0:T(128)} %plan.1.refs_0_.scalars, bf16[3072,1280]{1,0:T(8,128)(2,1)} %all-gather.3.cloned.1.call-done.refs_1_, bf16[384,432]{1,0:T(8,128)(2,1)} %get-tuple-element.183.refs_2_, ...), custom_call_target="tpu_custom_call" | custom-call | flops 1528823 | bytes 10435 | tf_op jit(solution)/shard_map/weight_grad/pallas_call | solution.py:46
  229.3 2.4 collective-permute-done.21
  232.3 1.6 collective-permute-start.25
  233.9 2.6 collective-permute-start.23
  236.5 1.5 collective-permute-start.24
  238.0 8.2 %collective-permute-done.25.refs_3_ = bf16[192,576]{1,0:T(8,128)(2,1)S(1)} collective-permute-done((bf16[192,576]{1,0:T(8,128)(2,1)S(1)}, bf16[192,576]{1,0:T(8,128)(2,1)S(1)}, u32[]{:S(2)}, u32[]{:S(2)}) %collective-permute-start.25) | collective-permute-done | bytes 221216 | tf_op jit(solution)/shard_map/ppermute | solution.py:849
  246.3 2.0 collective-permute-start.30
  248.3 4.3 %fusion.2 = bf16[1,768,1152]{2,1,0:T(8,128)(2,1)} fusion(bf16[384,1152]{1,0:T(8,128)(2,1)} %get-tuple-element.201, bf16[1,768,1152]{2,1,0:T(8,128)(2,1)} %param.15, pred[768]{0:T(1024)(128)(4,1)S(1)} %broadcast_compare_fusion, s32[384]{0:T(512)S(1)} %subtract_reduce_fusion), kind=kOutput, calls=%fused_computation.5 | convolution fusion | flops 681541632 | bytes 4425984 | tf_op jit(solution)/shard_map/dot_general | solution.py:32
  252.8 5.1 %collective-permute-done.23 = bf16[288,432]{1,0:T(8,128)(2,1)S(1)} collective-permute-done((bf16[288,432]{1,0:T(8,128)(2,1)}, bf16[288,432]{1,0:T(8,128)(2,1)S(1)}, u32[]{:S(2)}, u32[]{:S(2)}) %collective-permute-start.23) | collective-permute-done | bytes 248864 | tf_op jit(solution)/shard_map/ppermute | solution.py:911
  257.9 1.4 collective-permute-start.27
  259.6 10.8 %collective-permute-done.26.refs_4_ = bf16[192,576]{1,0:T(8,128)(2,1)S(1)} collective-permute-done((bf16[192,576]{1,0:T(8,128)(2,1)S(1)}, bf16[192,576]{1,0:T(8,128)(2,1)S(1)}, u32[]{:S(2)}, u32[]{:S(2)}) %collective-permute-start.26) | collective-permute-done | bytes 221216 | tf_op jit(solution)/shard_map/ppermute | solution.py:849
  270.4 2.6 collective-permute-done.27.refs_5_
  273.0 2.5 collective-permute-start.32
  275.9 4.6 %spread.1 = (f32[6,288,576]{2,1,0:T(8,128)}, f32[6,576]{1,0:T(8,128)}, f32[24,576]{1,0:T(8,128)}, f32[9,6,576]{2,1,0:T(8,128)}) custom-call(s32[23]{0:T(128)} %plan.1.refs_0_.scalars, s32[1536]{0:T(1024)} %reduce.refs_1_, bf16[192,576]{1,0:T(8,128)(2,1)} %copy-done.18, bf16[192,576]{1,0:T(8,128)(2,1)} %copy-done.34, bf16[192,576]{1,0:T(8,128)(2,1)} %copy-done.35, ...), custom_call_target="tpu_custom_call" | custom-call | bytes 5065 | tf_op jit(solution)/shard_map/spread/pallas_call | solution.py:46
  283.1 4.5 %convolution_bitcast_fusion = f32[18,1152]{1,0:T(8,128)S(1)} fusion(bf16[1152,6,576]{0,2,1:T(8,128)(2,1)} %param.28, bf16[18,6,576]{2,1,0:T(8,128)(2,1)S(1)} %pad_maximum_fusion), kind=kOutput, calls=%fused_computation.11 | convolution fusion | flops 143327232 | bytes 8169984 | tf_op jit(solution)/shard_map/sgf,dgf->sd/dot_general | solution.py:1115
  287.8 1.8 collective-permute-start.34
  289.7 7.5 %collective-permute-done.34.refs_4_ = bf16[288,432]{1,0:T(8,128)(2,1)S(1)} collective-permute-done((bf16[288,432]{1,0:T(8,128)(2,1)S(1)}, bf16[288,432]{1,0:T(8,128)(2,1)S(1)}, u32[]{:S(2)}, u32[]{:S(2)}) %collective-permute-start.34) | collective-permute-done | bytes 248864 | tf_op jit(solution)/shard_map/ppermute | solution.py:849
  297.2 1.7 collective-permute-start.39
  301.8 3.2 join_down.1
  305.0 2.0 collective-permute-start.38
  307.3 3.5 %collective-permute-done.35.refs_2_ = bf16[288,576]{1,0:T(8,128)(2,1)S(1)} collective-permute-done((bf16[288,576]{1,0:T(8,128)(2,1)}, bf16[288,576]{1,0:T(8,128)(2,1)S(1)}, u32[]{:S(2)}, u32[]{:S(2)}) %collective-permute-start.35) | collective-permute-done | bytes 331808 | tf_op jit(solution)/shard_map/ppermute | solution.py:849
  311.9 3.1 join_qkv.1
  315.0 3.6 %collective-permute-done.36.refs_3_ = bf16[288,576]{1,0:T(8,128)(2,1)S(1)} collective-permute-done((bf16[288,576]{1,0:T(8,128)(2,1)S(1)}, bf16[288,576]{1,0:T(8,128)(2,1)S(1)}, u32[]{:S(2)}, u32[]{:S(2)}) %collective-permute-start.36) | collective-permute-done | bytes 331808 | tf_op jit(solution)/shard_map/ppermute | solution.py:849
  318.6 5.7 %collective-permute-done.37.refs_4_ = bf16[288,576]{1,0:T(8,128)(2,1)S(1)} collective-permute-done((bf16[288,576]{1,0:T(8,128)(2,1)S(1)}, bf16[288,576]{1,0:T(8,128)(2,1)S(1)}, u32[]{:S(2)}, u32[]{:S(2)}) %collective-permute-start.37) | collective-permute-done | bytes 331808 | tf_op jit(solution)/shard_map/ppermute | solution.py:849
  325.1 2.7 join_output.1
  329.2 3.1 join_hidden.1
  (206 shorter events, 33.0 us)
Async XLA Ops:
  7.2 114.4 %all-gather.3.cloned.1.call-start = ((), (), s32[]{:S(2)}) async-start(), calls=%async_computation.3 | async-start | bytes 8847360 | tf_op jit(solution)/shard_map/all_gather | solution.py:897
  7.9 12.6 %copy-start.40 = (bf16[6,576]{1,0:T(8,128)(2,1)S(1)}, bf16[6,576]{1,0:T(8,128)(2,1)}, u32[]{:S(2)}) copy-start(bf16[6,576]{1,0:T(8,128)(2,1)} %param.29) | copy-start | bytes 20740
  7.9 13.3 %copy-start.30 = (bf16[1,9,1152]{2,1,0:T(8,128)(2,1)S(1)}, bf16[1,9,1152]{2,1,0:T(8,128)(2,1)}, u32[]{:S(2)}) copy-start(bf16[1,9,1152]{2,1,0:T(8,128)(2,1)} %param.16) | copy-start | bytes 62212
  10.5 16.3 %copy-start = (bf16[384,1152]{1,0:T(8,128)(2,1)}, bf16[384,1152]{1,0:T(8,128)(2,1)S(1)}, u32[]{:S(2)}) copy-start(bf16[384,1152]{1,0:T(8,128)(2,1)S(1)} %convolution_convert_fusion.4.own_ref.kept_ref) | copy-start | bytes 2654212
  10.5 16.3 %collective-permute-start = (bf16[192,1152]{1,0:T(8,128)(2,1)S(1)}, bf16[192,1152]{1,0:T(8,128)(2,1)S(1)}, u32[]{:S(2)}, u32[]{:S(2)}) collective-permute-start(bf16[192,1152]{1,0:T(8,128)(2,1)S(1)} %constant_dynamic-slice_fusion), channel_id=1, source_target_pairs={{0,2},{2,4},{4,6},{1,3},{3,5},{5,7},{8,10},{10,12},{12,14},{9,11},... | collective-permute-start | bytes 1327112 | tf_op jit(solution)/shard_map/ppermute | solution.py:859
  15.5 13.5 %collective-permute-start.1 = (bf16[192,1152]{1,0:T(8,128)(2,1)S(1)}, bf16[192,1152]{1,0:T(8,128)(2,1)S(1)}, u32[]{:S(2)}, u32[]{:S(2)}) collective-permute-start(bf16[192,1152]{1,0:T(8,128)(2,1)S(1)} %constant_dynamic-slice_fusion), channel_id=1, source_target_pairs={{2,0},{4,2},{6,4},{3,1},{5,3},{7,5},{10,8},{12,10},{14,12},{11,9},... | collective-permute-start | bytes 1327112 | tf_op jit(solution)/shard_map/ppermute | solution.py:859
  29.1 5.5 %collective-permute-start.2 = (bf16[192,1152]{1,0:T(8,128)(2,1)S(1)}, bf16[192,1152]{1,0:T(8,128)(2,1)S(1)}, u32[]{:S(2)}, u32[]{:S(2)}) collective-permute-start(bf16[192,1152]{1,0:T(8,128)(2,1)S(1)} %broadcast_select_fusion.1), channel_id=1, source_target_pairs={{0,1},{1,0},{2,3},{3,2},{4,5},{5,4},{6,7},{7,6},{8,9},{9,8},{10,11... | collective-permute-start | bytes 1327112 | tf_op jit(solution)/shard_map/ppermute | solution.py:849
  29.2 2.5 collective-permute-start.3
  42.0 146.8 %all-gather.5.cloned.1.call-start = ((), (), s32[]{:S(2)}) async-start(), calls=%async_computation.4 | async-start | bytes 4423680 | tf_op jit(solution)/shard_map/all_gather | solution.py:897
  50.9 12.4 %copy-start.3 = (f32[6,6,1152]{2,1,0:T(8,128)S(1)}, f32[6,6,1152]{2,1,0:T(8,128)}, u32[]{:S(2)}) copy-start(f32[6,6,1152]{2,1,0:T(8,128)} %pick.1.mod_ref) | copy-start | bytes 497668
  62.0 3.9 %collective-permute-start.4 = (f32[384,1152]{1,0:T(8,128)}, f32[384,1152]{1,0:T(8,128)S(1)}, u32[]{:S(2)}, u32[]{:S(2)}) collective-permute-start(f32[384,1152]{1,0:T(8,128)} %get-tuple-element.122.term_ref), channel_id=1, source_target_pairs={{0,1},{1,0},{2,3},{3,2},{4,5},{5,4},{6,7},{7,6},{8,9},{9,8},{10,11... | collective-permute-start | bytes 5308424 | tf_op jit(solution)/shard_map/ppermute | solution.py:849
  79.2 152.5 %reduce-scatter.4.cloned.1.call-start = ((), (), s32[]{:S(2)}) async-start(), calls=%async_computation.5 | async-start | bytes 1843200 | tf_op jit(solution)/shard_map/reduce_scatter | solution.py:1043
  79.8 24.0 %collective-permute-start.5 = (bf16[384,640]{1,0:T(8,128)(2,1)}, bf16[384,640]{1,0:T(8,128)(2,1)S(1)}, u32[]{:S(2)}, u32[]{:S(2)}) collective-permute-start(bf16[384,640]{1,0:T(8,128)(2,1)} %get-tuple-element.125), channel_id=1, source_target_pairs={{0,8},{8,0},{16,24},{24,16},{1,9},{9,1},{17,25},{25,17},{2,10},{10... | collective-permute-start | bytes 1474568 | tf_op jit(solution)/shard_map/ppermute | solution.py:849
  82.3 21.5 %collective-permute-start.6 = (bf16[384,640]{1,0:T(8,128)(2,1)}, bf16[384,640]{1,0:T(8,128)(2,1)S(1)}, u32[]{:S(2)}, u32[]{:S(2)}) collective-permute-start(bf16[384,640]{1,0:T(8,128)(2,1)} %get-tuple-element.126), channel_id=1, source_target_pairs={{0,16},{8,24},{16,0},{24,8},{1,17},{9,25},{17,1},{25,9},{2,18},{10... | collective-permute-start | bytes 1474568 | tf_op jit(solution)/shard_map/ppermute | solution.py:849
  83.9 20.9 %copy-start.49 = (bf16[384,640]{1,0:T(8,128)(2,1)S(1)}, bf16[384,640]{1,0:T(8,128)(2,1)}, u32[]{:S(2)}) copy-start(bf16[384,640]{1,0:T(8,128)(2,1)} %get-tuple-element.136) | copy-start | bytes 1474564
  104.8 3.9 %collective-permute-start.7 = (f32[384,1152]{1,0:T(8,128)}, f32[384,1152]{1,0:T(8,128)S(1)}, u32[]{:S(2)}, u32[]{:S(2)}) collective-permute-start(f32[384,1152]{1,0:T(8,128)} %get-tuple-element.133.term_ref), channel_id=1, source_target_pairs={{0,1},{1,0},{2,3},{3,2},{4,5},{5,4},{6,7},{7,6},{8,9},{9,8},{10,11... | collective-permute-start | bytes 5308424 | tf_op jit(solution)/shard_map/ppermute | solution.py:849
  104.8 16.7 %collective-permute-start.8 = (bf16[384,640]{1,0:T(8,128)(2,1)S(1)}, bf16[384,640]{1,0:T(8,128)(2,1)S(1)}, u32[]{:S(2)}, u32[]{:S(2)}) collective-permute-start(bf16[384,640]{1,0:T(8,128)(2,1)S(1)} %copy-done.49), channel_id=1, source_target_pairs={{0,24},{8,16},{16,8},{24,0},{1,25},{9,17},{17,9},{25,1},{2,26},{10... | collective-permute-start | bytes 1474568 | tf_op jit(solution)/shard_map/ppermute | solution.py:849
  117.5 12.7 %copy-start.48 = (bf16[384,640]{1,0:T(8,128)(2,1)S(1)}, bf16[384,640]{1,0:T(8,128)(2,1)}, u32[]{:S(2)}) copy-start(bf16[384,640]{1,0:T(8,128)(2,1)} %get-tuple-element.153) | copy-start | bytes 1474564
  117.5 13.9 %copy-start.47 = (bf16[384,640]{1,0:T(8,128)(2,1)S(1)}, bf16[384,640]{1,0:T(8,128)(2,1)}, u32[]{:S(2)}) copy-start(bf16[384,640]{1,0:T(8,128)(2,1)} %get-tuple-element.154) | copy-start | bytes 1474564
  121.6 24.3 %collective-permute-start.10 = (bf16[384,576]{1,0:T(8,128)(2,1)S(1)}, bf16[384,576]{1,0:T(8,128)(2,1)}, u32[]{:S(2)}, u32[]{:S(2)}) collective-permute-start(bf16[384,576]{1,0:T(8,128)(2,1)S(1)} %copy-done.11), channel_id=1, source_target_pairs={{2,0},{4,2},{6,4},{3,1},{5,3},{7,5},{10,8},{12,10},{14,12},{11,9},... | collective-permute-start | bytes 1327112 | tf_op jit(solution)/shard_map/ppermute | solution.py:859
  122.9 23.0 %collective-permute-start.9 = (bf16[384,576]{1,0:T(8,128)(2,1)S(1)}, bf16[384,576]{1,0:T(8,128)(2,1)}, u32[]{:S(2)}, u32[]{:S(2)}) collective-permute-start(bf16[384,576]{1,0:T(8,128)(2,1)S(1)} %copy-done.11), channel_id=1, source_target_pairs={{0,2},{2,4},{4,6},{1,3},{3,5},{5,7},{8,10},{10,12},{12,14},{9,11},... | collective-permute-start | bytes 1327112 | tf_op jit(solution)/shard_map/ppermute | solution.py:859
  128.2 24.7 %collective-permute-start.11 = (bf16[384,640]{1,0:T(8,128)(2,1)}, bf16[384,640]{1,0:T(8,128)(2,1)S(1)}, u32[]{:S(2)}, u32[]{:S(2)}) collective-permute-start(bf16[384,640]{1,0:T(8,128)(2,1)} %get-tuple-element.152), channel_id=1, source_target_pairs={{0,8},{8,0},{16,24},{24,16},{1,9},{9,1},{17,25},{25,17},{2,10},{10... | collective-permute-start | bytes 1474568 | tf_op jit(solution)/shard_map/ppermute | solution.py:849
  130.3 31.0 %collective-permute-start.12 = (bf16[384,640]{1,0:T(8,128)(2,1)S(1)}, bf16[384,640]{1,0:T(8,128)(2,1)S(1)}, u32[]{:S(2)}, u32[]{:S(2)}) collective-permute-start(bf16[384,640]{1,0:T(8,128)(2,1)S(1)} %copy-done.48), channel_id=1, source_target_pairs={{0,16},{8,24},{16,0},{24,8},{1,17},{9,25},{17,1},{25,9},{2,18},{10... | collective-permute-start | bytes 1474568 | tf_op jit(solution)/shard_map/ppermute | solution.py:849
  131.4 31.5 %collective-permute-start.13 = (bf16[384,640]{1,0:T(8,128)(2,1)S(1)}, bf16[384,640]{1,0:T(8,128)(2,1)}, u32[]{:S(2)}, u32[]{:S(2)}) collective-permute-start(bf16[384,640]{1,0:T(8,128)(2,1)S(1)} %copy-done.47), channel_id=1, source_target_pairs={{0,24},{8,16},{16,8},{24,0},{1,25},{9,17},{17,9},{25,1},{2,26},{10... | collective-permute-start | bytes 1474568 | tf_op jit(solution)/shard_map/ppermute | solution.py:849
  137.6 40.4 %copy-start.6 = (bf16[384,1152]{1,0:T(8,128)(2,1)}, bf16[384,1152]{1,0:T(8,128)(2,1)S(1)}, u32[]{:S(2)}) copy-start(bf16[384,1152]{1,0:T(8,128)(2,1)S(1)} %convolution_convert_fusion.2.term_ref) | copy-start | bytes 2654212
  152.9 25.1 %copy-start.10 = (bf16[384,640]{1,0:T(8,128)(2,1)}, bf16[384,640]{1,0:T(8,128)(2,1)S(1)}, u32[]{:S(2)}) copy-start(bf16[384,640]{1,0:T(8,128)(2,1)S(1)} %collective-permute-done.11.refs_3_) | copy-start | bytes 1474564
  161.3 16.8 %copy-start.12 = (bf16[384,640]{1,0:T(8,128)(2,1)}, bf16[384,640]{1,0:T(8,128)(2,1)S(1)}, u32[]{:S(2)}) copy-start(bf16[384,640]{1,0:T(8,128)(2,1)S(1)} %collective-permute-done.12.refs_4_) | copy-start | bytes 1474564
  163.0 126.7 %reduce-scatter.6.cloned.1.call-start = ((), (), s32[]{:S(2)}) async-start(), calls=%async_computation.6 | async-start | bytes 1843200 | tf_op jit(solution)/shard_map/reduce_scatter | solution.py:1044
  163.5 126.1 %reduce-scatter.8.cloned.1.call-start = ((), (), s32[]{:S(2)}) async-start(), calls=%async_computation.7 | async-start | bytes 1843200 | tf_op jit(solution)/shard_map/reduce_scatter | solution.py:1086
  163.8 24.4 %copy-start.44 = (bf16[1152]{0:T(1024)(128)(2,1)S(1)}, bf16[1152]{0:T(1024)(128)(2,1)}, u32[]{:S(2)}) copy-start(bf16[1152]{0:T(1024)(128)(2,1)} %param.27) | copy-start | bytes 6916
  178.1 17.5 %collective-permute-start.18 = (bf16[384,1152]{1,0:T(8,128)(2,1)S(1)}, bf16[384,1152]{1,0:T(8,128)(2,1)S(1)}, u32[]{:S(2)}, u32[]{:S(2)}) collective-permute-start(bf16[384,1152]{1,0:T(8,128)(2,1)S(1)} %convolution_convert_fusion.2.term_ref), channel_id=1, source_target_pairs={{0,1},{1,0},{2,3},{3,2},{4,5},{5,4},{6,7},{7,6},{8,9},{9,8},{10,11... | collective-permute-start | bytes 2654216 | tf_op jit(solution)/shard_map/ppermute | solution.py:849
  178.2 22.9 %collective-permute-start.17 = (bf16[384,1152]{1,0:T(8,128)(2,1)}, bf16[384,1152]{1,0:T(8,128)(2,1)S(1)}, u32[]{:S(2)}, u32[]{:S(2)}) collective-permute-start(bf16[384,1152]{1,0:T(8,128)(2,1)} %get-tuple-element.166.term_ref), channel_id=1, source_target_pairs={{0,1},{1,0},{2,3},{3,2},{4,5},{5,4},{6,7},{7,6},{8,9},{9,8},{10,11... | collective-permute-start | bytes 2654216 | tf_op jit(solution)/shard_map/ppermute | solution.py:849
  179.5 32.7 %collective-permute-start.14 = (bf16[384,432]{1,0:T(8,128)(2,1)}, bf16[384,432]{1,0:T(8,128)(2,1)S(1)}, u32[]{:S(2)}, u32[]{:S(2)}) collective-permute-start(bf16[384,432]{1,0:T(8,128)(2,1)} %get-tuple-element.163), channel_id=1, source_target_pairs={{0,8},{8,0},{16,24},{24,16},{1,9},{9,1},{17,25},{25,17},{2,10},{10... | collective-permute-start | bytes 995336 | tf_op jit(solution)/shard_map/ppermute | solution.py:849
  186.7 25.6 %collective-permute-start.15 = (bf16[384,432]{1,0:T(8,128)(2,1)}, bf16[384,432]{1,0:T(8,128)(2,1)S(1)}, u32[]{:S(2)}, u32[]{:S(2)}) collective-permute-start(bf16[384,432]{1,0:T(8,128)(2,1)} %get-tuple-element.164), channel_id=1, source_target_pairs={{0,16},{8,24},{16,0},{24,8},{1,17},{9,25},{17,1},{25,9},{2,18},{10... | collective-permute-start | bytes 995336 | tf_op jit(solution)/shard_map/ppermute | solution.py:849
  186.7 25.6 %collective-permute-start.16 = (bf16[384,432]{1,0:T(8,128)(2,1)}, bf16[384,432]{1,0:T(8,128)(2,1)}, u32[]{:S(2)}, u32[]{:S(2)}) collective-permute-start(bf16[384,432]{1,0:T(8,128)(2,1)} %get-tuple-element.165), channel_id=1, source_target_pairs={{0,24},{8,16},{16,8},{24,0},{1,25},{9,17},{17,9},{25,1},{2,26},{10... | collective-permute-start | bytes 995336 | tf_op jit(solution)/shard_map/ppermute | solution.py:849
  212.3 9.3 %collective-permute-start.19 = (bf16[48,576]{1,0:T(8,128)(2,1)S(1)}, bf16[48,576]{1,0:T(8,128)(2,1)S(1)}, u32[]{:S(2)}, u32[]{:S(2)}) collective-permute-start(bf16[48,576]{1,0:T(8,128)(2,1)S(1)} %copy-done.37), channel_id=1, source_target_pairs={{0,2},{2,0},{4,6},{6,4},{1,3},{3,1},{5,7},{7,5},{8,10},{10,8},{12,... | collective-permute-start | bytes 165896 | tf_op jit(solution)/shard_map/ppermute | solution.py:849
  212.3 17.0 %collective-permute-start.20 = (bf16[48,576]{1,0:T(8,128)(2,1)S(1)}, bf16[48,576]{1,0:T(8,128)(2,1)S(1)}, u32[]{:S(2)}, u32[]{:S(2)}) collective-permute-start(bf16[48,576]{1,0:T(8,128)(2,1)S(1)} %copy-done.37), channel_id=1, source_target_pairs={{0,4},{2,6},{4,0},{6,2},{1,5},{3,7},{5,1},{7,3},{8,12},{10,14},{12... | collective-permute-start | bytes 165896 | tf_op jit(solution)/shard_map/ppermute | solution.py:849
  221.6 10.1 %collective-permute-start.21 = (bf16[48,576]{1,0:T(8,128)(2,1)S(1)}, bf16[48,576]{1,0:T(8,128)(2,1)S(1)}, u32[]{:S(2)}, u32[]{:S(2)}) collective-permute-start(bf16[48,576]{1,0:T(8,128)(2,1)S(1)} %collective-permute-done.19), channel_id=1, source_target_pairs={{0,4},{2,6},{4,0},{6,2},{1,5},{3,7},{5,1},{7,3},{8,12},{10,14},{12... | collective-permute-start | bytes 165896 | tf_op jit(solution)/shard_map/ppermute | solution.py:849
  231.7 14.5 %collective-permute-start.28 = (bf16[288,640]{1,0:T(8,128)(2,1)}, bf16[288,640]{1,0:T(8,128)(2,1)S(1)}, u32[]{:S(2)}, u32[]{:S(2)}) collective-permute-start(bf16[288,640]{1,0:T(8,128)(2,1)} %reduce-scatter.4.cloned.1.call-done.refs_1_), channel_id=1, source_target_pairs={{0,8},{8,0},{16,24},{24,16},{1,9},{9,1},{17,25},{25,17},{2,10},{10... | collective-permute-start | bytes 1105928 | tf_op jit(solution)/shard_map/ppermute | solution.py:849
  232.3 20.3 %copy-start.18 = (bf16[192,576]{1,0:T(8,128)(2,1)}, bf16[192,576]{1,0:T(8,128)(2,1)S(1)}, u32[]{:S(2)}) copy-start(bf16[192,576]{1,0:T(8,128)(2,1)S(1)} %constant_dynamic-update-slice_fusion.refs_2_) | copy-start | bytes 663556
  232.3 27.1 %copy-start.9 = (f32[288,432]{1,0:T(8,128)S(1)}, f32[288,432]{1,0:T(8,128)}, u32[]{:S(2)}) copy-start(f32[288,432]{1,0:T(8,128)} %get-tuple-element.193) | copy-start | bytes 1492996
  232.3 13.9 %collective-permute-start.25 = (bf16[192,576]{1,0:T(8,128)(2,1)S(1)}, bf16[192,576]{1,0:T(8,128)(2,1)S(1)}, u32[]{:S(2)}, u32[]{:S(2)}) collective-permute-start(bf16[192,576]{1,0:T(8,128)(2,1)S(1)} %constant_dynamic-update-slice_fusion.refs_2_), channel_id=1, source_target_pairs={{0,8},{8,0},{16,24},{24,16},{1,9},{9,1},{17,25},{25,17},{2,10},{10... | collective-permute-start | bytes 663560 | tf_op jit(solution)/shard_map/ppermute | solution.py:849
  233.9 18.7 %collective-permute-start.22 = (bf16[288,432]{1,0:T(8,128)(2,1)}, bf16[288,432]{1,0:T(8,128)(2,1)S(1)}, u32[]{:S(2)}, u32[]{:S(2)}) collective-permute-start(bf16[288,432]{1,0:T(8,128)(2,1)} %get-tuple-element.194), channel_id=1, source_target_pairs={{0,2},{2,4},{4,6},{6,0},{1,3},{3,5},{5,7},{7,1},{8,10},{10,12},{12... | collective-permute-start | bytes 746504 | tf_op jit(solution)/shard_map/ppermute | solution.py:911
  233.9 24.0 %collective-permute-start.23 = (bf16[288,432]{1,0:T(8,128)(2,1)}, bf16[288,432]{1,0:T(8,128)(2,1)S(1)}, u32[]{:S(2)}, u32[]{:S(2)}) collective-permute-start(bf16[288,432]{1,0:T(8,128)(2,1)} %get-tuple-element.195), channel_id=1, source_target_pairs={{0,4},{2,6},{4,0},{6,2},{1,5},{3,7},{5,1},{7,3},{8,12},{10,14},{12... | collective-permute-start | bytes 746504 | tf_op jit(solution)/shard_map/ppermute | solution.py:911
  236.5 22.8 %collective-permute-start.24 = (bf16[288,432]{1,0:T(8,128)(2,1)}, bf16[288,432]{1,0:T(8,128)(2,1)S(1)}, u32[]{:S(2)}, u32[]{:S(2)}) collective-permute-start(bf16[288,432]{1,0:T(8,128)(2,1)} %get-tuple-element.196), channel_id=1, source_target_pairs={{0,6},{2,0},{4,2},{6,4},{1,7},{3,1},{5,3},{7,5},{8,14},{10,8},{12,... | collective-permute-start | bytes 746504 | tf_op jit(solution)/shard_map/ppermute | solution.py:911
  246.2 26.8 %collective-permute-start.29 = (bf16[288,640]{1,0:T(8,128)(2,1)}, bf16[288,640]{1,0:T(8,128)(2,1)S(1)}, u32[]{:S(2)}, u32[]{:S(2)}) collective-permute-start(bf16[288,640]{1,0:T(8,128)(2,1)} %reduce-scatter.4.cloned.1.call-done.refs_1_), channel_id=1, source_target_pairs={{0,16},{8,24},{16,0},{24,8},{1,17},{9,25},{17,1},{25,9},{2,18},{10... | collective-permute-start | bytes 1105928 | tf_op jit(solution)/shard_map/ppermute | solution.py:849
  246.3 26.7 %collective-permute-start.30 = (bf16[288,640]{1,0:T(8,128)(2,1)S(1)}, bf16[288,640]{1,0:T(8,128)(2,1)S(1)}, u32[]{:S(2)}, u32[]{:S(2)}) collective-permute-start(bf16[288,640]{1,0:T(8,128)(2,1)S(1)} %collective-permute-done.28.refs_2_), channel_id=1, source_target_pairs={{0,16},{8,24},{16,0},{24,8},{1,17},{9,25},{17,1},{25,9},{2,18},{10... | collective-permute-start | bytes 1105928 | tf_op jit(solution)/shard_map/ppermute | solution.py:849
  252.6 17.7 %collective-permute-start.26 = (bf16[192,576]{1,0:T(8,128)(2,1)S(1)}, bf16[192,576]{1,0:T(8,128)(2,1)S(1)}, u32[]{:S(2)}, u32[]{:S(2)}) collective-permute-start(bf16[192,576]{1,0:T(8,128)(2,1)S(1)} %constant_dynamic-update-slice_fusion.refs_2_), channel_id=1, source_target_pairs={{0,16},{8,24},{16,0},{24,8},{1,17},{9,25},{17,1},{25,9},{2,18},{10... | collective-permute-start | bytes 663560 | tf_op jit(solution)/shard_map/ppermute | solution.py:849
  257.9 15.1 %collective-permute-start.27 = (bf16[192,576]{1,0:T(8,128)(2,1)S(1)}, bf16[192,576]{1,0:T(8,128)(2,1)S(1)}, u32[]{:S(2)}, u32[]{:S(2)}) collective-permute-start(bf16[192,576]{1,0:T(8,128)(2,1)S(1)} %collective-permute-done.25.refs_3_), channel_id=1, source_target_pairs={{0,16},{8,24},{16,0},{24,8},{1,17},{9,25},{17,1},{25,9},{2,18},{10... | collective-permute-start | bytes 663560 | tf_op jit(solution)/shard_map/ppermute | solution.py:849
  259.5 28.1 %copy-start.4 = (bf16[288,432]{1,0:T(8,128)(2,1)}, bf16[288,432]{1,0:T(8,128)(2,1)S(1)}, u32[]{:S(2)}) copy-start(bf16[288,432]{1,0:T(8,128)(2,1)S(1)} %add_convert_fusion.1.refs_1_) | copy-start | bytes 746500
  273.0 14.6 %copy-start.25 = (bf16[288,640]{1,0:T(8,128)(2,1)}, bf16[288,640]{1,0:T(8,128)(2,1)S(1)}, u32[]{:S(2)}) copy-start(bf16[288,640]{1,0:T(8,128)(2,1)S(1)} %collective-permute-done.29.refs_3_) | copy-start | bytes 1105924
  273.0 14.6 %copy-start.26 = (bf16[288,640]{1,0:T(8,128)(2,1)}, bf16[288,640]{1,0:T(8,128)(2,1)S(1)}, u32[]{:S(2)}) copy-start(bf16[288,640]{1,0:T(8,128)(2,1)S(1)} %collective-permute-done.30.refs_4_) | copy-start | bytes 1105924
  273.0 14.7 %collective-permute-start.32 = (bf16[288,432]{1,0:T(8,128)(2,1)S(1)}, bf16[288,432]{1,0:T(8,128)(2,1)S(1)}, u32[]{:S(2)}, u32[]{:S(2)}) collective-permute-start(bf16[288,432]{1,0:T(8,128)(2,1)S(1)} %add_convert_fusion.1.refs_1_), channel_id=1, source_target_pairs={{0,8},{8,0},{16,24},{24,16},{1,9},{9,1},{17,25},{25,17},{2,10},{10... | collective-permute-start | bytes 746504 | tf_op jit(solution)/shard_map/ppermute | solution.py:849
  275.6 14.1 %collective-permute-start.33 = (bf16[288,432]{1,0:T(8,128)(2,1)S(1)}, bf16[288,432]{1,0:T(8,128)(2,1)S(1)}, u32[]{:S(2)}, u32[]{:S(2)}) collective-permute-start(bf16[288,432]{1,0:T(8,128)(2,1)S(1)} %add_convert_fusion.1.refs_1_), channel_id=1, source_target_pairs={{0,16},{8,24},{16,0},{24,8},{1,17},{9,25},{17,1},{25,9},{2,18},{10... | collective-permute-start | bytes 746504 | tf_op jit(solution)/shard_map/ppermute | solution.py:849
  287.6 23.5 %collective-permute-start.31 = (f32[9,1152]{1,0:T(8,128)S(1)}, f32[9,1152]{1,0:T(8,128)S(1)}, u32[]{:S(2)}, u32[]{:S(2)}) collective-permute-start(f32[9,1152]{1,0:T(8,128)S(1)} %slice_add_fusion), channel_id=1, source_target_pairs={{0,1},{1,0},{2,3},{3,2},{4,5},{5,4},{6,7},{7,6},{8,9},{9,8},{10,11... | collective-permute-start | bytes 124424 | tf_op jit(solution)/shard_map/ppermute | solution.py:849
  287.8 17.3 %copy-start.31 = (bf16[288,432]{1,0:T(8,128)(2,1)}, bf16[288,432]{1,0:T(8,128)(2,1)S(1)}, u32[]{:S(2)}) copy-start(bf16[288,432]{1,0:T(8,128)(2,1)S(1)} %collective-permute-done.32.refs_2_) | copy-start | bytes 746500
  287.8 9.5 %collective-permute-start.34 = (bf16[288,432]{1,0:T(8,128)(2,1)S(1)}, bf16[288,432]{1,0:T(8,128)(2,1)S(1)}, u32[]{:S(2)}, u32[]{:S(2)}) collective-permute-start(bf16[288,432]{1,0:T(8,128)(2,1)S(1)} %collective-permute-done.32.refs_2_), channel_id=1, source_target_pairs={{0,16},{8,24},{16,0},{24,8},{1,17},{9,25},{17,1},{25,9},{2,18},{10... | collective-permute-start | bytes 746504 | tf_op jit(solution)/shard_map/ppermute | solution.py:849
  289.7 15.3 %copy-start.32 = (bf16[288,432]{1,0:T(8,128)(2,1)}, bf16[288,432]{1,0:T(8,128)(2,1)S(1)}, u32[]{:S(2)}) copy-start(bf16[288,432]{1,0:T(8,128)(2,1)S(1)} %collective-permute-done.33.refs_3_) | copy-start | bytes 746500
  297.2 13.9 %collective-permute-start.39 = (bf16[288,640]{1,0:T(8,128)(2,1)}, bf16[288,640]{1,0:T(8,128)(2,1)S(1)}, u32[]{:S(2)}, u32[]{:S(2)}) collective-permute-start(bf16[288,640]{1,0:T(8,128)(2,1)} %reduce-scatter.8.cloned.1.call-done.refs_1_), channel_id=1, source_target_pairs={{0,16},{8,24},{16,0},{24,8},{1,17},{9,25},{17,1},{25,9},{2,18},{10... | collective-permute-start | bytes 1105928 | tf_op jit(solution)/shard_map/ppermute | solution.py:849
  299.0 11.8 %collective-permute-start.35 = (bf16[288,576]{1,0:T(8,128)(2,1)}, bf16[288,576]{1,0:T(8,128)(2,1)S(1)}, u32[]{:S(2)}, u32[]{:S(2)}) collective-permute-start(bf16[288,576]{1,0:T(8,128)(2,1)} %reduce-scatter.6.cloned.1.call-done.refs_1_), channel_id=1, source_target_pairs={{0,8},{8,0},{16,24},{24,16},{1,9},{9,1},{17,25},{25,17},{2,10},{10... | collective-permute-start | bytes 995336 | tf_op jit(solution)/shard_map/ppermute | solution.py:849
  305.0 22.7 %collective-permute-start.38 = (bf16[288,640]{1,0:T(8,128)(2,1)S(1)}, bf16[288,640]{1,0:T(8,128)(2,1)S(1)}, u32[]{:S(2)}, u32[]{:S(2)}) collective-permute-start(bf16[288,640]{1,0:T(8,128)(2,1)S(1)} %copy-done.23), channel_id=1, source_target_pairs={{0,8},{8,0},{16,24},{24,16},{1,9},{9,1},{17,25},{25,17},{2,10},{10... | collective-permute-start | bytes 1105928 | tf_op jit(solution)/shard_map/ppermute | solution.py:849
  307.1 11.5 %collective-permute-start.36 = (bf16[288,576]{1,0:T(8,128)(2,1)S(1)}, bf16[288,576]{1,0:T(8,128)(2,1)S(1)}, u32[]{:S(2)}, u32[]{:S(2)}) collective-permute-start(bf16[288,576]{1,0:T(8,128)(2,1)S(1)} %copy-done.19), channel_id=1, source_target_pairs={{0,16},{8,24},{16,0},{24,8},{1,17},{9,25},{17,1},{25,9},{2,18},{10... | collective-permute-start | bytes 995336 | tf_op jit(solution)/shard_map/ppermute | solution.py:849
  310.8 13.5 %collective-permute-start.37 = (bf16[288,576]{1,0:T(8,128)(2,1)S(1)}, bf16[288,576]{1,0:T(8,128)(2,1)S(1)}, u32[]{:S(2)}, u32[]{:S(2)}) collective-permute-start(bf16[288,576]{1,0:T(8,128)(2,1)S(1)} %collective-permute-done.35.refs_2_), channel_id=1, source_target_pairs={{0,16},{8,24},{16,0},{24,8},{1,17},{9,25},{17,1},{25,9},{2,18},{10... | collective-permute-start | bytes 995336 | tf_op jit(solution)/shard_map/ppermute | solution.py:849
  311.1 16.6 %collective-permute-start.40 = (bf16[288,640]{1,0:T(8,128)(2,1)S(1)}, bf16[288,640]{1,0:T(8,128)(2,1)S(1)}, u32[]{:S(2)}, u32[]{:S(2)}) collective-permute-start(bf16[288,640]{1,0:T(8,128)(2,1)S(1)} %collective-permute-done.39.refs_3_), channel_id=1, source_target_pairs={{0,8},{8,0},{16,24},{24,16},{1,9},{9,1},{17,25},{25,17},{2,10},{10... | collective-permute-start | bytes 1105928 | tf_op jit(solution)/shard_map/ppermute | solution.py:849
  (32 other events, 153.5 us)
Sparse Core Ops, SparseCore 0:
  42.1 62.5 all-gather.2
  106.6 48.4 all-gather.4
  163.1 36.4 reduce-scatter.3
  201.9 37.0 reduce-scatter.5
  241.7 47.7 reduce-scatter.7
where the time goes:
time: 345 us; the launch traced here: 339 us
  Pallas kernels  120 us (35%)
  waiting for transfers between devices  86.4 us (25%)
  starting transfers between devices  56.9 us (16%)
  matrix products  36.5 us (11%)
  local copies, waits for them, and re-layouts  16.4 us (5%)
  between operations  15.3 us (4%)
  other arithmetic  7.95 us (2%)
    pallas_call x20, Pallas kernels, kernel_call(): pl.pallas_call(body, name=name, out_shape=tuple(outs), grid=grid, in_spec...  120 us
    ppermute x34, waiting for transfers between devices, xor_permute(): lax.ppermute(block, axis, [(i, i ^ bits) for i in range(lax.axis_size(axi...  78.4 us
    ppermute x34, starting transfers between devices, xor_permute(): lax.ppermute(block, axis, [(i, i ^ bits) for i in range(lax.axis_size(axi...  38.8 us
    ppermute x4, starting transfers between devices, move(): return lax.ppermute(block, 'blk', pairs)  12.9 us
    dot_general x3, matrix products, bf_dot(): return jnp.dot(operand_a, operand_b, preferred_element_type=F32)  9.88 us
    unnamed x104, local copies, waits for them, and re-layouts  8.98 us
    dot_general x1, matrix products, local(): jnp.einsum('td,gfd->gtf', hidden_rows, qkv_turned, preferred_element_type...  8.42 us
    dot_general x2, matrix products, dot_by(): lax.dot_general(operand_a, operand_b, dims, preferred_element_type=F32)  8.12 us
  transfers between devices with their start and end apart: 46, of which 18 were waited for; matrix products, arithmetic and copies ran while one was open for 14% of the time, Pallas kernels for 32%

commit v1 on v0

--- a/solution.py
+++ b/solution.py
@@ -40,8 +40,12 @@
 
 
 def kernel_call(
-    body, name, outs, args, flops, grid=(), in_specs=None, out_specs=None, scratch=(), vmem=56
+    body, name, outs, args, flops, grid=(), in_specs=None, out_specs=None, scratch=(), far=(), vmem=48
 ):
+    args = [
+        pltpu.with_memory_space_constraint(a, pltpu.HBM) if number in far else a
+        for number, a in enumerate(args)
+    ]
     moved = sum(math.prod(a.shape) * a.dtype.itemsize for a in (*args, *outs))
     return pl.pallas_call(
         body,
@@ -147,36 +151,97 @@
     )[0]
 
 
-def pick_body(first, scalars, own_ref, other_ref, out_ref):
+def latents_body(first, scalars, condition_ref, own_ref, near_ref):
+    wide = condition_ref[...].astype(F32)
+    active = (wide / (1.0 + jnp.exp(-wide))).astype(BF16).astype(F32)
+    segments = lax.broadcasted_iota(jnp.int32, active.shape, 0)
+    number = 0
+    for out in (own_ref, near_ref):
+        rows = []
+        for _ in range(out.shape[0]):
+            chosen = jnp.where(segments == scalars[first + number], active, 0.0)
+            rows.append(jnp.sum(chosen, axis=0, keepdims=True))
+            number += 1
+        out[...] = jnp.concatenate(rows, axis=0).astype(BF16)
+
+
+def latents(scalars, first, condition, own, near):
+    width = condition.shape[1]
+    return kernel_call(
+        lambda *refs: latents_body(first, *refs),
+        "latents",
+        [array((own, width), BF16), array((near, width), BF16)],
+        [scalars, condition],
+        0,
+        in_specs=[SMEM, VMEM],
+    )
+
+
+def pick_body(scalars, own_ref, other_ref, out_ref):
     half = own_ref.shape[2]
-    core = scalars[0]
-    for place in range(out_ref.shape[0]):
-        segment = scalars[first + place]
-
-        def write(low, high):
-            out_ref[place, :, :half] = low[segment]
-            out_ref[place, :, half:] = high[segment]
-
-        pl.when(core == 0)(lambda: write(own_ref, other_ref))
-        pl.when(core == 1)(lambda: write(other_ref, own_ref))
-
-
-def pick(scalars, first, own, other, count):
-    shape = (count, own.shape[1], 2 * own.shape[2])
+
+    def write(low, high):
+        out_ref[:, :, :half] = low[...]
+        out_ref[:, :, half:] = high[...]
+
+    pl.when(scalars[0] == 0)(lambda: write(own_ref, other_ref))
+    pl.when(scalars[0] == 1)(lambda: write(other_ref, own_ref))
+
+
+def pick(scalars, own, other):
     return kernel_call(
-        lambda *refs: pick_body(first, *refs),
+        pick_body,
         "pick",
-        [array(shape, F32)],
+        [array((*own.shape[:2], 2 * own.shape[2]), F32)],
         [scalars, own, other],
         0,
         in_specs=[SMEM, VMEM, VMEM],
     )[0]
 
 
-def norm_body(scalars, own_ref, near_ref, up_ref, mod_ref, hidden_ref, down_in_ref, shares_ref):
+def others_body(first, places, scalars, shares_ref, mod_ref, hidden_ref, down_in_ref):
+    entry, core = pl.program_id(0), pl.program_id(1)
+    half = hidden_ref.shape[0]
+    size = SHORT // 2
+    for block in range(half // size):
+        rows = pl.ds(block * size, size)
+        place = first + entry * places + (core * (half // size) + block) // 2
+        normed, _ = layer_norm(shares_ref[rows].astype(F32))
+        shift, scale, gate = (mod_ref[place, group : group + 1] for group in (0, 1, 5))
+        hidden_ref[rows] = (normed * (1.0 + scale) + shift).astype(BF16)
+        upstream = shares_ref[pl.ds(half + block * size, size)].astype(F32)
+        down_in_ref[rows] = (gate * upstream).astype(BF16)
+
+
+def others(scalars, shares, mod_all, first, packs, count):
+    width = shares.shape[1]
+    shape = ((packs - 1) * count, width)
+
+    def source(r, c, scalars_ref):
+        return (jnp.bitwise_xor(scalars_ref[2 + packs], r + 1) * 2 + c, 0)
+
+    half_rows = pl.BlockSpec((count // 2, width), lambda r, c, _: (2 * r + c, 0))
+    return pl.pallas_call(
+        lambda *refs: others_body(first, count // SHORT, *refs),
+        name="others",
+        out_shape=(array(shape, BF16), array(shape, BF16)),
+        grid_spec=pltpu.PrefetchScalarGridSpec(
+            num_scalar_prefetch=1,
+            grid=(packs - 1, 2),
+            in_specs=[
+                pl.BlockSpec((count, width), source),
+                pl.BlockSpec(mod_all.shape, lambda r, c, _: (0, 0, 0)),
+            ],
+            out_specs=(half_rows, half_rows),
+        ),
+        compiler_params=pltpu.CompilerParams(vmem_limit_bytes=56 << 20),
+        cost_estimate=pl.CostEstimate(flops=0, bytes_accessed=0, transcendentals=0),
+    )(scalars, shares, mod_all)
+
+
+def norm_body(own_ref, near_ref, up_ref, mod_ref, hidden_ref, down_in_ref):
     step = pl.program_id(0)
     places = 3
-    half = shares_ref.shape[1] // 2
     shift, scale = mod_ref[0, 0:1], mod_ref[0, 1:2]
 
     def write(rows):
@@ -187,18 +252,14 @@
     def _():
         write(own_ref[...])
         down_in_ref[...] = (mod_ref[0, 5:6] * up_ref[...].astype(F32)).astype(BF16)
-        start = aligned(scalars[0] * (hidden_ref.shape[1] - half))
-        shares_ref[:, :half] = down_in_ref[:, pl.ds(start, half)]
-        shares_ref[:, half:] = hidden_ref[:, pl.ds(start, half)]
 
     pl.when(step >= places)(lambda: write(near_ref[...]))
 
 
-def norm(scalars, own, near, upstream, mod_places):
+def norm(own, near, upstream, mod_places):
     count, width = own.shape
     places = count // SHORT
     total = count + near.shape[0]
-    share = 2 * half_width(width)
 
     def own_place(i):
         return (jnp.minimum(i, places - 1), 0)
@@ -206,12 +267,11 @@
     return kernel_call(
         norm_body,
         "norm",
-        [array((total, width), BF16), array((count, width), BF16), array((count, share), BF16)],
-        [scalars, own, near, upstream, mod_places],
+        [array((total, width), BF16), array((count, width), BF16)],
+        [own, near, upstream, mod_places],
         0,
         grid=(total // SHORT,),
         in_specs=[
-            SMEM,
             pl.BlockSpec((SHORT, width), own_place),
             pl.BlockSpec((SHORT, width), lambda i: (jnp.maximum(i - places, 0), 0)),
             pl.BlockSpec((SHORT, width), own_place),
@@ -220,7 +280,6 @@
         out_specs=(
             pl.BlockSpec((SHORT, width), lambda i: (i, 0)),
             pl.BlockSpec((SHORT, width), own_place),
-            pl.BlockSpec((SHORT, share), own_place),
         ),
     )
 
@@ -273,6 +332,7 @@
         [array((count, own_width), BF16), array((count, width), F32)],
         [scalars, rows, weight],
         2 * count * own_width * (width + 2 * LONG),
+        far=(2,),
         in_specs=[SMEM, VMEM, VMEM],
         scratch=[
             pltpu.VMEM((3 * count, own_width), BF16),
@@ -350,6 +410,7 @@
         + [array((count, share), BF16)] * packs,
         [scalars, rows, grad, near_grad, weight],
         6 * count * own_width * width + 10 * own_width * LONG * LONG,
+        far=(4,),
         in_specs=[SMEM] + [VMEM] * 4,
         scratch=[
             pltpu.VMEM((4, 3 * count, own_width), BF16),
@@ -416,6 +477,7 @@
         outs,
         [scalars, kept, term, other, bias, mod_places, weight, hidden_bias],
         2 * count * width * hidden,
+        far=(6,),
         grid=(hidden // size,),
         in_specs=[
             SMEM,
@@ -467,6 +529,7 @@
         outs,
         [scalars, down_in, down, slope, weight],
         4 * count * width * hidden,
+        far=(2, 4),
         grid=(hidden // size,),
         in_specs=[
             SMEM,
@@ -500,7 +563,7 @@
     sums_ref[0, 2:3] = jnp.sum(hidden_grad * normed, axis=0, keepdims=True)
 
 
-def by_place(body, name, outs, args, flops):
+def by_place(body, name, outs, args, flops, far=()):
     places = args[0].shape[0] // SHORT
 
     def spec(a):
@@ -516,6 +579,7 @@
         outs,
         args,
         flops,
+        far=far,
         grid=(places,),
         in_specs=[spec(a) for a in args],
         out_specs=tuple(spec(a) for a in outs),
@@ -537,6 +601,7 @@
         ],
         [term, other, branch, kept, upstream, mod_places, weight],
         2 * count * width * weight.shape[0],
+        far=(6,),
     )
 
 
@@ -605,17 +670,19 @@
             rows_all[rows, :half] = shares[0][low, offset : offset + half]
             rows_all[rows, half:] = shares[0][high, offset + 2 * half - width : offset + half]
         elif entry == 0:
-            rows_all[rows] = shares[0][...]
+            rows_all[rows] = shares[0][:count]
         else:
-            skip = width - half
-            place = pl.ds(aligned(scalars[0] * skip), half)
-            rows_all[rows, place] = shares[1][(entry - 1) * count : entry * count]
-            place = pl.ds(aligned((1 - scalars[0]) * skip), half)
-            rows_all[rows, place] = shares[2][(entry - 1) * count : entry * count]
+            rows_all[rows] = shares[1][(entry - 1) * count : entry * count]
     if len(outs) == 1:
         outs[0][...] = dot_by(COLUMNS_BY_COLUMNS, rows_all[...], columns_all[...]).astype(BF16)
         return
-    total[...] = dot_by(COLUMNS_BY_COLUMNS, rows_all[...], columns_all[...])
+    total[:, :wide] = dot_by(COLUMNS_BY_COLUMNS, rows_all[...], columns_all[...])
+    if total.shape[1] > wide:
+        others, outs = outs[:packs], outs[packs:]
+        other = others[0][...].astype(F32)
+        for entry in range(1, packs):
+            other = other + others[entry][...].astype(F32)
+        total[:, wide:] = other.T
     cut_by_blk(scalars, total, outs)
 
 
@@ -633,71 +700,75 @@
     return [array((size, wide), F32)] + [array((size, wide), BF16)] * (blocks - 1)
 
 
-def weight_grad(scalars, width, offset, shares, columns, blocks=1):
+def weight_grad(scalars, width, offset, shares, columns, others=(), blocks=1):
     packs = len(columns)
     count, wide = columns[0].shape
+    total = wide + (others[0].shape[0] if others else 0)
     outs = [array((width, wide), BF16)]
     if blocks > 1:
-        outs = cut_shapes(width, wide, blocks)
+        outs = cut_shapes(width, total, blocks)
     return kernel_call(
         lambda *refs: weight_grad_body(packs, offset, len(shares), *refs),
         "weight_grad",
         outs,
-        [scalars, *shares, *columns],
+        [scalars, *shares, *columns, *others],
         2 * packs * count * width * wide,
-        in_specs=[SMEM] + [VMEM] * (packs + len(shares)),
+        in_specs=[SMEM] + [VMEM] * (packs + len(shares) + len(others)),
         scratch=[
             pltpu.VMEM((packs * count, width), BF16),
             pltpu.VMEM((packs * count, wide), BF16),
-            pltpu.VMEM((width, wide), F32),
+            pltpu.VMEM((width, total), F32),
         ],
     )
 
 
-def own_weight_grad_body(rows_ref, columns_ref, out_ref):
-    out_ref[...] = dot_by(COLUMNS_BY_COLUMNS, rows_ref[...], columns_ref[...]).astype(BF16)
-
-
-def own_weight_grad(rows, columns):
+def own_weight_grad_body(packs, scalars, rows_ref, columns_ref, *refs):
+    pieces, total = refs[:-1], refs[-1]
+    total[...] = dot_by(COLUMNS_BY_COLUMNS, rows_ref[...], columns_ref[...])
+    size = total.shape[0] // packs
+    for entry, piece in enumerate(pieces):
+        start = jnp.bitwise_xor(scalars[2 + packs], entry) * size
+        piece[...] = total[pl.ds(aligned(start, 8), size)].astype(BF16)
+
+
+def own_weight_grad(scalars, rows, columns, packs):
     shape = (rows.shape[1], columns.shape[1])
     return kernel_call(
-        own_weight_grad_body,
+        lambda *refs: own_weight_grad_body(packs, *refs),
         "own_weight_grad",
-        [array(shape, BF16)],
-        [rows, columns],
+        [array((shape[0] // packs, shape[1]), BF16)] * packs,
+        [scalars, rows, columns],
         2 * rows.shape[0] * math.prod(shape),
-    )[0]
+        in_specs=[SMEM, VMEM, VMEM],
+        scratch=[pltpu.VMEM(shape, F32)],
+    )
 
 
 def join_body(kind, starts, packs, scalars, *refs):
-    entries, outs, held = refs[:-2], refs[-2:-1], refs[-1]
-    size = entries[0].shape[0] // (packs if len(entries) == 1 else 1)
-    if len(entries) > 1:
+    outs, held = refs[1:-1], refs[-1]
+    size = refs[0].shape[0] // packs
+    stacked = kind == "hidden"
+    if not stacked:
+        entries, outs = refs[:packs], refs[packs:-1]
         for entry in range(packs):
             held[entry] = entries[entry][...]
-    if kind == "output":
-        total = held[scalars[2 + packs]].astype(F32)
-        for number in range(1, packs):
-            total = total + held[jnp.bitwise_xor(scalars[2 + packs], number)].astype(F32)
-        outs[0][...] = total
-        return
     for number in range(packs):
-        if len(entries) > 1:
+        if stacked:
+            piece = refs[0][number * size : (number + 1) * size].astype(F32)
+        else:
             piece = held[jnp.bitwise_xor(scalars[2 + packs], number)].astype(F32)
-        else:
-            piece = entries[0][number * size : (number + 1) * size].astype(F32)
         if kind == "qkv":
-            share = piece.shape[1] // 3
+            share = piece.shape[1] // 4
+            columns = pl.ds(number * share, share)
             for part in range(3):
-                columns = pl.ds(number * share, share)
                 outs[0][part, :, columns] = piece[:, part * share : (part + 1) * share]
+            outs[1][:, columns] = piece[:, 3 * share :]
         else:
             end = [*starts[1:], outs[0].shape[1]][number]
             outs[0][:, starts[number] : end] = piece[:, : end - starts[number]]
 
 
 def join(kind, scalars, entries, packs, shapes, starts=()):
-    held = (len(entries), *entries[0].shape) if len(entries) > 1 else (16, LANES)
     return kernel_call(
         lambda *refs: join_body(kind, starts, packs, *refs),
         "join_" + kind,
@@ -705,11 +776,11 @@
         [scalars, *entries],
         0,
         in_specs=[SMEM] + [VMEM] * len(entries),
-        scratch=[pltpu.VMEM(held, BF16)],
-    )
-
-
-def collect_body(first, scalars, input_ref, middle_ref, two_ref, active_ref, *refs):
+        scratch=[pltpu.VMEM((packs, *entries[0].shape), BF16)],
+    )
+
+
+def collect_body(scalars, input_ref, middle_ref, two_ref, active_ref, *refs):
     qkv_ref, output_ref, hidden_ref, down_ref, out_ref, held = refs
     places, _, width = middle_ref.shape
     half = width // 2
@@ -737,7 +808,7 @@
     pl.when(scalars[0] == 0)(lambda: put_sums(0))
     pl.when(scalars[0] == 1)(lambda: put_sums(half))
     for place in range(places):
-        active = active_ref[pl.ds(scalars[first + place], 1)]
+        active = active_ref[place : place + 1].astype(F32)
         put(active[:, :half])
         put(active[:, half:])
     put_twice(qkv_ref[0:1])
@@ -751,13 +822,13 @@
     out_ref[...] = held[...].astype(BF16)
 
 
-def collect(first, scalars, *args):
+def collect(scalars, *args):
     places, _, width = args[0].shape
     hidden = args[6].shape[1]
     used = places * 8 + 2 * (2 + 2 * hidden // width + 4)
     size = -(-used // 16) * 16
     return kernel_call(
-        lambda *refs: collect_body(first, *refs),
+        collect_body,
         "collect",
         [array((size, width // 2), BF16)],
         [scalars, *args],
@@ -777,10 +848,8 @@
         held[entry] = entries[entry][...].reshape(blocks, size, half)
     for number in range(packs):
         for block in range(blocks):
-            source = held[
-                jnp.bitwise_xor(pack, number), jnp.bitwise_xor(scalars[1], block)
-            ]
-            rows_all[number * blocks + block] = source.astype(F32)
+            piece = held[jnp.bitwise_xor(pack, number), jnp.bitwise_xor(scalars[1], block)]
+            rows_all[number * blocks + block] = piece.astype(F32)
     cut = 6 * places
     devices = packs * blocks
 
@@ -821,9 +890,9 @@
 
 
 def spread(scalars, segments, entries, packs, blocks, places, seg_count, width):
+    devices = packs * blocks
     size = entries[0].shape[0] // blocks
     half = entries[0].shape[1]
-    devices = packs * blocks
     return kernel_call(
         lambda *refs: spread_body(packs, blocks, places, size, *refs),
         "spread",
@@ -868,6 +937,10 @@
     return [held[entry] for entry in range(lax.axis_size(axis))]
 
 
+def gather_each(block, axis):
+    return [block] + [xor_permute(block, axis, r) for r in range(1, lax.axis_size(axis))]
+
+
 def in_order(entries, axis):
     order = jnp.arange(len(entries), dtype=jnp.int32) ^ lax.axis_index(axis)
     return jnp.take(jnp.stack(entries), order, axis=0)
@@ -903,12 +976,19 @@
     return jax.tree.unflatten(tree, held[: len(flat)])
 
 
-def sum_blk(pieces):
+def send_blk(pieces):
     count = len(pieces)
-    total = pieces[0]
+    found = [pieces[0]]
     for step in range(1, count):
         pairs = [(i, (i + step) % count) for i in range(count)]
-        total = total + lax.ppermute(pieces[step], "blk", pairs).astype(F32)
+        found.append(lax.ppermute(pieces[step], "blk", pairs))
+    return found
+
+
+def add_blk(found):
+    total = found[0]
+    for piece in found[1:]:
+        total = total + piece.astype(F32)
     return total.astype(BF16)
 
 
@@ -942,7 +1022,15 @@
     core = lax.axis_index("head")
     pack = lax.axis_index("pack")
 
-    local_index = kept_index[0] - blk * (2 * count)
+    modulation_turned = jnp.transpose(modulation_weight, (1, 2, 0))
+    starts, window = windows(hidden, packs)
+    place = jnp.stack([core, blk, pack, jnp.int32(blocks)]).astype(jnp.int32)
+    scalars = plan(longs, packs, starts, place, segment_ids[0])
+    base = 3 + packs
+    own_active, near_active = latents(
+        scalars, base + 3 + 2 * places, condition[0], places, places if longs == 1 else 2 * places
+    )
+    local_index, own_active = hold((kept_index[0] - blk * (2 * count), own_active))
     full_rows = tokens_full[0]
     cot_rows = cotangent[0]
     picker = (
@@ -951,10 +1039,6 @@
     kept_rows = bf_dot(picker, full_rows).astype(BF16)
     upstream = bf_dot(picker, cot_rows).astype(BF16)
 
-    starts, window = windows(hidden, packs)
-    place = jnp.stack([core, blk, pack, jnp.int32(blocks)]).astype(jnp.int32)
-    scalars = plan(longs, packs, starts, place, segment_ids[0])
-    base = 3 + packs
     reaches_low = scalars[-1] == 1
 
     def beside(block):
@@ -964,30 +1048,34 @@
         return jnp.concatenate([low, high], axis=0)
 
     half = count // 2
-    near_half = beside(lax.dynamic_slice_in_dim(kept_rows, core * half, half, 0))
+    kept_half = lax.dynamic_slice_in_dim(kept_rows, core * half, half, 0)
+    near_half = beside(kept_half)
+    token_shares = gather_shares(
+        jnp.concatenate(
+            [kept_half, lax.dynamic_slice_in_dim(upstream, core * half, half, 0)], axis=0
+        )
+    )
     other_half = swap(near_half)
     first = jnp.where(core == 0, near_half, other_half).reshape(-1, half, width)
     second = jnp.where(core == 0, other_half, near_half).reshape(-1, half, width)
     near_rows = jnp.concatenate([first, second], axis=1).reshape(-1, width)
 
-    cond_rows = condition[0].astype(F32)
-    active = jax.nn.silu(cond_rows).astype(BF16)
+    near_count = near_rows.shape[0] // SHORT
+    other_active = list(trade([own_active] * packs, "pack", range(1, packs)).values())
     mod_own = (
-        jnp.einsum("sd,dgf->sgf", active, modulation_weight, preferred_element_type=F32)
+        jnp.einsum(
+            "sd,gfd->sgf",
+            jnp.concatenate([own_active, near_active, *other_active], axis=0),
+            modulation_turned,
+            preferred_element_type=F32,
+        )
         + modulation_bias.astype(F32)[None]
     )
-    mod_near = pick(
-        scalars,
-        base + 3 + 2 * places,
-        mod_own,
-        swap(mod_own),
-        places + near_rows.shape[0] // SHORT,
-    )
-    mod_places = mod_near[:places]
+    mod_all = pick(scalars, mod_own, swap(mod_own))
+    mod_places = mod_all[:places]
     wide_bias = query_value_bias.astype(F32)
     qkv_bias = jnp.stack([wide_bias[0], jnp.zeros_like(wide_bias[0]), wide_bias[1]])[:, None]
-    hidden_rows, down_in, share = norm(scalars, kept_rows, near_rows, upstream, mod_near)
-    early_shares = gather_shares(share)
+    hidden_rows, down_in = norm(kept_rows, near_rows, upstream, mod_all)
     qkv_turned = jnp.transpose(qkv_weight, (1, 2, 0))
     projected = jnp.einsum("td,gfd->gtf", hidden_rows, qkv_turned, preferred_element_type=F32)
     qkv_rows = (projected + qkv_bias).astype(BF16)
@@ -1013,8 +1101,8 @@
             found.update(part)
         return [found[r] for r in range(packs)]
 
+    hidden_two_shares = gather_shares(hidden_two_share)
     gelu_first = trade(gelu_pieces, "pack", one_step)
-    hidden_two_shares = gather_shares(hidden_two_share)
     back_term, hidden_sums, pre_pieces = feed_back(
         scalars, down_in, down_weight, slope, hidden_weight, packs
     )
@@ -1025,40 +1113,44 @@
     middle_grad, branch_grad, attended_grad, middle_sums, output_sums = middle_back(
         back_term, swap(back_term), branch_one, kept_rows, upstream, mod_places, output_weight
     )
-    attended_grad, gelu_last, early_shares, pre_pieces, gelu = hold(
-        (attended_grad, gelu_last, early_shares, pre_pieces, gelu)
+    attended_grad, token_shares, pre_pieces, gelu, branch_grad = hold(
+        (attended_grad, token_shares, pre_pieces, gelu, branch_grad)
     )
     near_grad = beside(attended_grad)
+    rows = width // blocks
 
     pre_first = trade(pre_pieces, "pack", range(1, packs))
     gelu_all = by_entry(gelu_pieces, gelu_first, gelu_last)
-    down_raw = weight_grad(scalars, width, 0, [early_shares], gelu_all)[0]
-    two_term = bf_dot(gelu, down_weight).astype(BF16)
-    output_raw = own_weight_grad(branch_grad, attended)
-    near_grad, down_raw, output_raw, two_term, pre_first = hold(
-        (near_grad, down_raw, output_raw, two_term, pre_first)
-    )
-    half = half_width(width)
-    rows = width // blocks
+    hidden_other_packs, down_other_packs = others(
+        scalars, token_shares, mod_all, places + near_count, packs, count
+    )
+    down_raw = weight_grad(scalars, width, 0, [down_in, down_other_packs], gelu_all)[0]
+    output_pieces = own_weight_grad(scalars, attended, branch_grad, packs)
+    near_grad, down_raw, output_pieces, pre_first = hold(
+        (near_grad, down_raw, output_pieces, pre_first)
+    )
     down_term = lax.psum_scatter(down_raw, "blk", scatter_dimension=0, tiled=True)
-    output_term = lax.psum_scatter(output_raw, "blk", scatter_dimension=0, tiled=True)
+    output_first = trade(output_pieces, "pack", one_step)
     hidden_term, qkv_sums, qkv_pieces = attend_back(
         base, scalars, qkv_rows, attended_grad, near_grad, qkv_turned, packs
     )
-    hidden_term, qkv_pieces, two_term = hold((hidden_term, qkv_pieces, two_term))
-    qkv_all = by_entry(qkv_pieces, trade(qkv_pieces, "pack", range(1, packs)))
-
-    def put_rows(base, rows):
-        spread = dot_by(COLUMNS_BY_COLUMNS, picker, rows)
-        kept = jnp.max(picker, axis=0)[:, None] > 0
-        return jnp.where(kept, spread.astype(BF16), base)[None]
-
-    input_grad, input_sums = input_back(
-        hidden_term, swap(hidden_term), middle_grad, kept_rows, mod_places
-    )
-    tokens_grad = put_rows(cot_rows, input_grad)
+    hidden_term, qkv_pieces, output_first, output_pieces, gelu, pre_first = hold(
+        (hidden_term, qkv_pieces, output_first, output_pieces, gelu, pre_first)
+    )
+    qkv_first = trade(qkv_pieces, "pack", one_step)
+    qkv_last = trade(qkv_pieces, "pack", further)
+    output_last = trade(output_pieces, "pack", further)
+
     pre_all = by_entry(pre_pieces, pre_first)
     hidden_raw = weight_grad(scalars, width, 0, [hidden_two_shares], pre_all)[0]
+    hidden_reduced = lax.psum_scatter(hidden_raw, "blk", scatter_dimension=0, tiled=True)
+    hidden_other, qkv_first, output_last, hidden_raw, gelu = hold(
+        (swap(hidden_term), qkv_first, output_last, hidden_raw, gelu)
+    )
+    input_grad, input_sums = input_back(
+        hidden_term, hidden_other, middle_grad, kept_rows, mod_places
+    )
+    two_term = bf_dot(gelu, down_weight).astype(BF16)
     result_rows, two_sums, down_sums = result(
         two_term,
         swap(two_term),
@@ -1069,57 +1161,77 @@
         mod_places,
     )
     sent = collect(
-        base + 3 + 2 * places,
         scalars,
         input_sums,
         middle_sums,
         two_sums,
-        active.astype(F32),
+        own_active,
         qkv_sums,
         output_sums,
         hidden_sums,
         down_sums,
     )
-    qkv_all, tokens_grad, hidden_raw, result_rows, sent = hold(
-        (qkv_all, tokens_grad, hidden_raw, result_rows, sent)
-    )
-    hidden_term = lax.psum_scatter(hidden_raw, "blk", scatter_dimension=0, tiled=True)
-    by_blk = gather_xor(sent, "blk")
-    qkv_terms = weight_grad(scalars, width, half, [early_shares], qkv_all, blocks)
-    qkv_terms, result_rows, by_blk = hold((qkv_terms, result_rows, by_blk))
-    entries = gather_xor(jnp.concatenate(by_blk, axis=0), "pack")
+    qkv_last, sent = hold((qkv_last, sent))
+    by_blk = gather_each(sent, "blk")
+    qkv_terms = weight_grad(
+        scalars,
+        width,
+        0,
+        [hidden_rows, hidden_other_packs],
+        by_entry(qkv_pieces, qkv_first, qkv_last),
+        by_entry(output_pieces, output_first, output_last),
+        blocks,
+    )
+    qkv_terms, by_blk, result_rows, input_grad, down_term = hold(
+        (qkv_terms, by_blk, result_rows, input_grad, down_term)
+    )
+
+    def put_rows(base, rows):
+        spread = dot_by(COLUMNS_BY_COLUMNS, picker, rows)
+        kept = jnp.max(picker, axis=0)[:, None] > 0
+        return jnp.where(kept, spread.astype(BF16), base)[None]
+
+    qkv_found = send_blk(qkv_terms)
+    entries = gather_each(jnp.concatenate(by_blk, axis=0), "pack")
+    down_entries = gather_each(down_term, "pack")
     block_output = put_rows(full_rows, result_rows)
-    down_entries = gather_xor(down_term, "pack")
-    qkv_share, entries, block_output, down_entries = hold(
-        (sum_blk(qkv_terms), entries, block_output, down_entries)
-    )
-    qkv_entries = gather_xor(qkv_share, "pack")
+    tokens_grad = put_rows(cot_rows, input_grad)
+    qkv_found, entries, block_output, tokens_grad, down_entries = hold(
+        (qkv_found, entries, block_output, tokens_grad, down_entries)
+    )
+    qkv_entries = gather_each(add_blk(qkv_found), "pack")
+    hidden_gathered = lax.all_gather(hidden_reduced, "pack", axis=0, tiled=True)
     modulation_weight_grad, modulation_bias_grad, biases, mod_grad = spread(
         scalars, segment_ids[0], entries, packs, blocks, places, seg_count, width
     )
-    down_weight_grad = join("down", scalars, down_entries, packs, [(rows, hidden)], starts)[0].T
-    qkv_entries, output_term, hidden_term, modulation_weight_grad = hold(
-        (qkv_entries, output_term, hidden_term, modulation_weight_grad)
-    )
+    qkv_weight_grad, output_weight_grad = join(
+        "qkv", scalars, qkv_entries, packs, [(3, rows, own_width), (rows, own_width)]
+    )
+    down_weight_grad = join(
+        "down",
+        scalars,
+        down_entries,
+        packs,
+        [(rows, hidden)],
+        starts,
+    )[0].T
     hidden_weight_grad = join(
-        "hidden", scalars, gather_xor(hidden_term, "pack", True), packs, [(rows, hidden)], starts
+        "hidden", scalars, [hidden_gathered], packs, [(rows, hidden)], starts
     )[0]
-    output_weight_grad = join(
-        "output", scalars, gather_xor(output_term, "pack"), packs, [(rows, own_width)]
-    )[0].T
-    qkv_weight_grad = join("qkv", scalars, qkv_entries, packs, [(3, rows, own_width)])[0]
+    output_weight_grad = output_weight_grad.T
     qkv_weight_grad = jnp.swapaxes(qkv_weight_grad, 0, 1)
     modulation_weight_grad = jnp.swapaxes(modulation_weight_grad, 0, 1)
     mod_high = mod_grad.astype(BF16)
     mod_low = (mod_grad - mod_high.astype(F32)).astype(BF16)
     cond_terms = jnp.einsum(
-        "sgf,dgf->sd",
+        "sgf,gfd->sd",
         jnp.concatenate([mod_high, mod_low], axis=0),
-        modulation_weight,
+        modulation_turned,
         preferred_element_type=F32,
     )
     cond_term = cond_terms[:seg_count] + cond_terms[seg_count:]
     cond_total = cond_term + swap(cond_term)
+    cond_rows = condition[0].astype(F32)
     squashed = jax.nn.sigmoid(cond_rows)
     condition_grad = (cond_total * squashed * (1.0 + cond_rows * (1.0 - squashed)))[None]
 

time: 345 us -> 304 us (0.88)
  the two profiles are of different devices: /device:TPU:0 before, /device:TPU:24 now
where the time goes in v1:
time: 304 us; the launch traced here: 298 us
  Pallas kernels  109 us (36%)
  waiting for transfers between devices  56.1 us (18%)
  starting transfers between devices  50.6 us (17%)
  matrix products  30.6 us (10%)
  local copies, waits for them, and re-layouts  30.4 us (10%)
  between operations  15.6 us (5%)
  other arithmetic  6.27 us (2%)
    pallas_call x20, Pallas kernels, kernel_call(): pl.pallas_call(body, name=name, out_shape=tuple(outs), grid=grid, in_spec...  100 us
    ppermute x34, waiting for transfers between devices, xor_permute(): lax.ppermute(block, axis, [(i, i ^ bits) for i in range(lax.axis_size(axi...  41.4 us
    ppermute x34, starting transfers between devices, xor_permute(): lax.ppermute(block, axis, [(i, i ^ bits) for i in range(lax.axis_size(axi...  34.3 us
    unnamed x152, local copies, waits for them, and re-layouts  27.3 us
    ppermute x3, waiting for transfers between devices, send_blk(): found.append(lax.ppermute(pieces[step], 'blk', pairs))  14.5 us
    ppermute x4, starting transfers between devices, move(): return lax.ppermute(block, 'blk', pairs)  12.8 us
    dot_general x3, matrix products, bf_dot(): return jnp.dot(operand_a, operand_b, preferred_element_type=F32)  9.1 us
    pallas_call x1, Pallas kernels, others(): pl.pallas_call(lambda *refs: others_body(first, count // SHORT, *refs), n...  8.06 us
  transfers between devices with their start and end apart: 46, of which 15 were waited for; matrix products, arithmetic and copies ran while one was open for 12% of the time, Pallas kernels for 35%

profile of v1, /device:TPU:24, one launch (start us, length us, event | category | flops | bytes accessed | tf_op | source)
XLA Modules:
  0.0 298.0 jit_solution(663130173400055911)
XLA Ops:
  8.0 1.3 plan.1.refs_0_.scalars
  11.6 2.6 convolution_convert_fusion.4.own_ref.kept_ref
  16.4 1.3 collective-permute-start
  17.7 4.6 %collective-permute-start.1 = (bf16[192,1152]{1,0:T(8,128)(2,1)S(1)}, bf16[192,1152]{1,0:T(8,128)(2,1)S(1)}, u32[]{:S(2)}, u32[]{:S(2)}) collective-permute-start(bf16[192,1152]{1,0:T(8,128)(2,1)S(1)} %constant_dynamic-slice_fusion.1), channel_id=1, source_target_pairs={{2,0},{4,2},{6,4},{3,1},{5,3},{7,5},{10,8},{12,10},{14,12},{11,9},... | collective-permute-start | bytes 1327112 | tf_op jit(solution)/shard_map/ppermute | solution.py:928
  22.3 1.6 collective-permute-start.3
  23.8 1.5 collective-permute-start.4
  27.5 2.5 collective-permute-done.5
  30.2 5.6 %fusion.2 = f32[15,6,576]{2,0,1:T(8,128)S(1)} fusion(bf16[1152,6,576]{0,2,1:T(8,128)(2,1)} %param.28, bf16[15,1152]{1,0:T(8,128)(2,1)S(1)} %concatenate.16), kind=kOutput, calls=%fused_computation.2 | convolution fusion | flops 119439360 | bytes 8204544 | tf_op jit(solution)/shard_map/sd,gfd->sgf/dot_general | solution.py:1066
  36.7 1.5 collective-permute-done.6.other_ref
  39.3 2.1 norm.1
  42.6 4.4 %fusion.8.refs_1_ = bf16[3,768,576]{2,1,0:T(8,128)(2,1)S(1)} fusion(f32[3,576]{1,0:T(4,128)S(1)} %pad_maximum_fusion.2, bf16[768,1152]{1,0:T(8,128)(2,1)S(1)} %get-tuple-element.142.refs_1_, bf16[1152,3,576]{0,2,1:T(8,128)(2,1)S(1)} %copy-done.61), kind=kOutput, calls=%fused_computation.11 | convolution fusion | flops 3060301824 | bytes 8411904 | tf_op jit(solution)/shard_map/td,gfd->gtf/dot_general | solution.py:1080
  47.0 11.2 %attend.1 = (bf16[384,576]{1,0:T(8,128)(2,1)S(1)}, f32[384,1152]{1,0:T(8,128)S(1)}) custom-call(s32[23]{0:T(128)S(1)} %plan.1.refs_0_.scalars, bf16[3,768,576]{2,1,0:T(8,128)(2,1)S(1)} %fusion.8.refs_1_, bf16[576,1152]{1,0:T(8,128)(2,1)} %rest_0_.3), custom_call_target="tpu_custom_call" | custom-call | flops 962592 | bytes 6193 | tf_op jit(solution)/shard_map/attend/pallas_call | solution.py:50
  59.2 3.5 %collective-permute-done.7.other_ref = f32[384,1152]{1,0:T(8,128)S(1)} collective-permute-done((f32[384,1152]{1,0:T(8,128)S(1)}, f32[384,1152]{1,0:T(8,128)S(1)}, u32[]{:S(2)}, u32[]{:S(2)}) %collective-permute-start.7) | collective-permute-done | bytes 1769504 | tf_op jit(solution)/shard_map/ppermute | solution.py:918
  62.7 1.2 copy-done.62
  63.9 10.8 %feed_up.1 = (f32[384,1152]{1,0:T(8,128)S(1)}, bf16[384,1152]{1,0:T(8,128)(2,1)}, bf16[384,640]{1,0:T(8,128)(2,1)}, f32[384,2304]{1,0:T(8,128)}, bf16[384,2304]{...) custom-call(s32[23]{0:T(128)S(1)} %plan.1.refs_0_.scalars, ...), custom_call_target="tpu_custom_call" | custom-call | flops 2038431 | bytes 20249 | tf_op jit(solution)/shard_map/feed_up/pallas_call | solution.py:50
  74.7 1.2 copy-done.1
  77.7 1.4 collective-permute-start.9
  79.1 9.3 %feed_back.1 = (f32[384,1152]{1,0:T(8,128)S(1)}, f32[1,2304]{1,0:T(1,128)S(1)}, bf16[384,640]{1,0:T(8,128)(2,1)S(1)}, bf16[384,640]{1,0:T(8,128)(2,1)S(1)}, bf16...) custom-call(s32[23]{0:T(128)S(1)} %plan.1.refs_0_.scalars, ...), custom_call_target="tpu_custom_call" | custom-call | flops 4076863 | bytes 18785 | tf_op jit(solution)/shard_map/feed_back/pallas_call | solution.py:50
  90.6 4.7 %collective-permute-done.8.refs_4_ = bf16[384,640]{1,0:T(8,128)(2,1)S(1)} collective-permute-done((bf16[384,640]{1,0:T(8,128)(2,1)}, bf16[384,640]{1,0:T(8,128)(2,1)S(1)}, u32[]{:S(2)}, u32[]{:S(2)}) %collective-permute-start.8) | collective-permute-done | bytes 491552 | tf_op jit(solution)/shard_map/ppermute | solution.py:918
  96.8 2.4 collective-permute-start.13
  99.2 1.3 collective-permute-done.10.other_ref
  100.5 1.2 copy-done.63
  101.7 6.0 %middle_back.1 = (f32[384,1152]{1,0:T(8,128)S(1)}, bf16[384,1152]{1,0:T(8,128)(2,1)S(1)}, bf16[384,576]{1,0:T(8,128)(2,1)S(1)}, f32[3,3,1152]{2,1,0:T(4,128)S(1)}, f32[3,1,1152]{2,1,0:T(1,128)S(1)}) custom-call(f32[384,1152]{1,0:T(8,128)} %copy-done.5, f32[384,1152]{1,0:T(8,128)} %copy-done.63, f32[384,1152]{1,0:T(8,128)} %copy-done.1, ...), custom_call_target="tpu_custom_call" | custom-call | flops 509607 | bytes 11639 | tf_op jit(solution)/shard_map/middle_back/pallas_call | solution.py:50
  111.3 1.3 collective-permute-start.11
  112.6 5.7 %collective-permute-start.12 = (bf16[384,576]{1,0:T(8,128)(2,1)}, bf16[384,576]{1,0:T(8,128)(2,1)}, u32[]{:S(2)}, u32[]{:S(2)}) collective-permute-start(bf16[384,576]{1,0:T(8,128)(2,1)} %copy-done.15), channel_id=1, source_target_pairs={{2,0},{4,2},{6,4},{3,1},{5,3},{7,5},{10,8},{12,10},{14,12},{11,9},... | collective-permute-start | bytes 1327112 | tf_op jit(solution)/shard_map/ppermute | solution.py:928
  118.7 2.6 collective-permute-start.15
  123.0 2.5 own_weight_grad.1
  126.3 8.1 %others.1 = (bf16[1152,1152]{1,0:T(8,128)(2,1)}, bf16[1152,1152]{1,0:T(8,128)(2,1)}) custom-call(s32[23]{0:T(128)} %copy-done.34, bf16[3072,1152]{1,0:T(8,128)(2,1)} %all-gather.4.cloned.1.call-done.refs_1_, f32[15,6,1152]{2,1,0:T(8,128)} %copy-done.2), custom_call_target="tpu_custom_call" | custom-call | tf_op jit(solution)/shard_map/others/pallas_call | solution.py:224
  134.4 6.0 %weight_grad.3 = bf16[1152,640]{1,0:T(8,128)(2,1)} custom-call(s32[23]{0:T(128)S(1)} %copy-done.35, bf16[384,1152]{1,0:T(8,128)(2,1)S(1)} %get-tuple-element.143.down_in_ref.refs_1_, bf16[1152,1152]{1,0:T(8,128)(2,1)} %get-tuple-element.167.refs_2_, bf16[384,640]{1,0:T(8,128)(2,1)S(1)} %copy-done.18, bf16[384,640]{1,0:T(8,128)(2,1)S(1)} %copy-done.20, ...), custom_call_target="tpu_custom_call" | custom-call | flops 2264924 | bytes 6979 | tf_op jit(solution)/shard_map/weight_grad/pallas_call | solution.py:50
  141.5 1.7 collective-permute-done.16.refs_5_
  144.3 2.0 collective-permute-start.18
  147.3 17.0 %attend_back.1 = (bf16[384,1152]{1,0:T(8,128)(2,1)S(1)}, f32[2,576]{1,0:T(2,128)S(1)}, bf16[384,432]{1,0:T(8,128)(2,1)S(1)}, bf16[384,432]{1,0:T(8,128)(2,1)}, b...) custom-call(s32[23]{0:T(128)S(1)} %copy-done.35, bf16[3,768,576]{2,1,0:T(8,128)(2,1)} %copy-done, ...), custom_call_target="tpu_custom_call" | custom-call | flops 3038773 | bytes 9736 | tf_op jit(solution)/shard_map/attend_back/pallas_call | solution.py:50
  167.9 3.5 %collective-permute-start.22 = (bf16[144,1152]{1,0:T(8,128)(2,1)}, bf16[144,1152]{1,0:T(8,128)(2,1)}, u32[]{:S(2)}, u32[]{:S(2)}) collective-permute-start(bf16[144,1152]{1,0:T(8,128)(2,1)} %get-tuple-element.199), channel_id=1, source_target_pairs={{0,24},{8,16},{16,8},{24,0},{1,25},{9,17},{17,9},{25,1},{2,26},{10... | collective-permute-start | bytes 995336 | tf_op jit(solution)/shard_map/ppermute | solution.py:918
  172.4 6.7 %weight_grad.4 = bf16[1152,640]{1,0:T(8,128)(2,1)} custom-call(s32[23]{0:T(128)S(1)} %copy-done.35, bf16[3072,640]{1,0:T(8,128)(2,1)} %all-gather.6.cloned.1.call-done.refs_1_, bf16[384,640]{1,0:T(8,128)(2,1)S(1)} %copy-done.12, bf16[384,640]{1,0:T(8,128)(2,1)} %collective-permute-done.14.refs_3_, bf16[384,640]{1,0:T(8,128)(2,1)} %collective-permute-done.15.refs_4_, ...), custom_call_target="tpu_custom_call" | custom-call | flops 2264924 | bytes 7372 | tf_op jit(solution)/shard_map/weight_grad/pallas_call | solution.py:50
  180.0 6.7 %collective-permute-done.21.refs_5_ = bf16[384,432]{1,0:T(8,128)(2,1)S(1)} collective-permute-done((bf16[384,432]{1,0:T(8,128)(2,1)}, bf16[384,432]{1,0:T(8,128)(2,1)S(1)}, u32[]{:S(2)}, u32[]{:S(2)}) %collective-permute-start.21) | collective-permute-done | bytes 331808 | tf_op jit(solution)/shard_map/ppermute | solution.py:918
  186.8 5.5 %convolution_convert_fusion.2.term_ref = bf16[384,1152]{1,0:T(8,128)(2,1)S(1)} fusion(bf16[384,2304]{1,0:T(8,128)(2,1)} %get-tuple-element.213, bf16[2304,1152]{1,0:T(8,128)(2,1)} %down_ref.1), kind=kOutput, calls=%fused_computation.12 | convolution fusion | flops 2038874112 | bytes 7962624 | tf_op jit(solution)/shard_map/dot_general | solution.py:28
  192.4 1.6 collective-permute-start.23
  194.0 3.1 %input_back.1 = (bf16[384,1152]{1,0:T(8,128)(2,1)S(1)}, f32[3,2,1152]{2,1,0:T(2,128)S(1)}) custom-call(bf16[384,1152]{1,0:T(8,128)(2,1)S(1)} %get-tuple-element.196.term_ref, bf16[384,1152]{1,0:T(8,128)(2,1)} %collective-permute-done.19.other_ref, f32[384,1152]{1,0:T(8,128)S(1)} %copy-done.4, ...), custom_call_target="tpu_custom_call" | custom-call | bytes 5419 | tf_op jit(solution)/shard_map/input_back/pallas_call | solution.py:50
  197.2 3.2 %result.1 = (bf16[384,1152]{1,0:T(8,128)(2,1)S(1)}, f32[3,1,1152]{2,1,0:T(1,128)S(1)}, f32[3,1,1152]{2,1,0:T(1,128)S(1)}) custom-call(bf16[384,1152]{1,0:T(8,128)(2,1)S(1)} %convolution_convert_fusion.2.term_ref, bf16[384,1152]{1,0:T(8,128)(2,1)S(1)} %collective-permute-done.24.other_ref, f32[1,1152]{1,0:T(1,128)S(1)} %reshape.80.bias_ref, ...), custom_call_target="tpu_custom_call" | custom-call | bytes 6308 | tf_op jit(solution)/shard_map/result/pallas_call | solution.py:50
  202.0 2.8 collective-permute-done.23.refs_6_
  204.8 2.1 collective-permute-start.25
  206.9 2.4 collective-permute-start.27
  209.5 5.6 %weight_grad.5 = (f32[288,576]{1,0:T(8,128)S(1)}, bf16[288,576]{1,0:T(8,128)(2,1)}, bf16[288,576]{1,0:T(8,128)(2,1)S(1)}, bf16[288,576]{1,0:T(8,128)(2,1)S(1)}) custom-call(s32[23]{0:T(128)S(1)} %copy-done.35, bf16[768,1152]{1,0:T(8,128)(2,1)} %copy-done.7, bf16[1152,1152]{1,0:T(8,128)(2,1)} %get-tuple-element.165.refs_2_, bf16[384,432]{1,0:T(8,128)(2,1)S(1)} %copy-done.24, ...), custom_call_target="tpu_custom_call" | custom-call | flops 1528823 | bytes 8736 | tf_op jit(solution)/shard_map/weight_grad/pallas_call | solution.py:50
  216.6 1.5 collective-permute-start.28
  218.2 1.3 collective-permute-start.31
  219.5 1.5 collective-permute-start.32
  221.8 1.3 collective-permute-start.34
  223.0 4.1 %collective-permute-done.31.refs_3_ = bf16[192,576]{1,0:T(8,128)(2,1)S(1)} collective-permute-done((bf16[192,576]{1,0:T(8,128)(2,1)S(1)}, bf16[192,576]{1,0:T(8,128)(2,1)S(1)}, u32[]{:S(2)}, u32[]{:S(2)}) %collective-permute-start.31) | collective-permute-done | bytes 221216 | tf_op jit(solution)/shard_map/ppermute | solution.py:918
  227.2 1.2 collective-permute-start.35
  228.4 3.8 %collective-permute-done.32.refs_4_ = bf16[192,576]{1,0:T(8,128)(2,1)S(1)} collective-permute-done((bf16[192,576]{1,0:T(8,128)(2,1)S(1)}, bf16[192,576]{1,0:T(8,128)(2,1)S(1)}, u32[]{:S(2)}, u32[]{:S(2)}) %collective-permute-start.32) | collective-permute-done | bytes 221216 | tf_op jit(solution)/shard_map/ppermute | solution.py:918
  233.5 1.3 collective-permute-start.30
  234.8 4.3 %fusion.6 = bf16[1,768,1152]{2,1,0:T(8,128)(2,1)} fusion(bf16[384,1152]{1,0:T(8,128)(2,1)} %copy-done.50, bf16[1,768,1152]{2,1,0:T(8,128)(2,1)} %param.19, pred[768]{0:T(1024)(128)(4,1)S(1)} %broadcast_compare_fusion, s32[384]{0:T(512)S(1)} %copy-done.68), kind=kOutput, calls=%fused_computation.9 | convolution fusion | flops 681541632 | bytes 4425984 | tf_op jit(solution)/shard_map/dot_general | solution.py:32
  239.1 2.7 fusion.7
  241.8 14.5 %collective-permute-done.29 = bf16[288,576]{1,0:T(8,128)(2,1)} collective-permute-done((bf16[288,576]{1,0:T(8,128)(2,1)}, bf16[288,576]{1,0:T(8,128)(2,1)}, u32[]{:S(2)}, u32[]{:S(2)}) %collective-permute-start.29) | collective-permute-done | bytes 331808 | tf_op jit(solution)/shard_map/ppermute | solution.py:984
  256.4 1.3 add_convert_fusion.1.refs_1_
  257.7 1.4 collective-permute-start.38
  259.8 1.4 collective-permute-start.40
  261.2 5.6 %spread.1 = (f32[6,288,576]{2,1,0:T(8,128)}, f32[6,576]{1,0:T(8,128)}, f32[24,576]{1,0:T(8,128)S(1)}, f32[9,6,576]{2,1,0:T(8,128)S(1)}) custom-call(s32[23]{0:T(128)S(1)} %copy-done.35, s32[1536]{0:T(1024)S(1)} %copy-done.39, bf16[192,576]{1,0:T(8,128)(2,1)S(1)} %constant_dynamic-update-slice_fusion.refs_2_, ...), custom_call_target="tpu_custom_call" | custom-call | bytes 5065 | tf_op jit(solution)/shard_map/spread/pallas_call | solution.py:50
  266.9 4.5 %fusion.9 = f32[18,1152]{1,0:T(8,128)S(1)} fusion(bf16[1152,6,576]{0,2,1:T(8,128)(2,1)} %param.28, bf16[18,6,576]{2,1,0:T(8,128)(2,1)S(1)} %pad_maximum_fusion.1), kind=kOutput, calls=%fused_computation.15 | convolution fusion | flops 143327232 | bytes 8169984 | tf_op jit(solution)/shard_map/sgf,gfd->sd/dot_general | solution.py:1226
  274.3 2.3 join_down.1
  277.4 7.0 %collective-permute-done.40.refs_4_ = bf16[288,576]{1,0:T(8,128)(2,1)} collective-permute-done((bf16[288,576]{1,0:T(8,128)(2,1)S(1)}, bf16[288,576]{1,0:T(8,128)(2,1)}, u32[]{:S(2)}, u32[]{:S(2)}) %collective-permute-start.40) | collective-permute-done | bytes 331808 | tf_op jit(solution)/shard_map/ppermute | solution.py:918
  284.4 3.3 %join_qkv.1 = (f32[3,288,576]{2,1,0:T(8,128)}, f32[288,576]{1,0:T(8,128)}) custom-call(s32[23]{0:T(128)S(1)} %copy-done.35, bf16[288,576]{1,0:T(8,128)(2,1)S(1)} %add_convert_fusion.1.refs_1_, bf16[288,576]{1,0:T(8,128)(2,1)S(1)} %collective-permute-done.38.refs_2_, bf16[288,576]{1,0:T(8,128)(2,1)} %collective-permute-done.39.refs_3_, ...), custom_call_target="tpu_custom_call" | custom-call | bytes 3981 | tf_op jit(solution)/shard_map/join_qkv/pallas_call | solution.py:50
  287.7 1.4 copy-done.8
  289.1 2.2 join_hidden.1
  (257 shorter events, 41.5 us)
Async XLA Ops:
  7.2 104.1 %all-gather.4.cloned.1.call-start = ((), (), s32[]{:S(2)}) async-start(), calls=%async_computation.2 | async-start | bytes 7962624 | tf_op jit(solution)/shard_map/all_gather | solution.py:970
  9.4 112.5 %copy-start.34 = (s32[23]{0:T(128)}, s32[23]{0:T(128)S(1)}, u32[]{:S(2)}) copy-start(s32[23]{0:T(128)S(1)} %plan.1.refs_0_.scalars) | copy-start | bytes 280
  10.8 19.2 %copy-start.42 = (bf16[3,1152]{1,0:T(4,128)(2,1)}, bf16[3,1152]{1,0:T(4,128)(2,1)S(1)}, u32[]{:S(2)}) copy-start(bf16[3,1152]{1,0:T(4,128)(2,1)S(1)} %get-tuple-element.140.active_ref) | copy-start | bytes 20740
  16.3 155.1 %all-gather.6.cloned.1.call-start = ((), (), s32[]{:S(2)}) async-start(), calls=%async_computation.3 | async-start | bytes 4423680 | tf_op jit(solution)/shard_map/all_gather | solution.py:970
  16.4 19.4 %collective-permute-start = (bf16[192,1152]{1,0:T(8,128)(2,1)S(1)}, bf16[192,1152]{1,0:T(8,128)(2,1)S(1)}, u32[]{:S(2)}, u32[]{:S(2)}) collective-permute-start(bf16[192,1152]{1,0:T(8,128)(2,1)S(1)} %constant_dynamic-slice_fusion.1), channel_id=1, source_target_pairs={{0,2},{2,4},{4,6},{1,3},{3,5},{5,7},{8,10},{10,12},{12,14},{9,11},... | collective-permute-start | bytes 1327112 | tf_op jit(solution)/shard_map/ppermute | solution.py:928
  17.7 18.1 %collective-permute-start.1 = (bf16[192,1152]{1,0:T(8,128)(2,1)S(1)}, bf16[192,1152]{1,0:T(8,128)(2,1)S(1)}, u32[]{:S(2)}, u32[]{:S(2)}) collective-permute-start(bf16[192,1152]{1,0:T(8,128)(2,1)S(1)} %constant_dynamic-slice_fusion.1), channel_id=1, source_target_pairs={{2,0},{4,2},{6,4},{3,1},{5,3},{7,5},{10,8},{12,10},{14,12},{11,9},... | collective-permute-start | bytes 1327112 | tf_op jit(solution)/shard_map/ppermute | solution.py:928
  22.3 4.9 %collective-permute-start.3 = (bf16[3,1152]{1,0:T(4,128)(2,1)S(1)}, bf16[3,1152]{1,0:T(4,128)(2,1)S(1)}, u32[]{:S(2)}, u32[]{:S(2)}) collective-permute-start(bf16[3,1152]{1,0:T(4,128)(2,1)S(1)} %get-tuple-element.140.active_ref), channel_id=1, source_target_pairs={{0,8},{8,0},{16,24},{24,16},{1,9},{9,1},{17,25},{25,17},{2,10},{10... | collective-permute-start | bytes 20744 | tf_op jit(solution)/shard_map/ppermute | solution.py:918
  23.8 3.7 %collective-permute-start.4 = (bf16[3,1152]{1,0:T(4,128)(2,1)S(1)}, bf16[3,1152]{1,0:T(4,128)(2,1)S(1)}, u32[]{:S(2)}, u32[]{:S(2)}) collective-permute-start(bf16[3,1152]{1,0:T(4,128)(2,1)S(1)} %get-tuple-element.140.active_ref), channel_id=1, source_target_pairs={{0,16},{8,24},{16,0},{24,8},{1,17},{9,25},{17,1},{25,9},{2,18},{10... | collective-permute-start | bytes 20744 | tf_op jit(solution)/shard_map/ppermute | solution.py:918
  25.3 4.7 %collective-permute-start.5 = (bf16[3,1152]{1,0:T(4,128)(2,1)S(1)}, bf16[3,1152]{1,0:T(4,128)(2,1)S(1)}, u32[]{:S(2)}, u32[]{:S(2)}) collective-permute-start(bf16[3,1152]{1,0:T(4,128)(2,1)S(1)} %get-tuple-element.140.active_ref), channel_id=1, source_target_pairs={{0,24},{8,16},{16,8},{24,0},{1,25},{9,17},{17,9},{25,1},{2,26},{10... | collective-permute-start | bytes 20744 | tf_op jit(solution)/shard_map/ppermute | solution.py:918
  35.9 3.2 %collective-permute-start.2 = (bf16[192,1152]{1,0:T(8,128)(2,1)S(1)}, bf16[192,1152]{1,0:T(8,128)(2,1)S(1)}, u32[]{:S(2)}, u32[]{:S(2)}) collective-permute-start(bf16[192,1152]{1,0:T(8,128)(2,1)S(1)} %broadcast_select_fusion.1), channel_id=1, source_target_pairs={{0,1},{1,0},{2,3},{3,2},{4,5},{5,4},{6,7},{7,6},{8,9},{9,8},{10,11... | collective-permute-start | bytes 1327112 | tf_op jit(solution)/shard_map/ppermute | solution.py:918
  36.0 2.1 collective-permute-start.6
  39.0 20.2 %copy-start.2 = (f32[15,6,1152]{2,1,0:T(8,128)}, f32[15,6,1152]{2,1,0:T(8,128)S(1)}, u32[]{:S(2)}) copy-start(f32[15,6,1152]{2,1,0:T(8,128)S(1)} %pick.1.mod_ref.refs_2_) | copy-start | bytes 1244164
  59.0 3.7 %collective-permute-start.7 = (f32[384,1152]{1,0:T(8,128)S(1)}, f32[384,1152]{1,0:T(8,128)S(1)}, u32[]{:S(2)}, u32[]{:S(2)}) collective-permute-start(f32[384,1152]{1,0:T(8,128)S(1)} %get-tuple-element.144.term_ref), channel_id=1, source_target_pairs={{0,1},{1,0},{2,3},{3,2},{4,5},{5,4},{6,7},{7,6},{8,9},{9,8},{10,11... | collective-permute-start | bytes 5308424 | tf_op jit(solution)/shard_map/ppermute | solution.py:918
  77.6 139.1 %reduce-scatter.3.cloned.1.call-start = ((), (), s32[]{:S(2)}) async-start(), calls=%async_computation.4 | async-start | bytes 1843200 | tf_op jit(solution)/shard_map/reduce_scatter | solution.py:1132
  77.6 17.6 %collective-permute-start.8 = (bf16[384,640]{1,0:T(8,128)(2,1)}, bf16[384,640]{1,0:T(8,128)(2,1)S(1)}, u32[]{:S(2)}, u32[]{:S(2)}) collective-permute-start(bf16[384,640]{1,0:T(8,128)(2,1)} %copy-done.56), channel_id=1, source_target_pairs={{0,8},{8,0},{16,24},{24,16},{1,9},{9,1},{17,25},{25,17},{2,10},{10... | collective-permute-start | bytes 1474568 | tf_op jit(solution)/shard_map/ppermute | solution.py:918
  77.7 18.3 %collective-permute-start.9 = (bf16[384,640]{1,0:T(8,128)(2,1)S(1)}, bf16[384,640]{1,0:T(8,128)(2,1)S(1)}, u32[]{:S(2)}, u32[]{:S(2)}) collective-permute-start(bf16[384,640]{1,0:T(8,128)(2,1)S(1)} %get-tuple-element.148), channel_id=1, source_target_pairs={{0,16},{8,24},{16,0},{24,8},{1,17},{9,25},{17,1},{25,9},{2,18},{10... | collective-permute-start | bytes 1474568 | tf_op jit(solution)/shard_map/ppermute | solution.py:918
  96.8 3.7 %collective-permute-start.10 = (f32[384,1152]{1,0:T(8,128)S(1)}, f32[384,1152]{1,0:T(8,128)S(1)}, u32[]{:S(2)}, u32[]{:S(2)}) collective-permute-start(f32[384,1152]{1,0:T(8,128)S(1)} %get-tuple-element.155.term_ref), channel_id=1, source_target_pairs={{0,1},{1,0},{2,3},{3,2},{4,5},{5,4},{6,7},{7,6},{8,9},{9,8},{10,11... | collective-permute-start | bytes 5308424 | tf_op jit(solution)/shard_map/ppermute | solution.py:918
  96.8 24.5 %collective-permute-start.13 = (bf16[384,640]{1,0:T(8,128)(2,1)}, bf16[384,640]{1,0:T(8,128)(2,1)}, u32[]{:S(2)}, u32[]{:S(2)}) collective-permute-start(bf16[384,640]{1,0:T(8,128)(2,1)} %get-tuple-element.171), channel_id=1, source_target_pairs={{0,24},{8,16},{16,8},{24,0},{1,25},{9,17},{17,9},{25,1},{2,26},{10... | collective-permute-start | bytes 1474568 | tf_op jit(solution)/shard_map/ppermute | solution.py:918
  101.7 20.2 %copy-start.14 = (bf16[384,576]{1,0:T(8,128)(2,1)S(1)}, bf16[384,576]{1,0:T(8,128)(2,1)}, u32[]{:S(2)}) copy-start(bf16[384,576]{1,0:T(8,128)(2,1)} %copy-done.13) | copy-start | bytes 1327108
  111.3 23.1 %copy-start.44 = (f32[3,1,1152]{2,1,0:T(1,128)}, f32[3,1,1152]{2,1,0:T(1,128)S(1)}, u32[]{:S(2)}) copy-start(f32[3,1,1152]{2,1,0:T(1,128)S(1)} %get-tuple-element.216.refs_1_) | copy-start | bytes 41476
  111.3 29.1 %collective-permute-start.11 = (bf16[384,576]{1,0:T(8,128)(2,1)}, bf16[384,576]{1,0:T(8,128)(2,1)}, u32[]{:S(2)}, u32[]{:S(2)}) collective-permute-start(bf16[384,576]{1,0:T(8,128)(2,1)} %copy-done.15), channel_id=1, source_target_pairs={{0,2},{2,4},{4,6},{1,3},{3,5},{5,7},{8,10},{10,12},{12,14},{9,11},... | collective-permute-start | bytes 1327112 | tf_op jit(solution)/shard_map/ppermute | solution.py:928
  112.6 27.9 %collective-permute-start.12 = (bf16[384,576]{1,0:T(8,128)(2,1)}, bf16[384,576]{1,0:T(8,128)(2,1)}, u32[]{:S(2)}, u32[]{:S(2)}) collective-permute-start(bf16[384,576]{1,0:T(8,128)(2,1)} %copy-done.15), channel_id=1, source_target_pairs={{2,0},{4,2},{6,4},{3,1},{5,3},{7,5},{10,8},{12,10},{14,12},{11,9},... | collective-permute-start | bytes 1327112 | tf_op jit(solution)/shard_map/ppermute | solution.py:928
  118.3 23.2 %collective-permute-start.14 = (bf16[384,640]{1,0:T(8,128)(2,1)}, bf16[384,640]{1,0:T(8,128)(2,1)}, u32[]{:S(2)}, u32[]{:S(2)}) collective-permute-start(bf16[384,640]{1,0:T(8,128)(2,1)} %copy-done.55), channel_id=1, source_target_pairs={{0,8},{8,0},{16,24},{24,16},{1,9},{9,1},{17,25},{25,17},{2,10},{10... | collective-permute-start | bytes 1474568 | tf_op jit(solution)/shard_map/ppermute | solution.py:918
  118.7 22.8 %collective-permute-start.15 = (bf16[384,640]{1,0:T(8,128)(2,1)}, bf16[384,640]{1,0:T(8,128)(2,1)}, u32[]{:S(2)}, u32[]{:S(2)}) collective-permute-start(bf16[384,640]{1,0:T(8,128)(2,1)} %copy-done.54), channel_id=1, source_target_pairs={{0,16},{8,24},{16,0},{24,8},{1,17},{9,25},{17,1},{25,9},{2,18},{10... | collective-permute-start | bytes 1474568 | tf_op jit(solution)/shard_map/ppermute | solution.py:918
  121.2 22.0 %collective-permute-start.16 = (bf16[384,640]{1,0:T(8,128)(2,1)}, bf16[384,640]{1,0:T(8,128)(2,1)}, u32[]{:S(2)}, u32[]{:S(2)}) collective-permute-start(bf16[384,640]{1,0:T(8,128)(2,1)} %copy-done.53), channel_id=1, source_target_pairs={{0,24},{8,16},{16,8},{24,0},{1,25},{9,17},{17,9},{25,1},{2,26},{10... | collective-permute-start | bytes 1474568 | tf_op jit(solution)/shard_map/ppermute | solution.py:918
  143.3 98.5 %reduce-scatter.5.cloned.1.call-start = ((), (), s32[]{:S(2)}) async-start(), calls=%async_computation.5 | async-start | bytes 1843200 | tf_op jit(solution)/shard_map/reduce_scatter | solution.py:1146
  143.3 23.1 %collective-permute-start.17 = (bf16[144,1152]{1,0:T(8,128)(2,1)}, bf16[144,1152]{1,0:T(8,128)(2,1)S(1)}, u32[]{:S(2)}, u32[]{:S(2)}) collective-permute-start(bf16[144,1152]{1,0:T(8,128)(2,1)} %get-tuple-element.187), channel_id=1, source_target_pairs={{0,8},{8,0},{16,24},{24,16},{1,9},{9,1},{17,25},{25,17},{2,10},{10... | collective-permute-start | bytes 995336 | tf_op jit(solution)/shard_map/ppermute | solution.py:918
  144.3 22.8 %collective-permute-start.18 = (bf16[144,1152]{1,0:T(8,128)(2,1)}, bf16[144,1152]{1,0:T(8,128)(2,1)S(1)}, u32[]{:S(2)}, u32[]{:S(2)}) collective-permute-start(bf16[144,1152]{1,0:T(8,128)(2,1)} %get-tuple-element.188), channel_id=1, source_target_pairs={{0,16},{8,24},{16,0},{24,8},{1,17},{9,25},{17,1},{25,9},{2,18},{10... | collective-permute-start | bytes 995336 | tf_op jit(solution)/shard_map/ppermute | solution.py:918
  167.9 18.9 %collective-permute-start.19 = (bf16[384,1152]{1,0:T(8,128)(2,1)S(1)}, bf16[384,1152]{1,0:T(8,128)(2,1)}, u32[]{:S(2)}, u32[]{:S(2)}) collective-permute-start(bf16[384,1152]{1,0:T(8,128)(2,1)S(1)} %get-tuple-element.196.term_ref), channel_id=1, source_target_pairs={{0,1},{1,0},{2,3},{3,2},{4,5},{5,4},{6,7},{7,6},{8,9},{9,8},{10,11... | collective-permute-start | bytes 2654216 | tf_op jit(solution)/shard_map/ppermute | solution.py:918
  167.9 12.1 %collective-permute-start.20 = (bf16[384,432]{1,0:T(8,128)(2,1)}, bf16[384,432]{1,0:T(8,128)(2,1)S(1)}, u32[]{:S(2)}, u32[]{:S(2)}) collective-permute-start(bf16[384,432]{1,0:T(8,128)(2,1)} %get-tuple-element.197), channel_id=1, source_target_pairs={{0,8},{8,0},{16,24},{24,16},{1,9},{9,1},{17,25},{25,17},{2,10},{10... | collective-permute-start | bytes 995336 | tf_op jit(solution)/shard_map/ppermute | solution.py:918
  167.9 18.8 %collective-permute-start.21 = (bf16[384,432]{1,0:T(8,128)(2,1)}, bf16[384,432]{1,0:T(8,128)(2,1)S(1)}, u32[]{:S(2)}, u32[]{:S(2)}) collective-permute-start(bf16[384,432]{1,0:T(8,128)(2,1)} %get-tuple-element.198), channel_id=1, source_target_pairs={{0,16},{8,24},{16,0},{24,8},{1,17},{9,25},{17,1},{25,9},{2,18},{10... | collective-permute-start | bytes 995336 | tf_op jit(solution)/shard_map/ppermute | solution.py:918
  167.9 18.8 %collective-permute-start.22 = (bf16[144,1152]{1,0:T(8,128)(2,1)}, bf16[144,1152]{1,0:T(8,128)(2,1)}, u32[]{:S(2)}, u32[]{:S(2)}) collective-permute-start(bf16[144,1152]{1,0:T(8,128)(2,1)} %get-tuple-element.199), channel_id=1, source_target_pairs={{0,24},{8,16},{16,8},{24,0},{1,25},{9,17},{17,9},{25,1},{2,26},{10... | collective-permute-start | bytes 995336 | tf_op jit(solution)/shard_map/ppermute | solution.py:918
  179.1 108.6 %all-gather.8.cloned.1.call-start = ((), (), s32[]{:S(2)}) async-start(), calls=%async_computation.6 | async-start | bytes 1843200 | tf_op jit(solution)/shard_map/all_gather | solution.py:1203
  179.2 13.2 %copy-start.58 = (bf16[384,432]{1,0:T(8,128)(2,1)S(1)}, bf16[384,432]{1,0:T(8,128)(2,1)}, u32[]{:S(2)}) copy-start(bf16[384,432]{1,0:T(8,128)(2,1)} %copy-done.57) | copy-start | bytes 995332
  179.2 14.8 %copy-start.71 = (bf16[1152]{0:T(1024)(128)(2,1)S(1)}, bf16[1152]{0:T(1024)(128)(2,1)}, u32[]{:S(2)}) copy-start(bf16[1152]{0:T(1024)(128)(2,1)} %param.27) | copy-start | bytes 6916
  179.2 14.8 %copy-start.4 = (f32[384,1152]{1,0:T(8,128)S(1)}, f32[384,1152]{1,0:T(8,128)}, u32[]{:S(2)}) copy-start(f32[384,1152]{1,0:T(8,128)} %copy-done.3) | copy-start | bytes 5308420
  192.3 4.9 %collective-permute-start.24 = (bf16[384,1152]{1,0:T(8,128)(2,1)S(1)}, bf16[384,1152]{1,0:T(8,128)(2,1)S(1)}, u32[]{:S(2)}, u32[]{:S(2)}) collective-permute-start(bf16[384,1152]{1,0:T(8,128)(2,1)S(1)} %convolution_convert_fusion.2.term_ref), channel_id=1, source_target_pairs={{0,1},{1,0},{2,3},{3,2},{4,5},{5,4},{6,7},{7,6},{8,9},{9,8},{10,11... | collective-permute-start | bytes 2654216 | tf_op jit(solution)/shard_map/ppermute | solution.py:918
  192.4 12.4 %collective-permute-start.23 = (bf16[384,432]{1,0:T(8,128)(2,1)S(1)}, bf16[384,432]{1,0:T(8,128)(2,1)S(1)}, u32[]{:S(2)}, u32[]{:S(2)}) collective-permute-start(bf16[384,432]{1,0:T(8,128)(2,1)S(1)} %copy-done.58), channel_id=1, source_target_pairs={{0,24},{8,16},{16,8},{24,0},{1,25},{9,17},{17,9},{25,1},{2,26},{10... | collective-permute-start | bytes 995336 | tf_op jit(solution)/shard_map/ppermute | solution.py:918
  197.0 18.1 %copy-start.50 = (bf16[384,1152]{1,0:T(8,128)(2,1)}, bf16[384,1152]{1,0:T(8,128)(2,1)S(1)}, u32[]{:S(2)}) copy-start(bf16[384,1152]{1,0:T(8,128)(2,1)S(1)} %get-tuple-element.241) | copy-start | bytes 2654212
  197.1 12.4 %copy-start.24 = (bf16[384,432]{1,0:T(8,128)(2,1)S(1)}, bf16[384,432]{1,0:T(8,128)(2,1)}, u32[]{:S(2)}) copy-start(bf16[384,432]{1,0:T(8,128)(2,1)} %copy-done.23) | copy-start | bytes 995332
  197.1 12.4 %copy-start.27 = (bf16[144,1152]{1,0:T(8,128)(2,1)S(1)}, bf16[144,1152]{1,0:T(8,128)(2,1)}, u32[]{:S(2)}) copy-start(bf16[144,1152]{1,0:T(8,128)(2,1)} %copy-done.26) | copy-start | bytes 995332
  197.1 12.4 %copy-start.29 = (bf16[144,1152]{1,0:T(8,128)(2,1)S(1)}, bf16[144,1152]{1,0:T(8,128)(2,1)}, u32[]{:S(2)}) copy-start(bf16[144,1152]{1,0:T(8,128)(2,1)} %copy-done.28) | copy-start | bytes 995332
  197.1 12.4 %copy-start.31 = (bf16[144,1152]{1,0:T(8,128)(2,1)S(1)}, bf16[144,1152]{1,0:T(8,128)(2,1)}, u32[]{:S(2)}) copy-start(bf16[144,1152]{1,0:T(8,128)(2,1)} %copy-done.30) | copy-start | bytes 995332
  204.8 11.8 %collective-permute-start.25 = (bf16[48,576]{1,0:T(8,128)(2,1)S(1)}, bf16[48,576]{1,0:T(8,128)(2,1)S(1)}, u32[]{:S(2)}, u32[]{:S(2)}) collective-permute-start(bf16[48,576]{1,0:T(8,128)(2,1)S(1)} %collect.1), channel_id=1, source_target_pairs={{0,2},{2,0},{4,6},{6,4},{1,3},{3,1},{5,7},{7,5},{8,10},{10,8},{12,... | collective-permute-start | bytes 165896 | tf_op jit(solution)/shard_map/ppermute | solution.py:918
  206.9 9.7 %collective-permute-start.26 = (bf16[48,576]{1,0:T(8,128)(2,1)S(1)}, bf16[48,576]{1,0:T(8,128)(2,1)S(1)}, u32[]{:S(2)}, u32[]{:S(2)}) collective-permute-start(bf16[48,576]{1,0:T(8,128)(2,1)S(1)} %collect.1), channel_id=1, source_target_pairs={{0,4},{2,6},{4,0},{6,2},{1,5},{3,7},{5,1},{7,3},{8,12},{10,14},{12... | collective-permute-start | bytes 165896 | tf_op jit(solution)/shard_map/ppermute | solution.py:918
  206.9 9.7 %collective-permute-start.27 = (bf16[48,576]{1,0:T(8,128)(2,1)S(1)}, bf16[48,576]{1,0:T(8,128)(2,1)S(1)}, u32[]{:S(2)}, u32[]{:S(2)}) collective-permute-start(bf16[48,576]{1,0:T(8,128)(2,1)S(1)} %collect.1), channel_id=1, source_target_pairs={{0,6},{2,4},{4,2},{6,0},{1,7},{3,5},{5,3},{7,1},{8,14},{10,12},{12... | collective-permute-start | bytes 165896 | tf_op jit(solution)/shard_map/ppermute | solution.py:918
  209.5 25.3 %copy-start.68 = (s32[384]{0:T(512)S(1)}, s32[384]{0:T(512)}, u32[]{:S(2)}) copy-start(s32[384]{0:T(512)} %copy-done.66) | copy-start | bytes 4612
  216.6 16.8 %collective-permute-start.28 = (bf16[288,576]{1,0:T(8,128)(2,1)}, bf16[288,576]{1,0:T(8,128)(2,1)S(1)}, u32[]{:S(2)}, u32[]{:S(2)}) collective-permute-start(bf16[288,576]{1,0:T(8,128)(2,1)} %get-tuple-element.233), channel_id=1, source_target_pairs={{0,2},{2,4},{4,6},{6,0},{1,3},{3,5},{5,7},{7,1},{8,10},{10,12},{12... | collective-permute-start | bytes 995336 | tf_op jit(solution)/shard_map/ppermute | solution.py:984
  218.2 9.0 %collective-permute-start.31 = (bf16[192,576]{1,0:T(8,128)(2,1)S(1)}, bf16[192,576]{1,0:T(8,128)(2,1)S(1)}, u32[]{:S(2)}, u32[]{:S(2)}) collective-permute-start(bf16[192,576]{1,0:T(8,128)(2,1)S(1)} %constant_dynamic-update-slice_fusion.refs_2_), channel_id=1, source_target_pairs={{0,8},{8,0},{16,24},{24,16},{1,9},{9,1},{17,25},{25,17},{2,10},{10... | collective-permute-start | bytes 663560 | tf_op jit(solution)/shard_map/ppermute | solution.py:918
  219.5 12.7 %collective-permute-start.32 = (bf16[192,576]{1,0:T(8,128)(2,1)S(1)}, bf16[192,576]{1,0:T(8,128)(2,1)S(1)}, u32[]{:S(2)}, u32[]{:S(2)}) collective-permute-start(bf16[192,576]{1,0:T(8,128)(2,1)S(1)} %constant_dynamic-update-slice_fusion.refs_2_), channel_id=1, source_target_pairs={{0,16},{8,24},{16,0},{24,8},{1,17},{9,25},{17,1},{25,9},{2,18},{10... | collective-permute-start | bytes 663560 | tf_op jit(solution)/shard_map/ppermute | solution.py:918
  221.0 12.2 %collective-permute-start.33 = (bf16[192,576]{1,0:T(8,128)(2,1)S(1)}, bf16[192,576]{1,0:T(8,128)(2,1)S(1)}, u32[]{:S(2)}, u32[]{:S(2)}) collective-permute-start(bf16[192,576]{1,0:T(8,128)(2,1)S(1)} %constant_dynamic-update-slice_fusion.refs_2_), channel_id=1, source_target_pairs={{0,24},{8,16},{16,8},{24,0},{1,25},{9,17},{17,9},{25,1},{2,26},{10... | collective-permute-start | bytes 663560 | tf_op jit(solution)/shard_map/ppermute | solution.py:918
  221.8 17.3 %copy-start.52 = (bf16[384,1152]{1,0:T(8,128)(2,1)S(1)}, bf16[384,1152]{1,0:T(8,128)(2,1)}, u32[]{:S(2)}) copy-start(bf16[384,1152]{1,0:T(8,128)(2,1)} %copy-done.51) | copy-start | bytes 2654212
  221.8 17.4 %copy-start.73 = (bf16[1,768,1152]{2,1,0:T(8,128)(2,1)S(1)}, bf16[1,768,1152]{2,1,0:T(8,128)(2,1)}, u32[]{:S(2)}) copy-start(bf16[1,768,1152]{2,1,0:T(8,128)(2,1)} %param.15) | copy-start | bytes 5308420
  221.8 34.6 %collective-permute-start.34 = (bf16[288,640]{1,0:T(8,128)(2,1)}, bf16[288,640]{1,0:T(8,128)(2,1)S(1)}, u32[]{:S(2)}, u32[]{:S(2)}) collective-permute-start(bf16[288,640]{1,0:T(8,128)(2,1)} %reduce-scatter.3.cloned.1.call-done.refs_1_), channel_id=1, source_target_pairs={{0,8},{8,0},{16,24},{24,16},{1,9},{9,1},{17,25},{25,17},{2,10},{10... | collective-permute-start | bytes 1105928 | tf_op jit(solution)/shard_map/ppermute | solution.py:918
  227.2 29.2 %collective-permute-start.35 = (bf16[288,640]{1,0:T(8,128)(2,1)}, bf16[288,640]{1,0:T(8,128)(2,1)S(1)}, u32[]{:S(2)}, u32[]{:S(2)}) collective-permute-start(bf16[288,640]{1,0:T(8,128)(2,1)} %reduce-scatter.3.cloned.1.call-done.refs_1_), channel_id=1, source_target_pairs={{0,16},{8,24},{16,0},{24,8},{1,17},{9,25},{17,1},{25,9},{2,18},{10... | collective-permute-start | bytes 1105928 | tf_op jit(solution)/shard_map/ppermute | solution.py:918
  232.2 24.2 %collective-permute-start.36 = (bf16[288,640]{1,0:T(8,128)(2,1)}, bf16[288,640]{1,0:T(8,128)(2,1)S(1)}, u32[]{:S(2)}, u32[]{:S(2)}) collective-permute-start(bf16[288,640]{1,0:T(8,128)(2,1)} %reduce-scatter.3.cloned.1.call-done.refs_1_), channel_id=1, source_target_pairs={{0,24},{8,16},{16,8},{24,0},{1,25},{9,17},{17,9},{25,1},{2,26},{10... | collective-permute-start | bytes 1105928 | tf_op jit(solution)/shard_map/ppermute | solution.py:918
  233.1 23.2 %collective-permute-start.29 = (bf16[288,576]{1,0:T(8,128)(2,1)}, bf16[288,576]{1,0:T(8,128)(2,1)}, u32[]{:S(2)}, u32[]{:S(2)}) collective-permute-start(bf16[288,576]{1,0:T(8,128)(2,1)} %copy-done.60), channel_id=1, source_target_pairs={{0,4},{2,6},{4,0},{6,2},{1,5},{3,7},{5,1},{7,3},{8,12},{10,14},{12... | collective-permute-start | bytes 995336 | tf_op jit(solution)/shard_map/ppermute | solution.py:984
  233.5 22.9 %collective-permute-start.30 = (bf16[288,576]{1,0:T(8,128)(2,1)}, bf16[288,576]{1,0:T(8,128)(2,1)}, u32[]{:S(2)}, u32[]{:S(2)}) collective-permute-start(bf16[288,576]{1,0:T(8,128)(2,1)} %copy-done.59), channel_id=1, source_target_pairs={{0,6},{2,0},{4,2},{6,4},{1,7},{3,1},{5,3},{7,5},{8,14},{10,8},{12,... | collective-permute-start | bytes 995336 | tf_op jit(solution)/shard_map/ppermute | solution.py:984
  241.8 19.4 %copy-start.39 = (s32[1536]{0:T(1024)S(1)}, s32[1536]{0:T(1024)}, u32[]{:S(2)}) copy-start(s32[1536]{0:T(1024)} %copy-done.38) | copy-start | bytes 18436
  241.8 19.4 %copy-start.33 = (bf16[192,576]{1,0:T(8,128)(2,1)S(1)}, bf16[192,576]{1,0:T(8,128)(2,1)}, u32[]{:S(2)}) copy-start(bf16[192,576]{1,0:T(8,128)(2,1)} %copy-done.32) | copy-start | bytes 663556
  257.7 19.7 %collective-permute-start.38 = (bf16[288,576]{1,0:T(8,128)(2,1)S(1)}, bf16[288,576]{1,0:T(8,128)(2,1)S(1)}, u32[]{:S(2)}, u32[]{:S(2)}) collective-permute-start(bf16[288,576]{1,0:T(8,128)(2,1)S(1)} %add_convert_fusion.1.refs_1_), channel_id=1, source_target_pairs={{0,8},{8,0},{16,24},{24,16},{1,9},{9,1},{17,25},{25,17},{2,10},{10... | collective-permute-start | bytes 995336 | tf_op jit(solution)/shard_map/ppermute | solution.py:918
  259.1 18.3 %collective-permute-start.39 = (bf16[288,576]{1,0:T(8,128)(2,1)S(1)}, bf16[288,576]{1,0:T(8,128)(2,1)}, u32[]{:S(2)}, u32[]{:S(2)}) collective-permute-start(bf16[288,576]{1,0:T(8,128)(2,1)S(1)} %add_convert_fusion.1.refs_1_), channel_id=1, source_target_pairs={{0,16},{8,24},{16,0},{24,8},{1,17},{9,25},{17,1},{25,9},{2,18},{10... | collective-permute-start | bytes 995336 | tf_op jit(solution)/shard_map/ppermute | solution.py:918
  259.8 24.5 %collective-permute-start.40 = (bf16[288,576]{1,0:T(8,128)(2,1)S(1)}, bf16[288,576]{1,0:T(8,128)(2,1)}, u32[]{:S(2)}, u32[]{:S(2)}) collective-permute-start(bf16[288,576]{1,0:T(8,128)(2,1)S(1)} %add_convert_fusion.1.refs_1_), channel_id=1, source_target_pairs={{0,24},{8,16},{16,8},{24,0},{1,25},{9,17},{17,9},{25,1},{2,26},{10... | collective-permute-start | bytes 995336 | tf_op jit(solution)/shard_map/ppermute | solution.py:918
  271.4 5.2 %collective-permute-start.37 = (f32[9,1152]{1,0:T(8,128)S(1)}, f32[9,1152]{1,0:T(8,128)S(1)}, u32[]{:S(2)}, u32[]{:S(2)}) collective-permute-start(f32[9,1152]{1,0:T(8,128)S(1)} %slice_add_fusion), channel_id=1, source_target_pairs={{0,1},{1,0},{2,3},{3,2},{4,5},{5,4},{6,7},{7,6},{8,9},{9,8},{10,11... | collective-permute-start | bytes 124424 | tf_op jit(solution)/shard_map/ppermute | solution.py:918
  (56 other events, 208.8 us)
Sparse Core Ops, SparseCore 0:
  16.4 49.9 all-gather.3
  77.7 46.3 all-gather.5
  143.4 32.6 reduce-scatter.2
  179.2 34.8 reduce-scatter.4
  242.0 43.4 all-gather.7

commit v2 on v1

--- a/solution.py
+++ b/solution.py
@@ -941,11 +941,6 @@
     return [block] + [xor_permute(block, axis, r) for r in range(1, lax.axis_size(axis))]
 
 
-def in_order(entries, axis):
-    order = jnp.arange(len(entries), dtype=jnp.int32) ^ lax.axis_index(axis)
-    return jnp.take(jnp.stack(entries), order, axis=0)
-
-
 def trade(pieces, axis, entries):
     return {r: xor_permute(pieces[r], axis, r) for r in entries}
 
@@ -958,12 +953,6 @@
 
 def half_width(width):
     return -(-width // (2 * LANES)) * LANES
-
-
-def share_of(block):
-    half = half_width(block.shape[1])
-    first, last = block[:, :half], block[:, block.shape[1] - half :]
-    return jnp.where(lax.axis_index("head") == 0, first, last)
 
 
 def gather_shares(share):
@@ -1110,22 +1099,26 @@
         (back_term, gelu_first, gelu_pieces, pre_pieces)
     )
     gelu_last = trade(gelu_pieces, "pack", further)
+    hidden_other_packs, down_other_packs = others(
+        scalars, token_shares, mod_all, places + near_count, packs, count
+    )
+    back_other, hidden_other_packs, down_other_packs = hold(
+        (swap(back_term), hidden_other_packs, down_other_packs)
+    )
     middle_grad, branch_grad, attended_grad, middle_sums, output_sums = middle_back(
-        back_term, swap(back_term), branch_one, kept_rows, upstream, mod_places, output_weight
-    )
-    attended_grad, token_shares, pre_pieces, gelu, branch_grad = hold(
-        (attended_grad, token_shares, pre_pieces, gelu, branch_grad)
+        back_term, back_other, branch_one, kept_rows, upstream, mod_places, output_weight
+    )
+    attended_grad, pre_pieces, gelu, branch_grad = hold(
+        (attended_grad, pre_pieces, gelu, branch_grad)
     )
     near_grad = beside(attended_grad)
     rows = width // blocks
 
-    pre_first = trade(pre_pieces, "pack", range(1, packs))
+    pre_first = trade(pre_pieces, "pack", one_step)
     gelu_all = by_entry(gelu_pieces, gelu_first, gelu_last)
-    hidden_other_packs, down_other_packs = others(
-        scalars, token_shares, mod_all, places + near_count, packs, count
-    )
     down_raw = weight_grad(scalars, width, 0, [down_in, down_other_packs], gelu_all)[0]
     output_pieces = own_weight_grad(scalars, attended, branch_grad, packs)
+    pre_last = trade(pre_pieces, "pack", further)
     near_grad, down_raw, output_pieces, pre_first = hold(
         (near_grad, down_raw, output_pieces, pre_first)
     )
@@ -1134,14 +1127,14 @@
     hidden_term, qkv_sums, qkv_pieces = attend_back(
         base, scalars, qkv_rows, attended_grad, near_grad, qkv_turned, packs
     )
-    hidden_term, qkv_pieces, output_first, output_pieces, gelu, pre_first = hold(
-        (hidden_term, qkv_pieces, output_first, output_pieces, gelu, pre_first)
+    hidden_term, qkv_pieces, output_first, output_pieces, gelu, pre_last = hold(
+        (hidden_term, qkv_pieces, output_first, output_pieces, gelu, pre_last)
     )
     qkv_first = trade(qkv_pieces, "pack", one_step)
     qkv_last = trade(qkv_pieces, "pack", further)
     output_last = trade(output_pieces, "pack", further)
 
-    pre_all = by_entry(pre_pieces, pre_first)
+    pre_all = by_entry(pre_pieces, pre_first, pre_last)
     hidden_raw = weight_grad(scalars, width, 0, [hidden_two_shares], pre_all)[0]
     hidden_reduced = lax.psum_scatter(hidden_raw, "blk", scatter_dimension=0, tiled=True)
     hidden_other, qkv_first, output_last, hidden_raw, gelu = hold(

time: 304 us -> 302 us (level)
  the two profiles are of different devices: /device:TPU:24 before, /device:TPU:0 now
where the time goes in v2:
time: 302 us; the launch traced here: 297 us
  Pallas kernels  102 us (34%)
  starting transfers between devices  64.4 us (21%)
  waiting for transfers between devices  52.6 us (17%)
  matrix products  30.6 us (10%)
  local copies, waits for them, and re-layouts  25.4 us (8%)
  between operations  15.5 us (5%)
  other arithmetic  6.43 us (2%)
    pallas_call x20, Pallas kernels, kernel_call(): pl.pallas_call(body, name=name, out_shape=tuple(outs), grid=grid, in_spec...  94.3 us
    ppermute x34, starting transfers between devices, xor_permute(): lax.ppermute(block, axis, [(i, i ^ bits) for i in range(lax.axis_size(axi...  41.8 us
    ppermute x34, waiting for transfers between devices, xor_permute(): lax.ppermute(block, axis, [(i, i ^ bits) for i in range(lax.axis_size(axi...  31.9 us
    unnamed x114, local copies, waits for them, and re-layouts  22.3 us
    ppermute x4, starting transfers between devices, move(): return lax.ppermute(block, 'blk', pairs)  18.2 us
    all_gather x1, waiting for transfers between devices, local(): hidden_gathered = lax.all_gather(hidden_reduced, 'pack', axis=0, tiled=True)  10.1 us
    ppermute x3, waiting for transfers between devices, send_blk(): found.append(lax.ppermute(pieces[step], 'blk', pairs))  9.21 us
    dot_general x3, matrix products, bf_dot(): return jnp.dot(operand_a, operand_b, preferred_element_type=F32)  9.09 us
  transfers between devices with their start and end apart: 46, of which 16 were waited for; matrix products, arithmetic and copies ran while one was open for 12% of the time, Pallas kernels for 33%

profile of v2, /device:TPU:0, one launch (start us, length us, event | category | flops | bytes accessed | tf_op | source)
XLA Modules:
  0.0 297.1 jit_solution(17210720793749138248)
XLA Ops:
  8.7 1.3 plan.1.refs_0_.scalars
  11.5 2.6 convolution_convert_fusion.4.own_ref.kept_ref
  16.3 4.0 %collective-permute-start.5 = (bf16[3,1152]{1,0:T(4,128)(2,1)S(1)}, bf16[3,1152]{1,0:T(4,128)(2,1)S(1)}, u32[]{:S(2)}, u32[]{:S(2)}) collective-permute-start(bf16[3,1152]{1,0:T(4,128)(2,1)S(1)} %get-tuple-element.139.active_ref), channel_id=1, source_target_pairs={{0,24},{8,16},{16,8},{24,0},{1,25},{9,17},{17,9},{25,1},{2,26},{10... | collective-permute-start | bytes 20744 | tf_op jit(solution)/shard_map/ppermute | solution.py:918
  20.9 1.3 collective-permute-start.1
  22.2 4.6 %collective-permute-start = (bf16[192,1152]{1,0:T(8,128)(2,1)S(1)}, bf16[192,1152]{1,0:T(8,128)(2,1)S(1)}, u32[]{:S(2)}, u32[]{:S(2)}) collective-permute-start(bf16[192,1152]{1,0:T(8,128)(2,1)S(1)} %constant_dynamic-slice_fusion.1), channel_id=1, source_target_pairs={{0,2},{2,4},{4,6},{1,3},{3,5},{5,7},{8,10},{10,12},{12,14},{9,11},... | collective-permute-start | bytes 1327112 | tf_op jit(solution)/shard_map/ppermute | solution.py:928
  28.4 5.6 %fusion.2 = f32[15,6,576]{2,0,1:T(8,128)S(1)} fusion(bf16[1152,6,576]{0,2,1:T(8,128)(2,1)} %param.28, bf16[15,1152]{1,0:T(8,128)(2,1)S(1)} %concatenate.16), kind=kOutput, calls=%fused_computation.2 | convolution fusion | flops 119439360 | bytes 8204544 | tf_op jit(solution)/shard_map/sd,gfd->sgf/dot_general | solution.py:1055
  36.2 1.5 collective-permute-done.6.other_ref
  38.8 2.1 norm.1
  40.9 1.2 copy-done.6
  42.1 4.4 %fusion.8.refs_1_ = bf16[3,768,576]{2,1,0:T(8,128)(2,1)S(1)} fusion(f32[3,576]{1,0:T(4,128)S(1)} %pad_maximum_fusion.2, bf16[768,1152]{1,0:T(8,128)(2,1)S(1)} %get-tuple-element.141.refs_1_, bf16[1152,3,576]{0,2,1:T(8,128)(2,1)S(1)} %copy-done.45), kind=kOutput, calls=%fused_computation.11 | convolution fusion | flops 3060301824 | bytes 8411904 | tf_op jit(solution)/shard_map/td,gfd->gtf/dot_general | solution.py:1069
  46.5 9.7 %attend.1 = (bf16[384,576]{1,0:T(8,128)(2,1)S(1)}, f32[384,1152]{1,0:T(8,128)S(1)}) custom-call(s32[23]{0:T(128)S(1)} %plan.1.refs_0_.scalars, bf16[3,768,576]{2,1,0:T(8,128)(2,1)S(1)} %fusion.8.refs_1_, bf16[576,1152]{1,0:T(8,128)(2,1)} %rest_0_.3), custom_call_target="tpu_custom_call" | custom-call | flops 962592 | bytes 6193 | tf_op jit(solution)/shard_map/attend/pallas_call | solution.py:50
  57.3 3.7 %collective-permute-done.7.other_ref = f32[384,1152]{1,0:T(8,128)S(1)} collective-permute-done((f32[384,1152]{1,0:T(8,128)S(1)}, f32[384,1152]{1,0:T(8,128)S(1)}, u32[]{:S(2)}, u32[]{:S(2)}) %collective-permute-start.7) | collective-permute-done | bytes 1769504 | tf_op jit(solution)/shard_map/ppermute | solution.py:918
  61.0 1.2 copy-done.46
  62.2 10.7 %feed_up.1 = (f32[384,1152]{1,0:T(8,128)S(1)}, bf16[384,1152]{1,0:T(8,128)(2,1)}, bf16[384,640]{1,0:T(8,128)(2,1)}, f32[384,2304]{1,0:T(8,128)}, bf16[384,2304]{...) custom-call(s32[23]{0:T(128)S(1)} %plan.1.refs_0_.scalars, ...), custom_call_target="tpu_custom_call" | custom-call | flops 2038431 | bytes 20249 | tf_op jit(solution)/shard_map/feed_up/pallas_call | solution.py:50
  72.9 1.2 copy-done.1
  76.6 1.5 collective-permute-start.8
  78.1 1.5 collective-permute-start.9
  79.5 10.6 %feed_back.1 = (f32[384,1152]{1,0:T(8,128)}, f32[1,2304]{1,0:T(1,128)S(1)}, bf16[384,640]{1,0:T(8,128)(2,1)S(1)}, bf16[384,640]{1,0:T(8,128)(2,1)}, bf16[384,640]{1,0:T(8,128)(2,1)}, /*index=5*/bf16[384,640]{1,0:T(8,128)(2,1)}) custom-call(s32[23]{0:T(128)S(1)} %plan.1.refs_0_.scalars, bf16[384,1152]{1,0:T(8,128)(2,1)S(1)} %get-tuple-element.142.down_in_ref.refs_1_, ...), custom_call_target="tpu_custom_call" | custom-call | flops 4076863 | bytes 18785 | tf_op jit(solution)/shard_map/feed_back/pallas_call | solution.py:50
  91.0 1.3 collective-permute-done.9.refs_5_
  93.5 7.9 %others.1 = (bf16[1152,1152]{1,0:T(8,128)(2,1)}, bf16[1152,1152]{1,0:T(8,128)(2,1)}) custom-call(s32[23]{0:T(128)} %copy-done.33, bf16[3072,1152]{1,0:T(8,128)(2,1)} %all-gather.4.cloned.1.call-done.refs_1_, f32[15,6,1152]{2,1,0:T(8,128)} %copy-done.2), custom_call_target="tpu_custom_call" | custom-call | tf_op jit(solution)/shard_map/others/pallas_call | solution.py:224
  101.5 6.5 %middle_back.1 = (f32[384,1152]{1,0:T(8,128)S(1)}, bf16[384,1152]{1,0:T(8,128)(2,1)S(1)}, bf16[384,576]{1,0:T(8,128)(2,1)}, f32[3,3,1152]{2,1,0:T(4,128)S(1)}, f32[3,1,1152]{2,1,0:T(1,128)S(1)}) custom-call(f32[384,1152]{1,0:T(8,128)} %get-tuple-element.154.term_ref, f32[384,1152]{1,0:T(8,128)} %collective-permute-done.10.other_ref, f32[384,1152]{1,0:T(8,128)} %copy-done.1, ...), custom_call_target="tpu_custom_call" | custom-call | flops 509607 | bytes 11639 | tf_op jit(solution)/shard_map/middle_back/pallas_call | solution.py:50
  108.0 1.2 copy-done.3
  109.2 1.7 collective-permute-start.12
  110.9 10.7 %collective-permute-start.11 = (bf16[384,576]{1,0:T(8,128)(2,1)}, bf16[384,576]{1,0:T(8,128)(2,1)}, u32[]{:S(2)}, u32[]{:S(2)}) collective-permute-start(bf16[384,576]{1,0:T(8,128)(2,1)} %get-tuple-element.167.refs_2_), channel_id=1, source_target_pairs={{0,2},{2,4},{4,6},{1,3},{3,5},{5,7},{8,10},{10,12},{12,14},{9,11},... | collective-permute-start | bytes 1327112 | tf_op jit(solution)/shard_map/ppermute | solution.py:928
  122.8 2.3 collective-permute-start.15
  125.1 2.5 own_weight_grad.1
  128.3 6.0 %weight_grad.3 = bf16[1152,640]{1,0:T(8,128)(2,1)} custom-call(s32[23]{0:T(128)S(1)} %copy-done.34, bf16[384,1152]{1,0:T(8,128)(2,1)S(1)} %get-tuple-element.142.down_in_ref.refs_1_, bf16[1152,1152]{1,0:T(8,128)(2,1)} %get-tuple-element.168.refs_2_, bf16[384,640]{1,0:T(8,128)(2,1)S(1)} %copy-done.15, bf16[384,640]{1,0:T(8,128)(2,1)S(1)} %copy-done.17, ...), custom_call_target="tpu_custom_call" | custom-call | flops 2264924 | bytes 6979 | tf_op jit(solution)/shard_map/weight_grad/pallas_call | solution.py:50
  136.5 1.5 collective-permute-start.18
  138.1 1.7 collective-permute-start.16
  140.1 13.2 %attend_back.1 = (bf16[384,1152]{1,0:T(8,128)(2,1)S(1)}, f32[2,576]{1,0:T(2,128)S(1)}, bf16[384,432]{1,0:T(8,128)(2,1)S(1)}, bf16[384,432]{1,0:T(8,128)(2,1)}, b...) custom-call(s32[23]{0:T(128)S(1)} %copy-done.34, bf16[3,768,576]{2,1,0:T(8,128)(2,1)} %copy-done, ...), custom_call_target="tpu_custom_call" | custom-call | flops 3038773 | bytes 9736 | tf_op jit(solution)/shard_map/attend_back/pallas_call | solution.py:50
  155.6 1.5 collective-permute-done.16.refs_8_
  159.4 1.4 collective-permute-start.20
  160.8 1.2 collective-permute-start.21
  164.1 6.6 %weight_grad.4 = bf16[1152,640]{1,0:T(8,128)(2,1)} custom-call(s32[23]{0:T(128)S(1)} %copy-done.34, bf16[3072,640]{1,0:T(8,128)(2,1)} %all-gather.6.cloned.1.call-done.refs_1_, bf16[384,640]{1,0:T(8,128)(2,1)S(1)} %copy-done.9, bf16[384,640]{1,0:T(8,128)(2,1)} %collective-permute-done.14.refs_3_, bf16[384,640]{1,0:T(8,128)(2,1)} %collective-permute-done.15.refs_4_, ...), custom_call_target="tpu_custom_call" | custom-call | flops 2264924 | bytes 7372 | tf_op jit(solution)/shard_map/weight_grad/pallas_call | solution.py:50
  170.7 6.8 %collective-permute-done.20.refs_4_ = bf16[384,432]{1,0:T(8,128)(2,1)S(1)} collective-permute-done((bf16[384,432]{1,0:T(8,128)(2,1)}, bf16[384,432]{1,0:T(8,128)(2,1)S(1)}, u32[]{:S(2)}, u32[]{:S(2)}) %collective-permute-start.20) | collective-permute-done | bytes 331808 | tf_op jit(solution)/shard_map/ppermute | solution.py:918
  178.4 5.5 %convolution_convert_fusion.2.term_ref = bf16[384,1152]{1,0:T(8,128)(2,1)S(1)} fusion(bf16[384,2304]{1,0:T(8,128)(2,1)} %get-tuple-element.211, bf16[2304,1152]{1,0:T(8,128)(2,1)} %down_ref.1), kind=kOutput, calls=%fused_computation.12 | convolution fusion | flops 2038874112 | bytes 7962624 | tf_op jit(solution)/shard_map/dot_general | solution.py:28
  184.8 3.0 %input_back.1 = (bf16[384,1152]{1,0:T(8,128)(2,1)S(1)}, f32[3,2,1152]{2,1,0:T(2,128)S(1)}) custom-call(bf16[384,1152]{1,0:T(8,128)(2,1)S(1)} %get-tuple-element.194.term_ref, bf16[384,1152]{1,0:T(8,128)(2,1)} %collective-permute-done.19.other_ref, f32[384,1152]{1,0:T(8,128)S(1)} %copy-done.4, ...), custom_call_target="tpu_custom_call" | custom-call | bytes 5419 | tf_op jit(solution)/shard_map/input_back/pallas_call | solution.py:50
  188.8 3.0 result.1
  192.4 4.0 %collective-permute-done.23.refs_6_ = bf16[384,432]{1,0:T(8,128)(2,1)S(1)} collective-permute-done((bf16[384,432]{1,0:T(8,128)(2,1)S(1)}, bf16[384,432]{1,0:T(8,128)(2,1)S(1)}, u32[]{:S(2)}, u32[]{:S(2)}) %collective-permute-start.23) | collective-permute-done | bytes 331808 | tf_op jit(solution)/shard_map/ppermute | solution.py:918
  196.4 4.9 %collective-permute-start.27 = (bf16[48,576]{1,0:T(8,128)(2,1)S(1)}, bf16[48,576]{1,0:T(8,128)(2,1)S(1)}, u32[]{:S(2)}, u32[]{:S(2)}) collective-permute-start(bf16[48,576]{1,0:T(8,128)(2,1)S(1)} %collect.1), channel_id=1, source_target_pairs={{0,6},{2,4},{4,2},{6,0},{1,7},{3,5},{5,3},{7,1},{8,14},{10,12},{12... | collective-permute-start | bytes 165896 | tf_op jit(solution)/shard_map/ppermute | solution.py:918
  201.2 3.9 %collective-permute-start.26 = (bf16[48,576]{1,0:T(8,128)(2,1)S(1)}, bf16[48,576]{1,0:T(8,128)(2,1)S(1)}, u32[]{:S(2)}, u32[]{:S(2)}) collective-permute-start(bf16[48,576]{1,0:T(8,128)(2,1)S(1)} %collect.1), channel_id=1, source_target_pairs={{0,4},{2,6},{4,0},{6,2},{1,5},{3,7},{5,1},{7,3},{8,12},{10,14},{12... | collective-permute-start | bytes 165896 | tf_op jit(solution)/shard_map/ppermute | solution.py:918
  205.4 5.7 %weight_grad.5 = (f32[288,576]{1,0:T(8,128)S(1)}, bf16[288,576]{1,0:T(8,128)(2,1)}, bf16[288,576]{1,0:T(8,128)(2,1)S(1)}, bf16[288,576]{1,0:T(8,128)(2,1)S(1)}) custom-call(s32[23]{0:T(128)S(1)} %copy-done.34, bf16[768,1152]{1,0:T(8,128)(2,1)} %copy-done.6, bf16[1152,1152]{1,0:T(8,128)(2,1)} %get-tuple-element.157.refs_2_, bf16[384,432]{1,0:T(8,128)(2,1)S(1)} %copy-done.21, ...), custom_call_target="tpu_custom_call" | custom-call | flops 1528823 | bytes 8736 | tf_op jit(solution)/shard_map/weight_grad/pallas_call | solution.py:50
  211.1 2.5 collective-permute-done.26
  213.6 2.4 collective-permute-start.33
  217.2 2.4 collective-permute-start.36
  219.6 3.8 %collective-permute-done.33.refs_5_ = bf16[192,576]{1,0:T(8,128)(2,1)S(1)} collective-permute-done((bf16[192,576]{1,0:T(8,128)(2,1)S(1)}, bf16[192,576]{1,0:T(8,128)(2,1)S(1)}, u32[]{:S(2)}, u32[]{:S(2)}) %collective-permute-start.33) | collective-permute-done | bytes 221216 | tf_op jit(solution)/shard_map/ppermute | solution.py:918
  223.5 1.5 collective-permute-start.35
  224.9 3.9 %collective-permute-done.32.refs_4_ = bf16[192,576]{1,0:T(8,128)(2,1)S(1)} collective-permute-done((bf16[192,576]{1,0:T(8,128)(2,1)S(1)}, bf16[192,576]{1,0:T(8,128)(2,1)S(1)}, u32[]{:S(2)}, u32[]{:S(2)}) %collective-permute-start.32) | collective-permute-done | bytes 221216 | tf_op jit(solution)/shard_map/ppermute | solution.py:918
  229.5 1.5 collective-permute-start.34
  231.0 2.0 collective-permute-start.29
  233.0 2.1 collective-permute-start.30
  235.1 4.3 %fusion.7 = bf16[1,768,1152]{2,1,0:T(8,128)(2,1)} fusion(bf16[384,1152]{1,0:T(8,128)(2,1)} %copy-done.39, bf16[1,768,1152]{2,1,0:T(8,128)(2,1)} %param.15, pred[768]{0:T(1024)(128)(4,1)S(1)} %broadcast_compare_fusion, s32[384]{0:T(512)S(1)} %subtract_reduce_fusion), kind=kOutput, calls=%fused_computation.10 | convolution fusion | flops 681541632 | bytes 4425984 | tf_op jit(solution)/shard_map/dot_general | solution.py:32
  239.4 2.7 fusion.6
  242.2 9.2 %collective-permute-done.29 = bf16[288,576]{1,0:T(8,128)(2,1)S(1)} collective-permute-done((bf16[288,576]{1,0:T(8,128)(2,1)}, bf16[288,576]{1,0:T(8,128)(2,1)S(1)}, u32[]{:S(2)}, u32[]{:S(2)}) %collective-permute-start.29) | collective-permute-done | bytes 331808 | tf_op jit(solution)/shard_map/ppermute | solution.py:973
  252.1 1.4 add_convert_fusion.1.refs_1_
  253.6 2.0 collective-permute-start.40
  256.1 1.4 collective-permute-start.38
  258.5 3.9 %spread.1 = (f32[6,288,576]{2,1,0:T(8,128)}, f32[6,576]{1,0:T(8,128)}, f32[24,576]{1,0:T(8,128)S(1)}, f32[9,6,576]{2,1,0:T(8,128)S(1)}) custom-call(s32[23]{0:T(128)S(1)} %copy-done.34, s32[1536]{0:T(1024)S(1)} %reduce.refs_1_, bf16[192,576]{1,0:T(8,128)(2,1)S(1)} %constant_dynamic-update-slice_fusion.refs_2_, bf16[192,576]{1,0:T(8,128)(2,1)S(1)} %copy-done.32, ...), custom_call_target="tpu_custom_call" | custom-call | bytes 5065 | tf_op jit(solution)/shard_map/spread/pallas_call | solution.py:50
  262.5 4.5 %fusion.9 = f32[18,1152]{1,0:T(8,128)S(1)} fusion(bf16[1152,6,576]{0,2,1:T(8,128)(2,1)} %param.28, bf16[18,6,576]{2,1,0:T(8,128)(2,1)S(1)} %pad_maximum_fusion.1), kind=kOutput, calls=%fused_computation.15 | convolution fusion | flops 143327232 | bytes 8169984 | tf_op jit(solution)/shard_map/sgf,gfd->sd/dot_general | solution.py:1219
  269.9 2.3 join_down.1
  274.0 2.7 join_qkv.1
  276.7 10.1 %all-gather.8.cloned.1.call-done.refs_1_ = bf16[1152,640]{1,0:T(8,128)(2,1)} async-done(((bf16[288,640]{1,0:T(8,128)(2,1)}), bf16[1152,640]{1,0:T(8,128)(2,1)}) %all-gather.8.cloned.1.call-update) | async-done | bytes 1474576 | tf_op jit(solution)/shard_map/all_gather | solution.py:1196
  286.8 1.4 copy-done.7
  288.2 2.2 join_hidden.1
  (219 shorter events, 38.8 us)
Async XLA Ops:
  7.2 86.4 %all-gather.4.cloned.1.call-start = ((), (), s32[]{:S(2)}) async-start(), calls=%async_computation.2 | async-start | bytes 7962624 | tf_op jit(solution)/shard_map/all_gather | solution.py:959
  10.0 69.5 %copy-start.33 = (s32[23]{0:T(128)}, s32[23]{0:T(128)S(1)}, u32[]{:S(2)}) copy-start(s32[23]{0:T(128)S(1)} %plan.1.refs_0_.scalars) | copy-start | bytes 280
  16.3 145.7 %all-gather.6.cloned.1.call-start = ((), (), s32[]{:S(2)}) async-start(), calls=%async_computation.3 | async-start | bytes 4423680 | tf_op jit(solution)/shard_map/all_gather | solution.py:959
  16.3 11.8 %collective-permute-start.5 = (bf16[3,1152]{1,0:T(4,128)(2,1)S(1)}, bf16[3,1152]{1,0:T(4,128)(2,1)S(1)}, u32[]{:S(2)}, u32[]{:S(2)}) collective-permute-start(bf16[3,1152]{1,0:T(4,128)(2,1)S(1)} %get-tuple-element.139.active_ref), channel_id=1, source_target_pairs={{0,24},{8,16},{16,8},{24,0},{1,25},{9,17},{17,9},{25,1},{2,26},{10... | collective-permute-start | bytes 20744 | tf_op jit(solution)/shard_map/ppermute | solution.py:918
  20.3 7.9 %collective-permute-start.4 = (bf16[3,1152]{1,0:T(4,128)(2,1)S(1)}, bf16[3,1152]{1,0:T(4,128)(2,1)S(1)}, u32[]{:S(2)}, u32[]{:S(2)}) collective-permute-start(bf16[3,1152]{1,0:T(4,128)(2,1)S(1)} %get-tuple-element.139.active_ref), channel_id=1, source_target_pairs={{0,16},{8,24},{16,0},{24,8},{1,17},{9,25},{17,1},{25,9},{2,18},{10... | collective-permute-start | bytes 20744 | tf_op jit(solution)/shard_map/ppermute | solution.py:918
  20.8 7.4 %collective-permute-start.3 = (bf16[3,1152]{1,0:T(4,128)(2,1)S(1)}, bf16[3,1152]{1,0:T(4,128)(2,1)S(1)}, u32[]{:S(2)}, u32[]{:S(2)}) collective-permute-start(bf16[3,1152]{1,0:T(4,128)(2,1)S(1)} %get-tuple-element.139.active_ref), channel_id=1, source_target_pairs={{0,8},{8,0},{16,24},{24,16},{1,9},{9,1},{17,25},{25,17},{2,10},{10... | collective-permute-start | bytes 20744 | tf_op jit(solution)/shard_map/ppermute | solution.py:918
  20.9 13.2 %collective-permute-start.1 = (bf16[192,1152]{1,0:T(8,128)(2,1)S(1)}, bf16[192,1152]{1,0:T(8,128)(2,1)S(1)}, u32[]{:S(2)}, u32[]{:S(2)}) collective-permute-start(bf16[192,1152]{1,0:T(8,128)(2,1)S(1)} %constant_dynamic-slice_fusion.1), channel_id=1, source_target_pairs={{2,0},{4,2},{6,4},{3,1},{5,3},{7,5},{10,8},{12,10},{14,12},{11,9},... | collective-permute-start | bytes 1327112 | tf_op jit(solution)/shard_map/ppermute | solution.py:928
  22.2 13.1 %collective-permute-start = (bf16[192,1152]{1,0:T(8,128)(2,1)S(1)}, bf16[192,1152]{1,0:T(8,128)(2,1)S(1)}, u32[]{:S(2)}, u32[]{:S(2)}) collective-permute-start(bf16[192,1152]{1,0:T(8,128)(2,1)S(1)} %constant_dynamic-slice_fusion.1), channel_id=1, source_target_pairs={{0,2},{2,4},{4,6},{1,3},{3,5},{5,7},{8,10},{10,12},{12,14},{9,11},... | collective-permute-start | bytes 1327112 | tf_op jit(solution)/shard_map/ppermute | solution.py:928
  35.4 3.2 %collective-permute-start.2 = (bf16[192,1152]{1,0:T(8,128)(2,1)S(1)}, bf16[192,1152]{1,0:T(8,128)(2,1)S(1)}, u32[]{:S(2)}, u32[]{:S(2)}) collective-permute-start(bf16[192,1152]{1,0:T(8,128)(2,1)S(1)} %broadcast_select_fusion.1), channel_id=1, source_target_pairs={{0,1},{1,0},{2,3},{3,2},{4,5},{5,4},{6,7},{7,6},{8,9},{9,8},{10,11... | collective-permute-start | bytes 1327112 | tf_op jit(solution)/shard_map/ppermute | solution.py:918
  35.6 2.1 collective-permute-start.6
  38.6 18.7 %copy-start.2 = (f32[15,6,1152]{2,1,0:T(8,128)}, f32[15,6,1152]{2,1,0:T(8,128)S(1)}, u32[]{:S(2)}) copy-start(f32[15,6,1152]{2,1,0:T(8,128)S(1)} %pick.1.mod_ref.refs_2_) | copy-start | bytes 1244164
  57.1 3.9 %collective-permute-start.7 = (f32[384,1152]{1,0:T(8,128)S(1)}, f32[384,1152]{1,0:T(8,128)S(1)}, u32[]{:S(2)}, u32[]{:S(2)}) collective-permute-start(f32[384,1152]{1,0:T(8,128)S(1)} %get-tuple-element.143.term_ref), channel_id=1, source_target_pairs={{0,1},{1,0},{2,3},{3,2},{4,5},{5,4},{6,7},{7,6},{8,9},{9,8},{10,11... | collective-permute-start | bytes 5308424 | tf_op jit(solution)/shard_map/ppermute | solution.py:918
  76.5 137.0 %reduce-scatter.3.cloned.1.call-start = ((), (), s32[]{:S(2)}) async-start(), calls=%async_computation.4 | async-start | bytes 1843200 | tf_op jit(solution)/shard_map/reduce_scatter | solution.py:1125
  76.6 14.4 %collective-permute-start.8 = (bf16[384,640]{1,0:T(8,128)(2,1)}, bf16[384,640]{1,0:T(8,128)(2,1)S(1)}, u32[]{:S(2)}, u32[]{:S(2)}) collective-permute-start(bf16[384,640]{1,0:T(8,128)(2,1)} %copy-done.41), channel_id=1, source_target_pairs={{0,8},{8,0},{16,24},{24,16},{1,9},{9,1},{17,25},{25,17},{2,10},{10... | collective-permute-start | bytes 1474568 | tf_op jit(solution)/shard_map/ppermute | solution.py:918
  78.1 14.2 %collective-permute-start.9 = (bf16[384,640]{1,0:T(8,128)(2,1)}, bf16[384,640]{1,0:T(8,128)(2,1)S(1)}, u32[]{:S(2)}, u32[]{:S(2)}) collective-permute-start(bf16[384,640]{1,0:T(8,128)(2,1)} %copy-done.40), channel_id=1, source_target_pairs={{0,16},{8,24},{16,0},{24,8},{1,17},{9,25},{17,1},{25,9},{2,18},{10... | collective-permute-start | bytes 1474568 | tf_op jit(solution)/shard_map/ppermute | solution.py:918
  93.1 8.4 %collective-permute-start.10 = (f32[384,1152]{1,0:T(8,128)}, f32[384,1152]{1,0:T(8,128)}, u32[]{:S(2)}, u32[]{:S(2)}) collective-permute-start(f32[384,1152]{1,0:T(8,128)} %get-tuple-element.154.term_ref), channel_id=1, source_target_pairs={{0,1},{1,0},{2,3},{3,2},{4,5},{5,4},{6,7},{7,6},{8,9},{9,8},{10,11... | collective-permute-start | bytes 5308424 | tf_op jit(solution)/shard_map/ppermute | solution.py:918
  93.1 35.2 %collective-permute-start.13 = (bf16[384,640]{1,0:T(8,128)(2,1)}, bf16[384,640]{1,0:T(8,128)(2,1)}, u32[]{:S(2)}, u32[]{:S(2)}) collective-permute-start(bf16[384,640]{1,0:T(8,128)(2,1)} %get-tuple-element.172), channel_id=1, source_target_pairs={{0,24},{8,16},{16,8},{24,0},{1,25},{9,17},{17,9},{25,1},{2,26},{10... | collective-permute-start | bytes 1474568 | tf_op jit(solution)/shard_map/ppermute | solution.py:918
  101.5 23.6 %copy-start.11 = (bf16[384,576]{1,0:T(8,128)(2,1)S(1)}, bf16[384,576]{1,0:T(8,128)(2,1)}, u32[]{:S(2)}) copy-start(bf16[384,576]{1,0:T(8,128)(2,1)} %copy-done.10) | copy-start | bytes 1327108
  101.5 23.6 %copy-start.34 = (s32[23]{0:T(128)S(1)}, s32[23]{0:T(128)}, u32[]{:S(2)}) copy-start(s32[23]{0:T(128)} %copy-done.33) | copy-start | bytes 280
  101.5 26.8 %copy-start.15 = (bf16[384,640]{1,0:T(8,128)(2,1)S(1)}, bf16[384,640]{1,0:T(8,128)(2,1)}, u32[]{:S(2)}) copy-start(bf16[384,640]{1,0:T(8,128)(2,1)} %copy-done.14) | copy-start | bytes 1474564
  101.5 26.8 %copy-start.17 = (bf16[384,640]{1,0:T(8,128)(2,1)S(1)}, bf16[384,640]{1,0:T(8,128)(2,1)}, u32[]{:S(2)}) copy-start(bf16[384,640]{1,0:T(8,128)(2,1)} %copy-done.16) | copy-start | bytes 1474564
  101.5 26.8 %copy-start.19 = (bf16[384,640]{1,0:T(8,128)(2,1)S(1)}, bf16[384,640]{1,0:T(8,128)(2,1)}, u32[]{:S(2)}) copy-start(bf16[384,640]{1,0:T(8,128)(2,1)} %copy-done.18) | copy-start | bytes 1474564
  109.2 25.1 %collective-permute-start.12 = (bf16[384,576]{1,0:T(8,128)(2,1)}, bf16[384,576]{1,0:T(8,128)(2,1)}, u32[]{:S(2)}, u32[]{:S(2)}) collective-permute-start(bf16[384,576]{1,0:T(8,128)(2,1)} %get-tuple-element.167.refs_2_), channel_id=1, source_target_pairs={{2,0},{4,2},{6,4},{3,1},{5,3},{7,5},{10,8},{12,10},{14,12},{11,9},... | collective-permute-start | bytes 1327112 | tf_op jit(solution)/shard_map/ppermute | solution.py:928
  110.9 23.4 %collective-permute-start.11 = (bf16[384,576]{1,0:T(8,128)(2,1)}, bf16[384,576]{1,0:T(8,128)(2,1)}, u32[]{:S(2)}, u32[]{:S(2)}) collective-permute-start(bf16[384,576]{1,0:T(8,128)(2,1)} %get-tuple-element.167.refs_2_), channel_id=1, source_target_pairs={{0,2},{2,4},{4,6},{1,3},{3,5},{5,7},{8,10},{10,12},{12,14},{9,11},... | collective-permute-start | bytes 1327112 | tf_op jit(solution)/shard_map/ppermute | solution.py:928
  121.6 13.8 %collective-permute-start.14 = (bf16[384,640]{1,0:T(8,128)(2,1)}, bf16[384,640]{1,0:T(8,128)(2,1)}, u32[]{:S(2)}, u32[]{:S(2)}) collective-permute-start(bf16[384,640]{1,0:T(8,128)(2,1)} %get-tuple-element.179), channel_id=1, source_target_pairs={{0,8},{8,0},{16,24},{24,16},{1,9},{9,1},{17,25},{25,17},{2,10},{10... | collective-permute-start | bytes 1474568 | tf_op jit(solution)/shard_map/ppermute | solution.py:918
  122.8 13.7 %collective-permute-start.15 = (bf16[384,640]{1,0:T(8,128)(2,1)}, bf16[384,640]{1,0:T(8,128)(2,1)}, u32[]{:S(2)}, u32[]{:S(2)}) collective-permute-start(bf16[384,640]{1,0:T(8,128)(2,1)} %get-tuple-element.180), channel_id=1, source_target_pairs={{0,16},{8,24},{16,0},{24,8},{1,17},{9,25},{17,1},{25,9},{2,18},{10... | collective-permute-start | bytes 1474568 | tf_op jit(solution)/shard_map/ppermute | solution.py:918
  136.5 105.6 %reduce-scatter.5.cloned.1.call-start = ((), (), s32[]{:S(2)}) async-start(), calls=%async_computation.5 | async-start | bytes 1843200 | tf_op jit(solution)/shard_map/reduce_scatter | solution.py:1139
  136.5 18.3 %collective-permute-start.18 = (bf16[384,640]{1,0:T(8,128)(2,1)}, bf16[384,640]{1,0:T(8,128)(2,1)S(1)}, u32[]{:S(2)}, u32[]{:S(2)}) collective-permute-start(bf16[384,640]{1,0:T(8,128)(2,1)} %get-tuple-element.192), channel_id=1, source_target_pairs={{0,24},{8,16},{16,8},{24,0},{1,25},{9,17},{17,9},{25,1},{2,26},{10... | collective-permute-start | bytes 1474568 | tf_op jit(solution)/shard_map/ppermute | solution.py:918
  138.1 19.0 %collective-permute-start.16 = (bf16[144,1152]{1,0:T(8,128)(2,1)}, bf16[144,1152]{1,0:T(8,128)(2,1)S(1)}, u32[]{:S(2)}, u32[]{:S(2)}) collective-permute-start(bf16[144,1152]{1,0:T(8,128)(2,1)} %get-tuple-element.187), channel_id=1, source_target_pairs={{0,8},{8,0},{16,24},{24,16},{1,9},{9,1},{17,25},{25,17},{2,10},{10... | collective-permute-start | bytes 995336 | tf_op jit(solution)/shard_map/ppermute | solution.py:918
  139.8 18.0 %collective-permute-start.17 = (bf16[144,1152]{1,0:T(8,128)(2,1)}, bf16[144,1152]{1,0:T(8,128)(2,1)S(1)}, u32[]{:S(2)}, u32[]{:S(2)}) collective-permute-start(bf16[144,1152]{1,0:T(8,128)(2,1)} %get-tuple-element.188), channel_id=1, source_target_pairs={{0,16},{8,24},{16,0},{24,8},{1,17},{9,25},{17,1},{25,9},{2,18},{10... | collective-permute-start | bytes 995336 | tf_op jit(solution)/shard_map/ppermute | solution.py:918
  158.5 19.9 %collective-permute-start.19 = (bf16[384,1152]{1,0:T(8,128)(2,1)S(1)}, bf16[384,1152]{1,0:T(8,128)(2,1)}, u32[]{:S(2)}, u32[]{:S(2)}) collective-permute-start(bf16[384,1152]{1,0:T(8,128)(2,1)S(1)} %get-tuple-element.194.term_ref), channel_id=1, source_target_pairs={{0,1},{1,0},{2,3},{3,2},{4,5},{5,4},{6,7},{7,6},{8,9},{9,8},{10,11... | collective-permute-start | bytes 2654216 | tf_op jit(solution)/shard_map/ppermute | solution.py:918
  158.5 12.2 %collective-permute-start.22 = (bf16[144,1152]{1,0:T(8,128)(2,1)}, bf16[144,1152]{1,0:T(8,128)(2,1)}, u32[]{:S(2)}, u32[]{:S(2)}) collective-permute-start(bf16[144,1152]{1,0:T(8,128)(2,1)} %get-tuple-element.197), channel_id=1, source_target_pairs={{0,24},{8,16},{16,8},{24,0},{1,25},{9,17},{17,9},{25,1},{2,26},{10... | collective-permute-start | bytes 995336 | tf_op jit(solution)/shard_map/ppermute | solution.py:918
  159.4 18.1 %collective-permute-start.20 = (bf16[384,432]{1,0:T(8,128)(2,1)}, bf16[384,432]{1,0:T(8,128)(2,1)S(1)}, u32[]{:S(2)}, u32[]{:S(2)}) collective-permute-start(bf16[384,432]{1,0:T(8,128)(2,1)} %get-tuple-element.195), channel_id=1, source_target_pairs={{0,8},{8,0},{16,24},{24,16},{1,9},{9,1},{17,25},{25,17},{2,10},{10... | collective-permute-start | bytes 995336 | tf_op jit(solution)/shard_map/ppermute | solution.py:918
  160.8 17.5 %collective-permute-start.21 = (bf16[384,432]{1,0:T(8,128)(2,1)}, bf16[384,432]{1,0:T(8,128)(2,1)}, u32[]{:S(2)}, u32[]{:S(2)}) collective-permute-start(bf16[384,432]{1,0:T(8,128)(2,1)} %get-tuple-element.196), channel_id=1, source_target_pairs={{0,16},{8,24},{16,0},{24,8},{1,17},{9,25},{17,1},{25,9},{2,18},{10... | collective-permute-start | bytes 995336 | tf_op jit(solution)/shard_map/ppermute | solution.py:918
  170.6 14.1 %copy-start.52 = (bf16[1152]{0:T(1024)(128)(2,1)S(1)}, bf16[1152]{0:T(1024)(128)(2,1)}, u32[]{:S(2)}) copy-start(bf16[1152]{0:T(1024)(128)(2,1)} %param.27) | copy-start | bytes 6916
  170.7 116.1 %all-gather.8.cloned.1.call-start = ((), (), s32[]{:S(2)}) async-start(), calls=%async_computation.6 | async-start | bytes 1843200 | tf_op jit(solution)/shard_map/all_gather | solution.py:1196
  170.7 13.2 %copy-start.43 = (bf16[384,432]{1,0:T(8,128)(2,1)S(1)}, bf16[384,432]{1,0:T(8,128)(2,1)}, u32[]{:S(2)}) copy-start(bf16[384,432]{1,0:T(8,128)(2,1)} %copy-done.42) | copy-start | bytes 995332
  170.7 14.0 %copy-start.4 = (f32[384,1152]{1,0:T(8,128)S(1)}, f32[384,1152]{1,0:T(8,128)}, u32[]{:S(2)}) copy-start(f32[384,1152]{1,0:T(8,128)} %copy-done.3) | copy-start | bytes 5308420
  183.9 4.9 %collective-permute-start.24 = (bf16[384,1152]{1,0:T(8,128)(2,1)S(1)}, bf16[384,1152]{1,0:T(8,128)(2,1)S(1)}, u32[]{:S(2)}, u32[]{:S(2)}) collective-permute-start(bf16[384,1152]{1,0:T(8,128)(2,1)S(1)} %convolution_convert_fusion.2.term_ref), channel_id=1, source_target_pairs={{0,1},{1,0},{2,3},{3,2},{4,5},{5,4},{6,7},{7,6},{8,9},{9,8},{10,11... | collective-permute-start | bytes 2654216 | tf_op jit(solution)/shard_map/ppermute | solution.py:918
  184.0 12.4 %collective-permute-start.23 = (bf16[384,432]{1,0:T(8,128)(2,1)S(1)}, bf16[384,432]{1,0:T(8,128)(2,1)S(1)}, u32[]{:S(2)}, u32[]{:S(2)}) collective-permute-start(bf16[384,432]{1,0:T(8,128)(2,1)S(1)} %copy-done.43), channel_id=1, source_target_pairs={{0,24},{8,16},{16,8},{24,0},{1,25},{9,17},{17,9},{25,1},{2,26},{10... | collective-permute-start | bytes 995336 | tf_op jit(solution)/shard_map/ppermute | solution.py:918
  188.7 16.6 %copy-start.21 = (bf16[384,432]{1,0:T(8,128)(2,1)S(1)}, bf16[384,432]{1,0:T(8,128)(2,1)}, u32[]{:S(2)}) copy-start(bf16[384,432]{1,0:T(8,128)(2,1)} %copy-done.20) | copy-start | bytes 995332
  188.7 16.6 %copy-start.24 = (bf16[144,1152]{1,0:T(8,128)(2,1)S(1)}, bf16[144,1152]{1,0:T(8,128)(2,1)}, u32[]{:S(2)}) copy-start(bf16[144,1152]{1,0:T(8,128)(2,1)} %copy-done.23) | copy-start | bytes 995332
  188.7 16.6 %copy-start.26 = (bf16[144,1152]{1,0:T(8,128)(2,1)S(1)}, bf16[144,1152]{1,0:T(8,128)(2,1)}, u32[]{:S(2)}) copy-start(bf16[144,1152]{1,0:T(8,128)(2,1)} %copy-done.25) | copy-start | bytes 995332
  188.7 16.6 %copy-start.28 = (bf16[144,1152]{1,0:T(8,128)(2,1)S(1)}, bf16[144,1152]{1,0:T(8,128)(2,1)}, u32[]{:S(2)}) copy-start(bf16[144,1152]{1,0:T(8,128)(2,1)} %copy-done.27) | copy-start | bytes 995332
  191.7 13.4 %copy-start.39 = (bf16[384,1152]{1,0:T(8,128)(2,1)}, bf16[384,1152]{1,0:T(8,128)(2,1)S(1)}, u32[]{:S(2)}) copy-start(bf16[384,1152]{1,0:T(8,128)(2,1)S(1)} %get-tuple-element.238) | copy-start | bytes 2654212
  196.4 14.7 %collective-permute-start.27 = (bf16[48,576]{1,0:T(8,128)(2,1)S(1)}, bf16[48,576]{1,0:T(8,128)(2,1)S(1)}, u32[]{:S(2)}, u32[]{:S(2)}) collective-permute-start(bf16[48,576]{1,0:T(8,128)(2,1)S(1)} %collect.1), channel_id=1, source_target_pairs={{0,6},{2,4},{4,2},{6,0},{1,7},{3,5},{5,3},{7,1},{8,14},{10,12},{12... | collective-permute-start | bytes 165896 | tf_op jit(solution)/shard_map/ppermute | solution.py:918
  201.2 12.3 %collective-permute-start.26 = (bf16[48,576]{1,0:T(8,128)(2,1)S(1)}, bf16[48,576]{1,0:T(8,128)(2,1)S(1)}, u32[]{:S(2)}, u32[]{:S(2)}) collective-permute-start(bf16[48,576]{1,0:T(8,128)(2,1)S(1)} %collect.1), channel_id=1, source_target_pairs={{0,4},{2,6},{4,0},{6,2},{1,5},{3,7},{5,1},{7,3},{8,12},{10,14},{12... | collective-permute-start | bytes 165896 | tf_op jit(solution)/shard_map/ppermute | solution.py:918
  205.1 8.4 %collective-permute-start.25 = (bf16[48,576]{1,0:T(8,128)(2,1)S(1)}, bf16[48,576]{1,0:T(8,128)(2,1)S(1)}, u32[]{:S(2)}, u32[]{:S(2)}) collective-permute-start(bf16[48,576]{1,0:T(8,128)(2,1)S(1)} %collect.1), channel_id=1, source_target_pairs={{0,2},{2,0},{4,6},{6,4},{1,3},{3,1},{5,7},{7,5},{8,10},{10,8},{12,... | collective-permute-start | bytes 165896 | tf_op jit(solution)/shard_map/ppermute | solution.py:918
  213.6 19.4 %collective-permute-start.28 = (bf16[288,576]{1,0:T(8,128)(2,1)}, bf16[288,576]{1,0:T(8,128)(2,1)}, u32[]{:S(2)}, u32[]{:S(2)}) collective-permute-start(bf16[288,576]{1,0:T(8,128)(2,1)} %get-tuple-element.231), channel_id=1, source_target_pairs={{0,2},{2,4},{4,6},{6,0},{1,3},{3,5},{5,7},{7,1},{8,10},{10,12},{12... | collective-permute-start | bytes 995336 | tf_op jit(solution)/shard_map/ppermute | solution.py:973
  213.6 9.8 %collective-permute-start.33 = (bf16[192,576]{1,0:T(8,128)(2,1)S(1)}, bf16[192,576]{1,0:T(8,128)(2,1)S(1)}, u32[]{:S(2)}, u32[]{:S(2)}) collective-permute-start(bf16[192,576]{1,0:T(8,128)(2,1)S(1)} %constant_dynamic-update-slice_fusion.refs_2_), channel_id=1, source_target_pairs={{0,24},{8,16},{16,8},{24,0},{1,25},{9,17},{17,9},{25,1},{2,26},{10... | collective-permute-start | bytes 663560 | tf_op jit(solution)/shard_map/ppermute | solution.py:918
  216.1 12.7 %collective-permute-start.32 = (bf16[192,576]{1,0:T(8,128)(2,1)S(1)}, bf16[192,576]{1,0:T(8,128)(2,1)S(1)}, u32[]{:S(2)}, u32[]{:S(2)}) collective-permute-start(bf16[192,576]{1,0:T(8,128)(2,1)S(1)} %constant_dynamic-update-slice_fusion.refs_2_), channel_id=1, source_target_pairs={{0,16},{8,24},{16,0},{24,8},{1,17},{9,25},{17,1},{25,9},{2,18},{10... | collective-permute-start | bytes 663560 | tf_op jit(solution)/shard_map/ppermute | solution.py:918
  216.6 14.3 %collective-permute-start.31 = (bf16[192,576]{1,0:T(8,128)(2,1)S(1)}, bf16[192,576]{1,0:T(8,128)(2,1)S(1)}, u32[]{:S(2)}, u32[]{:S(2)}) collective-permute-start(bf16[192,576]{1,0:T(8,128)(2,1)S(1)} %constant_dynamic-update-slice_fusion.refs_2_), channel_id=1, source_target_pairs={{0,8},{8,0},{16,24},{24,16},{1,9},{9,1},{17,25},{25,17},{2,10},{10... | collective-permute-start | bytes 663560 | tf_op jit(solution)/shard_map/ppermute | solution.py:918
  217.2 22.2 %copy-start.38 = (bf16[384,1152]{1,0:T(8,128)(2,1)S(1)}, bf16[384,1152]{1,0:T(8,128)(2,1)}, u32[]{:S(2)}) copy-start(bf16[384,1152]{1,0:T(8,128)(2,1)} %copy-done.37) | copy-start | bytes 2654212
  217.2 22.2 %copy-start.54 = (bf16[1,768,1152]{2,1,0:T(8,128)(2,1)S(1)}, bf16[1,768,1152]{2,1,0:T(8,128)(2,1)}, u32[]{:S(2)}) copy-start(bf16[1,768,1152]{2,1,0:T(8,128)(2,1)} %param.19) | copy-start | bytes 5308420
  217.2 34.2 %collective-permute-start.36 = (bf16[288,640]{1,0:T(8,128)(2,1)}, bf16[288,640]{1,0:T(8,128)(2,1)S(1)}, u32[]{:S(2)}, u32[]{:S(2)}) collective-permute-start(bf16[288,640]{1,0:T(8,128)(2,1)} %reduce-scatter.3.cloned.1.call-done.refs_1_), channel_id=1, source_target_pairs={{0,24},{8,16},{16,8},{24,0},{1,25},{9,17},{17,9},{25,1},{2,26},{10... | collective-permute-start | bytes 1105928 | tf_op jit(solution)/shard_map/ppermute | solution.py:918
  223.5 27.9 %collective-permute-start.35 = (bf16[288,640]{1,0:T(8,128)(2,1)}, bf16[288,640]{1,0:T(8,128)(2,1)S(1)}, u32[]{:S(2)}, u32[]{:S(2)}) collective-permute-start(bf16[288,640]{1,0:T(8,128)(2,1)} %reduce-scatter.3.cloned.1.call-done.refs_1_), channel_id=1, source_target_pairs={{0,16},{8,24},{16,0},{24,8},{1,17},{9,25},{17,1},{25,9},{2,18},{10... | collective-permute-start | bytes 1105928 | tf_op jit(solution)/shard_map/ppermute | solution.py:918
  229.5 22.6 %collective-permute-start.34 = (bf16[288,640]{1,0:T(8,128)(2,1)}, bf16[288,640]{1,0:T(8,128)(2,1)S(1)}, u32[]{:S(2)}, u32[]{:S(2)}) collective-permute-start(bf16[288,640]{1,0:T(8,128)(2,1)} %reduce-scatter.3.cloned.1.call-done.refs_1_), channel_id=1, source_target_pairs={{0,8},{8,0},{16,24},{24,16},{1,9},{9,1},{17,25},{25,17},{2,10},{10... | collective-permute-start | bytes 1105928 | tf_op jit(solution)/shard_map/ppermute | solution.py:918
  231.0 20.4 %collective-permute-start.29 = (bf16[288,576]{1,0:T(8,128)(2,1)}, bf16[288,576]{1,0:T(8,128)(2,1)S(1)}, u32[]{:S(2)}, u32[]{:S(2)}) collective-permute-start(bf16[288,576]{1,0:T(8,128)(2,1)} %copy-done.44), channel_id=1, source_target_pairs={{0,4},{2,6},{4,0},{6,2},{1,5},{3,7},{5,1},{7,3},{8,12},{10,14},{12... | collective-permute-start | bytes 995336 | tf_op jit(solution)/shard_map/ppermute | solution.py:973
  233.0 18.4 %collective-permute-start.30 = (bf16[288,576]{1,0:T(8,128)(2,1)S(1)}, bf16[288,576]{1,0:T(8,128)(2,1)}, u32[]{:S(2)}, u32[]{:S(2)}) collective-permute-start(bf16[288,576]{1,0:T(8,128)(2,1)S(1)} %get-tuple-element.233), channel_id=1, source_target_pairs={{0,6},{2,0},{4,2},{6,4},{1,7},{3,1},{5,3},{7,5},{8,14},{10,8},{12,... | collective-permute-start | bytes 995336 | tf_op jit(solution)/shard_map/ppermute | solution.py:973
  242.1 15.4 %copy-start.32 = (bf16[192,576]{1,0:T(8,128)(2,1)S(1)}, bf16[192,576]{1,0:T(8,128)(2,1)}, u32[]{:S(2)}) copy-start(bf16[192,576]{1,0:T(8,128)(2,1)} %copy-done.31) | copy-start | bytes 663556
  253.6 19.4 %collective-permute-start.40 = (bf16[288,576]{1,0:T(8,128)(2,1)S(1)}, bf16[288,576]{1,0:T(8,128)(2,1)S(1)}, u32[]{:S(2)}, u32[]{:S(2)}) collective-permute-start(bf16[288,576]{1,0:T(8,128)(2,1)S(1)} %add_convert_fusion.1.refs_1_), channel_id=1, source_target_pairs={{0,24},{8,16},{16,8},{24,0},{1,25},{9,17},{17,9},{25,1},{2,26},{10... | collective-permute-start | bytes 995336 | tf_op jit(solution)/shard_map/ppermute | solution.py:918
  255.6 18.4 %collective-permute-start.39 = (bf16[288,576]{1,0:T(8,128)(2,1)S(1)}, bf16[288,576]{1,0:T(8,128)(2,1)S(1)}, u32[]{:S(2)}, u32[]{:S(2)}) collective-permute-start(bf16[288,576]{1,0:T(8,128)(2,1)S(1)} %add_convert_fusion.1.refs_1_), channel_id=1, source_target_pairs={{0,16},{8,24},{16,0},{24,8},{1,17},{9,25},{17,1},{25,9},{2,18},{10... | collective-permute-start | bytes 995336 | tf_op jit(solution)/shard_map/ppermute | solution.py:918
  256.1 17.8 %collective-permute-start.38 = (bf16[288,576]{1,0:T(8,128)(2,1)S(1)}, bf16[288,576]{1,0:T(8,128)(2,1)S(1)}, u32[]{:S(2)}, u32[]{:S(2)}) collective-permute-start(bf16[288,576]{1,0:T(8,128)(2,1)S(1)} %add_convert_fusion.1.refs_1_), channel_id=1, source_target_pairs={{0,8},{8,0},{16,24},{24,16},{1,9},{9,1},{17,25},{25,17},{2,10},{10... | collective-permute-start | bytes 995336 | tf_op jit(solution)/shard_map/ppermute | solution.py:918
  267.0 5.2 %collective-permute-start.37 = (f32[9,1152]{1,0:T(8,128)S(1)}, f32[9,1152]{1,0:T(8,128)S(1)}, u32[]{:S(2)}, u32[]{:S(2)}) collective-permute-start(f32[9,1152]{1,0:T(8,128)S(1)} %slice_add_fusion), channel_id=1, source_target_pairs={{0,1},{1,0},{2,3},{3,2},{4,5},{5,4},{6,7},{7,6},{8,9},{9,8},{10,11... | collective-permute-start | bytes 124424 | tf_op jit(solution)/shard_map/ppermute | solution.py:918
  (37 other events, 117.6 us)
Sparse Core Ops, SparseCore 0:
  16.4 51.5 all-gather.3
  76.6 47.6 all-gather.5
  136.6 34.2 reduce-scatter.2
  173.8 39.3 reduce-scatter.4
  242.3 44.4 all-gather.7

commit v3 on v2

--- a/solution.py
+++ b/solution.py
@@ -1137,8 +1137,8 @@
     pre_all = by_entry(pre_pieces, pre_first, pre_last)
     hidden_raw = weight_grad(scalars, width, 0, [hidden_two_shares], pre_all)[0]
     hidden_reduced = lax.psum_scatter(hidden_raw, "blk", scatter_dimension=0, tiled=True)
-    hidden_other, qkv_first, output_last, hidden_raw, gelu = hold(
-        (swap(hidden_term), qkv_first, output_last, hidden_raw, gelu)
+    hidden_other, qkv_first, output_last, hidden_raw = hold(
+        (swap(hidden_term), qkv_first, output_last, hidden_raw)
     )
     input_grad, input_sums = input_back(
         hidden_term, hidden_other, middle_grad, kept_rows, mod_places

time: 302 us -> 305 us (level)
    ppermute x34, waiting for transfers between devices: 31.9 us -> 37.8 us  [xor_permute(): lax.ppermute(block, axis, [(i, i ^ bits) for i in range(lax.axis_size(axi...]
    ppermute x3, waiting for transfers between devices: 9.21 us -> 3.94 us  [send_blk(): found.append(lax.ppermute(pieces[step], 'blk', pairs))]
    ppermute x4, starting transfers between devices: 18.2 us -> 15 us  [move(): return lax.ppermute(block, 'blk', pairs)]
    unnamed x114 -> x124, local copies, waits for them, and re-layouts: 22.3 us -> 24.6 us
  transfers between devices with their start and end apart: 46 -> 46, of which waited for: 16 -> 13; matrix products, arithmetic and copies ran while one was open for 12% -> 11% of each run, Pallas kernels for 33% -> 33%
where the time goes in v3:
time: 305 us; the launch traced here: 301 us
  Pallas kernels  102 us (33%)
  starting transfers between devices  65.4 us (21%)
  waiting for transfers between devices  53.4 us (18%)
  matrix products  30.7 us (10%)
  local copies, waits for them, and re-layouts  27.7 us (9%)
  between operations  15.5 us (5%)
  other arithmetic  6.3 us (2%)
    pallas_call x20, Pallas kernels, kernel_call(): pl.pallas_call(body, name=name, out_shape=tuple(outs), grid=grid, in_spec...  94.4 us
    ppermute x34, starting transfers between devices, xor_permute(): lax.ppermute(block, axis, [(i, i ^ bits) for i in range(lax.axis_size(axi...  44.5 us
    ppermute x34, waiting for transfers between devices, xor_permute(): lax.ppermute(block, axis, [(i, i ^ bits) for i in range(lax.axis_size(axi...  37.8 us
    unnamed x124, local copies, waits for them, and re-layouts  24.6 us
    ppermute x4, starting transfers between devices, move(): return lax.ppermute(block, 'blk', pairs)  15 us
    all_gather x1, waiting for transfers between devices, local(): hidden_gathered = lax.all_gather(hidden_reduced, 'pack', axis=0, tiled=True)  10.1 us
    dot_general x3, matrix products, bf_dot(): return jnp.dot(operand_a, operand_b, preferred_element_type=F32)  9.26 us
    pallas_call x1, Pallas kernels, others(): pl.pallas_call(lambda *refs: others_body(first, count // SHORT, *refs), n...  7.84 us
  transfers between devices with their start and end apart: 46, of which 13 were waited for; matrix products, arithmetic and copies ran while one was open for 11% of the time, Pallas kernels for 33%

profile of v3, /device:TPU:0, one launch (start us, length us, event | category | flops | bytes accessed | tf_op | source)
XLA Modules:
  0.0 301.1 jit_solution(5803642798128167552)
XLA Ops:
  8.7 1.3 plan.1.refs_0_.scalars
  11.5 2.6 convolution_convert_fusion.4.own_ref.kept_ref
  16.3 4.0 %collective-permute-start.5 = (bf16[3,1152]{1,0:T(4,128)(2,1)S(1)}, bf16[3,1152]{1,0:T(4,128)(2,1)S(1)}, u32[]{:S(2)}, u32[]{:S(2)}) collective-permute-start(bf16[3,1152]{1,0:T(4,128)(2,1)S(1)} %get-tuple-element.138.active_ref), channel_id=1, source_target_pairs={{0,24},{8,16},{16,8},{24,0},{1,25},{9,17},{17,9},{25,1},{2,26},{10... | collective-permute-start | bytes 20744 | tf_op jit(solution)/shard_map/ppermute | solution.py:918
  20.9 1.3 collective-permute-start.1
  22.2 4.6 %collective-permute-start = (bf16[192,1152]{1,0:T(8,128)(2,1)S(1)}, bf16[192,1152]{1,0:T(8,128)(2,1)S(1)}, u32[]{:S(2)}, u32[]{:S(2)}) collective-permute-start(bf16[192,1152]{1,0:T(8,128)(2,1)S(1)} %constant_dynamic-slice_fusion.1), channel_id=1, source_target_pairs={{0,2},{2,4},{4,6},{1,3},{3,5},{5,7},{8,10},{10,12},{12,14},{9,11},... | collective-permute-start | bytes 1327112 | tf_op jit(solution)/shard_map/ppermute | solution.py:928
  28.4 5.6 %fusion.2 = f32[15,6,576]{2,0,1:T(8,128)S(1)} fusion(bf16[1152,6,576]{0,2,1:T(8,128)(2,1)} %param.28, bf16[15,1152]{1,0:T(8,128)(2,1)S(1)} %concatenate.16), kind=kOutput, calls=%fused_computation.2 | convolution fusion | flops 119439360 | bytes 8204544 | tf_op jit(solution)/shard_map/sd,gfd->sgf/dot_general | solution.py:1055
  34.2 1.2 collective-permute-done
  36.2 1.5 collective-permute-done.6.other_ref
  38.8 2.1 norm.1
  40.9 1.2 copy-done.6
  42.1 4.4 %fusion.8.refs_1_ = bf16[3,768,576]{2,1,0:T(8,128)(2,1)S(1)} fusion(f32[3,576]{1,0:T(4,128)S(1)} %pad_maximum_fusion.2, bf16[768,1152]{1,0:T(8,128)(2,1)S(1)} %get-tuple-element.140.refs_1_, bf16[1152,3,576]{0,2,1:T(8,128)(2,1)S(1)} %copy-done.50), kind=kOutput, calls=%fused_computation.11 | convolution fusion | flops 3060301824 | bytes 8411904 | tf_op jit(solution)/shard_map/td,gfd->gtf/dot_general | solution.py:1069
  46.6 9.7 %attend.1 = (bf16[384,576]{1,0:T(8,128)(2,1)S(1)}, f32[384,1152]{1,0:T(8,128)S(1)}) custom-call(s32[23]{0:T(128)S(1)} %plan.1.refs_0_.scalars, bf16[3,768,576]{2,1,0:T(8,128)(2,1)S(1)} %fusion.8.refs_1_, bf16[576,1152]{1,0:T(8,128)(2,1)} %rest_0_.3), custom_call_target="tpu_custom_call" | custom-call | flops 962592 | bytes 6193 | tf_op jit(solution)/shard_map/attend/pallas_call | solution.py:50
  57.3 3.7 %collective-permute-done.7.other_ref = f32[384,1152]{1,0:T(8,128)S(1)} collective-permute-done((f32[384,1152]{1,0:T(8,128)S(1)}, f32[384,1152]{1,0:T(8,128)S(1)}, u32[]{:S(2)}, u32[]{:S(2)}) %collective-permute-start.7) | collective-permute-done | bytes 1769504 | tf_op jit(solution)/shard_map/ppermute | solution.py:918
  61.0 1.2 copy-done.51
  62.2 10.7 %feed_up.1 = (f32[384,1152]{1,0:T(8,128)S(1)}, bf16[384,1152]{1,0:T(8,128)(2,1)}, bf16[384,640]{1,0:T(8,128)(2,1)}, f32[384,2304]{1,0:T(8,128)}, bf16[384,2304]{...) custom-call(s32[23]{0:T(128)S(1)} %plan.1.refs_0_.scalars, ...), custom_call_target="tpu_custom_call" | custom-call | flops 2038431 | bytes 20249 | tf_op jit(solution)/shard_map/feed_up/pallas_call | solution.py:50
  72.9 1.2 copy-done.1
  76.6 3.1 %collective-permute-start.8 = (bf16[384,640]{1,0:T(8,128)(2,1)}, bf16[384,640]{1,0:T(8,128)(2,1)S(1)}, u32[]{:S(2)}, u32[]{:S(2)}) collective-permute-start(bf16[384,640]{1,0:T(8,128)(2,1)} %copy-done.41), channel_id=1, source_target_pairs={{0,8},{8,0},{16,24},{24,16},{1,9},{9,1},{17,25},{25,17},{2,10},{10... | collective-permute-start | bytes 1474568 | tf_op jit(solution)/shard_map/ppermute | solution.py:918
  79.7 10.8 %feed_back.1 = (f32[384,1152]{1,0:T(8,128)}, f32[1,2304]{1,0:T(1,128)S(1)}, bf16[384,640]{1,0:T(8,128)(2,1)S(1)}, bf16[384,640]{1,0:T(8,128)(2,1)}, bf16[384,640]{1,0:T(8,128)(2,1)}, /*index=5*/bf16[384,640]{1,0:T(8,128)(2,1)}) custom-call(s32[23]{0:T(128)S(1)} %plan.1.refs_0_.scalars, bf16[384,1152]{1,0:T(8,128)(2,1)S(1)} %get-tuple-element.141.down_in_ref.refs_1_, ...), custom_call_target="tpu_custom_call" | custom-call | flops 4076863 | bytes 18785 | tf_op jit(solution)/shard_map/feed_back/pallas_call | solution.py:50
  91.3 3.7 %collective-permute-done.8.refs_4_ = bf16[384,640]{1,0:T(8,128)(2,1)S(1)} collective-permute-done((bf16[384,640]{1,0:T(8,128)(2,1)}, bf16[384,640]{1,0:T(8,128)(2,1)S(1)}, u32[]{:S(2)}, u32[]{:S(2)}) %collective-permute-start.8) | collective-permute-done | bytes 491552 | tf_op jit(solution)/shard_map/ppermute | solution.py:918
  95.0 2.2 collective-permute-done.9.refs_5_
  98.0 1.3 collective-permute-start.13
  99.3 7.8 %others.1 = (bf16[1152,1152]{1,0:T(8,128)(2,1)}, bf16[1152,1152]{1,0:T(8,128)(2,1)}) custom-call(s32[23]{0:T(128)} %copy-done.33, bf16[3072,1152]{1,0:T(8,128)(2,1)} %all-gather.4.cloned.1.call-done.refs_1_, f32[15,6,1152]{2,1,0:T(8,128)} %copy-done.2), custom_call_target="tpu_custom_call" | custom-call | tf_op jit(solution)/shard_map/others/pallas_call | solution.py:224
  107.2 6.5 %middle_back.1 = (f32[384,1152]{1,0:T(8,128)S(1)}, bf16[384,1152]{1,0:T(8,128)(2,1)S(1)}, bf16[384,576]{1,0:T(8,128)(2,1)}, f32[3,3,1152]{2,1,0:T(4,128)S(1)}, f32[3,1,1152]{2,1,0:T(1,128)S(1)}) custom-call(f32[384,1152]{1,0:T(8,128)} %get-tuple-element.153.term_ref, f32[384,1152]{1,0:T(8,128)} %collective-permute-done.10.other_ref, f32[384,1152]{1,0:T(8,128)} %copy-done.1, ...), custom_call_target="tpu_custom_call" | custom-call | flops 509607 | bytes 11639 | tf_op jit(solution)/shard_map/middle_back/pallas_call | solution.py:50
  113.7 1.2 copy-done.3
  114.9 1.7 collective-permute-start.12
  116.6 7.5 %collective-permute-start.11 = (bf16[384,576]{1,0:T(8,128)(2,1)}, bf16[384,576]{1,0:T(8,128)(2,1)}, u32[]{:S(2)}, u32[]{:S(2)}) collective-permute-start(bf16[384,576]{1,0:T(8,128)(2,1)} %get-tuple-element.166.refs_2_), channel_id=1, source_target_pairs={{0,2},{2,4},{4,6},{1,3},{3,5},{5,7},{8,10},{10,12},{12,14},{9,11},... | collective-permute-start | bytes 1327112 | tf_op jit(solution)/shard_map/ppermute | solution.py:928
  124.1 1.8 collective-permute-start.14
  126.4 2.4 own_weight_grad.1
  130.3 6.0 %weight_grad.3 = bf16[1152,640]{1,0:T(8,128)(2,1)} custom-call(s32[23]{0:T(128)S(1)} %copy-done.34, bf16[384,1152]{1,0:T(8,128)(2,1)S(1)} %get-tuple-element.141.down_in_ref.refs_1_, bf16[1152,1152]{1,0:T(8,128)(2,1)} %get-tuple-element.167.refs_2_, bf16[384,640]{1,0:T(8,128)(2,1)S(1)} %copy-done.15, bf16[384,640]{1,0:T(8,128)(2,1)S(1)} %copy-done.17, ...), custom_call_target="tpu_custom_call" | custom-call | flops 2264924 | bytes 6979 | tf_op jit(solution)/shard_map/weight_grad/pallas_call | solution.py:50
  137.1 1.1 broadcast_select_fusion.refs_3_
  139.6 1.7 collective-permute-start.16
  141.4 1.3 collective-permute-start.17
  142.7 13.2 %attend_back.1 = (bf16[384,1152]{1,0:T(8,128)(2,1)S(1)}, f32[2,576]{1,0:T(2,128)S(1)}, bf16[384,432]{1,0:T(8,128)(2,1)S(1)}, bf16[384,432]{1,0:T(8,128)(2,1)S(1)...) custom-call(s32[23]{0:T(128)S(1)} %copy-done.34, bf16[3,768,576]{2,1,0:T(8,128)(2,1)} %copy-done, ...), custom_call_target="tpu_custom_call" | custom-call | flops 3038773 | bytes 9736 | tf_op jit(solution)/shard_map/attend_back/pallas_call | solution.py:50
  163.1 6.6 %weight_grad.4 = bf16[1152,640]{1,0:T(8,128)(2,1)} custom-call(s32[23]{0:T(128)S(1)} %copy-done.34, bf16[3072,640]{1,0:T(8,128)(2,1)} %all-gather.6.cloned.1.call-done.refs_1_, bf16[384,640]{1,0:T(8,128)(2,1)S(1)} %copy-done.9, bf16[384,640]{1,0:T(8,128)(2,1)} %collective-permute-done.14.refs_3_, bf16[384,640]{1,0:T(8,128)(2,1)} %collective-permute-done.15.refs_4_, ...), custom_call_target="tpu_custom_call" | custom-call | flops 2264924 | bytes 7372 | tf_op jit(solution)/shard_map/weight_grad/pallas_call | solution.py:50
  169.9 5.6 %convolution_convert_fusion.2.term_ref = bf16[384,1152]{1,0:T(8,128)(2,1)S(1)} fusion(bf16[384,2304]{1,0:T(8,128)(2,1)} %get-tuple-element.209, bf16[2304,1152]{1,0:T(8,128)(2,1)} %down_ref.1), kind=kOutput, calls=%fused_computation.12 | convolution fusion | flops 2038874112 | bytes 7962624 | tf_op jit(solution)/shard_map/dot_general | solution.py:28
  176.8 5.8 %collective-permute-start.20 = (bf16[384,432]{1,0:T(8,128)(2,1)S(1)}, bf16[384,432]{1,0:T(8,128)(2,1)S(1)}, u32[]{:S(2)}, u32[]{:S(2)}) collective-permute-start(bf16[384,432]{1,0:T(8,128)(2,1)S(1)} %copy-done.47), channel_id=1, source_target_pairs={{0,8},{8,0},{16,24},{24,16},{1,9},{9,1},{17,25},{25,17},{2,10},{10... | collective-permute-start | bytes 995336 | tf_op jit(solution)/shard_map/ppermute | solution.py:918
  182.6 5.0 %collective-permute-done.22.refs_10_ = bf16[144,1152]{1,0:T(8,128)(2,1)S(1)} collective-permute-done((bf16[144,1152]{1,0:T(8,128)(2,1)S(1)}, bf16[144,1152]{1,0:T(8,128)(2,1)S(1)}, u32[]{:S(2)}, u32[]{:S(2)}) %collective-permute-start.22) | collective-permute-done | bytes 331808 | tf_op jit(solution)/shard_map/ppermute | solution.py:918
  188.4 11.3 %collective-permute-done.20.refs_4_ = bf16[384,432]{1,0:T(8,128)(2,1)S(1)} collective-permute-done((bf16[384,432]{1,0:T(8,128)(2,1)S(1)}, bf16[384,432]{1,0:T(8,128)(2,1)S(1)}, u32[]{:S(2)}, u32[]{:S(2)}) %collective-permute-start.20) | collective-permute-done | bytes 331808 | tf_op jit(solution)/shard_map/ppermute | solution.py:918
  199.7 3.1 %input_back.1 = (bf16[384,1152]{1,0:T(8,128)(2,1)S(1)}, f32[3,2,1152]{2,1,0:T(2,128)S(1)}) custom-call(bf16[384,1152]{1,0:T(8,128)(2,1)S(1)} %get-tuple-element.193.term_ref, bf16[384,1152]{1,0:T(8,128)(2,1)} %collective-permute-done.19.other_ref, f32[384,1152]{1,0:T(8,128)S(1)} %copy-done.4, ...), custom_call_target="tpu_custom_call" | custom-call | bytes 5419 | tf_op jit(solution)/shard_map/input_back/pallas_call | solution.py:50
  203.7 3.0 result.1
  207.5 3.9 %collective-permute-start.26 = (bf16[48,576]{1,0:T(8,128)(2,1)S(1)}, bf16[48,576]{1,0:T(8,128)(2,1)S(1)}, u32[]{:S(2)}, u32[]{:S(2)}) collective-permute-start(bf16[48,576]{1,0:T(8,128)(2,1)S(1)} %collect.1), channel_id=1, source_target_pairs={{0,4},{2,6},{4,0},{6,2},{1,5},{3,7},{5,1},{7,3},{8,12},{10,14},{12... | collective-permute-start | bytes 165896 | tf_op jit(solution)/shard_map/ppermute | solution.py:918
  212.1 5.6 %weight_grad.5 = (f32[288,576]{1,0:T(8,128)S(1)}, bf16[288,576]{1,0:T(8,128)(2,1)}, bf16[288,576]{1,0:T(8,128)(2,1)S(1)}, bf16[288,576]{1,0:T(8,128)(2,1)S(1)}) custom-call(s32[23]{0:T(128)S(1)} %copy-done.34, bf16[768,1152]{1,0:T(8,128)(2,1)} %copy-done.6, bf16[1152,1152]{1,0:T(8,128)(2,1)} %get-tuple-element.156.refs_2_, bf16[384,432]{1,0:T(8,128)(2,1)S(1)} %copy-done.21, ...), custom_call_target="tpu_custom_call" | custom-call | flops 1528823 | bytes 8736 | tf_op jit(solution)/shard_map/weight_grad/pallas_call | solution.py:50
  217.8 1.6 collective-permute-start.28
  220.3 1.7 collective-permute-start.32
  222.0 1.4 collective-permute-start.31
  223.4 1.5 collective-permute-start.36
  225.0 4.3 %collective-permute-done.33.refs_5_ = bf16[192,576]{1,0:T(8,128)(2,1)S(1)} collective-permute-done((bf16[192,576]{1,0:T(8,128)(2,1)S(1)}, bf16[192,576]{1,0:T(8,128)(2,1)S(1)}, u32[]{:S(2)}, u32[]{:S(2)}) %collective-permute-start.33) | collective-permute-done | bytes 221216 | tf_op jit(solution)/shard_map/ppermute | solution.py:918
  229.3 2.5 collective-permute-start.35
  231.8 5.1 %collective-permute-done.32.refs_4_ = bf16[192,576]{1,0:T(8,128)(2,1)S(1)} collective-permute-done((bf16[192,576]{1,0:T(8,128)(2,1)S(1)}, bf16[192,576]{1,0:T(8,128)(2,1)S(1)}, u32[]{:S(2)}, u32[]{:S(2)}) %collective-permute-start.32) | collective-permute-done | bytes 221216 | tf_op jit(solution)/shard_map/ppermute | solution.py:918
  237.6 4.9 %collective-permute-start.34 = (bf16[288,640]{1,0:T(8,128)(2,1)}, bf16[288,640]{1,0:T(8,128)(2,1)S(1)}, u32[]{:S(2)}, u32[]{:S(2)}) collective-permute-start(bf16[288,640]{1,0:T(8,128)(2,1)} %reduce-scatter.3.cloned.1.call-done.refs_1_), channel_id=1, source_target_pairs={{0,8},{8,0},{16,24},{24,16},{1,9},{9,1},{17,25},{25,17},{2,10},{10... | collective-permute-start | bytes 1105928 | tf_op jit(solution)/shard_map/ppermute | solution.py:918
  243.6 3.1 %collective-permute-start.30 = (bf16[288,576]{1,0:T(8,128)(2,1)S(1)}, bf16[288,576]{1,0:T(8,128)(2,1)}, u32[]{:S(2)}, u32[]{:S(2)}) collective-permute-start(bf16[288,576]{1,0:T(8,128)(2,1)S(1)} %get-tuple-element.231), channel_id=1, source_target_pairs={{0,6},{2,0},{4,2},{6,4},{1,7},{3,1},{5,3},{7,5},{8,14},{10,8},{12,... | collective-permute-start | bytes 995336 | tf_op jit(solution)/shard_map/ppermute | solution.py:973
  246.6 4.3 %fusion.7 = bf16[1,768,1152]{2,1,0:T(8,128)(2,1)} fusion(bf16[384,1152]{1,0:T(8,128)(2,1)} %copy-done.39, bf16[1,768,1152]{2,1,0:T(8,128)(2,1)} %param.15, pred[768]{0:T(1024)(128)(4,1)S(1)} %broadcast_compare_fusion, s32[384]{0:T(512)S(1)} %subtract_reduce_fusion), kind=kOutput, calls=%fused_computation.10 | convolution fusion | flops 681541632 | bytes 4425984 | tf_op jit(solution)/shard_map/dot_general | solution.py:32
  251.0 2.6 fusion.6
  253.6 3.9 %collective-permute-done.29 = bf16[288,576]{1,0:T(8,128)(2,1)} collective-permute-done((bf16[288,576]{1,0:T(8,128)(2,1)S(1)}, bf16[288,576]{1,0:T(8,128)(2,1)}, u32[]{:S(2)}, u32[]{:S(2)}) %collective-permute-start.29) | collective-permute-done | bytes 331808 | tf_op jit(solution)/shard_map/ppermute | solution.py:973
  257.6 1.3 add_convert_fusion.1.refs_1_
  258.9 1.1 collective-permute-start.40
  260.0 1.9 collective-permute-start.39
  263.4 3.9 %spread.1 = (f32[6,288,576]{2,1,0:T(8,128)}, f32[6,576]{1,0:T(8,128)}, f32[24,576]{1,0:T(8,128)S(1)}, f32[9,6,576]{2,1,0:T(8,128)S(1)}) custom-call(s32[23]{0:T(128)S(1)} %copy-done.34, s32[1536]{0:T(1024)S(1)} %reduce.refs_1_, bf16[192,576]{1,0:T(8,128)(2,1)S(1)} %constant_dynamic-update-slice_fusion.refs_2_, bf16[192,576]{1,0:T(8,128)(2,1)S(1)} %copy-done.32, ...), custom_call_target="tpu_custom_call" | custom-call | bytes 5065 | tf_op jit(solution)/shard_map/spread/pallas_call | solution.py:50
  267.5 4.5 %fusion.9 = f32[18,1152]{1,0:T(8,128)S(1)} fusion(bf16[1152,6,576]{0,2,1:T(8,128)(2,1)} %param.28, bf16[18,6,576]{2,1,0:T(8,128)(2,1)S(1)} %pad_maximum_fusion.1), kind=kOutput, calls=%fused_computation.15 | convolution fusion | flops 143327232 | bytes 8169984 | tf_op jit(solution)/shard_map/sgf,gfd->sd/dot_general | solution.py:1219
  274.8 2.3 join_down.1
  277.9 2.7 join_qkv.1
  280.6 10.1 %all-gather.8.cloned.1.call-done.refs_1_ = bf16[1152,640]{1,0:T(8,128)(2,1)} async-done(((bf16[288,640]{1,0:T(8,128)(2,1)}), bf16[1152,640]{1,0:T(8,128)(2,1)}) %all-gather.8.cloned.1.call-update) | async-done | bytes 1474576 | tf_op jit(solution)/shard_map/all_gather | solution.py:1196
  290.8 1.4 copy-done.7
  292.1 2.2 join_hidden.1
  (229 shorter events, 37.6 us)
Async XLA Ops:
  7.2 92.1 %all-gather.4.cloned.1.call-start = ((), (), s32[]{:S(2)}) async-start(), calls=%async_computation.2 | async-start | bytes 7962624 | tf_op jit(solution)/shard_map/all_gather | solution.py:959
  10.0 69.6 %copy-start.33 = (s32[23]{0:T(128)}, s32[23]{0:T(128)S(1)}, u32[]{:S(2)}) copy-start(s32[23]{0:T(128)S(1)} %plan.1.refs_0_.scalars) | copy-start | bytes 280
  15.2 11.6 %copy-start.53 = (bf16[2,576]{1,0:T(2,128)(2,1)S(1)}, bf16[2,576]{1,0:T(2,128)(2,1)}, u32[]{:S(2)}) copy-start(bf16[2,576]{1,0:T(2,128)(2,1)} %param.21) | copy-start | bytes 6916
  15.2 12.2 %copy-start.54 = (bf16[6,576]{1,0:T(8,128)(2,1)S(1)}, bf16[6,576]{1,0:T(8,128)(2,1)}, u32[]{:S(2)}) copy-start(bf16[6,576]{1,0:T(8,128)(2,1)} %param.29) | copy-start | bytes 20740
  16.3 144.8 %all-gather.6.cloned.1.call-start = ((), (), s32[]{:S(2)}) async-start(), calls=%async_computation.3 | async-start | bytes 4423680 | tf_op jit(solution)/shard_map/all_gather | solution.py:959
  16.3 11.8 %collective-permute-start.5 = (bf16[3,1152]{1,0:T(4,128)(2,1)S(1)}, bf16[3,1152]{1,0:T(4,128)(2,1)S(1)}, u32[]{:S(2)}, u32[]{:S(2)}) collective-permute-start(bf16[3,1152]{1,0:T(4,128)(2,1)S(1)} %get-tuple-element.138.active_ref), channel_id=1, source_target_pairs={{0,24},{8,16},{16,8},{24,0},{1,25},{9,17},{17,9},{25,1},{2,26},{10... | collective-permute-start | bytes 20744 | tf_op jit(solution)/shard_map/ppermute | solution.py:918
  20.3 7.9 %collective-permute-start.4 = (bf16[3,1152]{1,0:T(4,128)(2,1)S(1)}, bf16[3,1152]{1,0:T(4,128)(2,1)S(1)}, u32[]{:S(2)}, u32[]{:S(2)}) collective-permute-start(bf16[3,1152]{1,0:T(4,128)(2,1)S(1)} %get-tuple-element.138.active_ref), channel_id=1, source_target_pairs={{0,16},{8,24},{16,0},{24,8},{1,17},{9,25},{17,1},{25,9},{2,18},{10... | collective-permute-start | bytes 20744 | tf_op jit(solution)/shard_map/ppermute | solution.py:918
  20.8 7.4 %collective-permute-start.3 = (bf16[3,1152]{1,0:T(4,128)(2,1)S(1)}, bf16[3,1152]{1,0:T(4,128)(2,1)S(1)}, u32[]{:S(2)}, u32[]{:S(2)}) collective-permute-start(bf16[3,1152]{1,0:T(4,128)(2,1)S(1)} %get-tuple-element.138.active_ref), channel_id=1, source_target_pairs={{0,8},{8,0},{16,24},{24,16},{1,9},{9,1},{17,25},{25,17},{2,10},{10... | collective-permute-start | bytes 20744 | tf_op jit(solution)/shard_map/ppermute | solution.py:918
  20.9 13.2 %collective-permute-start.1 = (bf16[192,1152]{1,0:T(8,128)(2,1)S(1)}, bf16[192,1152]{1,0:T(8,128)(2,1)S(1)}, u32[]{:S(2)}, u32[]{:S(2)}) collective-permute-start(bf16[192,1152]{1,0:T(8,128)(2,1)S(1)} %constant_dynamic-slice_fusion.1), channel_id=1, source_target_pairs={{2,0},{4,2},{6,4},{3,1},{5,3},{7,5},{10,8},{12,10},{14,12},{11,9},... | collective-permute-start | bytes 1327112 | tf_op jit(solution)/shard_map/ppermute | solution.py:928
  22.2 13.1 %collective-permute-start = (bf16[192,1152]{1,0:T(8,128)(2,1)S(1)}, bf16[192,1152]{1,0:T(8,128)(2,1)S(1)}, u32[]{:S(2)}, u32[]{:S(2)}) collective-permute-start(bf16[192,1152]{1,0:T(8,128)(2,1)S(1)} %constant_dynamic-slice_fusion.1), channel_id=1, source_target_pairs={{0,2},{2,4},{4,6},{1,3},{3,5},{5,7},{8,10},{10,12},{12,14},{9,11},... | collective-permute-start | bytes 1327112 | tf_op jit(solution)/shard_map/ppermute | solution.py:928
  35.4 3.2 %collective-permute-start.2 = (bf16[192,1152]{1,0:T(8,128)(2,1)S(1)}, bf16[192,1152]{1,0:T(8,128)(2,1)S(1)}, u32[]{:S(2)}, u32[]{:S(2)}) collective-permute-start(bf16[192,1152]{1,0:T(8,128)(2,1)S(1)} %broadcast_select_fusion.1), channel_id=1, source_target_pairs={{0,1},{1,0},{2,3},{3,2},{4,5},{5,4},{6,7},{7,6},{8,9},{9,8},{10,11... | collective-permute-start | bytes 1327112 | tf_op jit(solution)/shard_map/ppermute | solution.py:918
  35.6 2.1 collective-permute-start.6
  38.6 18.7 %copy-start.2 = (f32[15,6,1152]{2,1,0:T(8,128)}, f32[15,6,1152]{2,1,0:T(8,128)S(1)}, u32[]{:S(2)}) copy-start(f32[15,6,1152]{2,1,0:T(8,128)S(1)} %pick.1.mod_ref.refs_2_) | copy-start | bytes 1244164
  46.5 10.7 %copy-start.56 = (bf16[1152]{0:T(1024)(128)(2,1)S(1)}, bf16[1152]{0:T(1024)(128)(2,1)}, u32[]{:S(2)}) copy-start(bf16[1152]{0:T(1024)(128)(2,1)} %param.23) | copy-start | bytes 6916
  57.1 3.9 %collective-permute-start.7 = (f32[384,1152]{1,0:T(8,128)S(1)}, f32[384,1152]{1,0:T(8,128)S(1)}, u32[]{:S(2)}, u32[]{:S(2)}) collective-permute-start(f32[384,1152]{1,0:T(8,128)S(1)} %get-tuple-element.142.term_ref), channel_id=1, source_target_pairs={{0,1},{1,0},{2,3},{3,2},{4,5},{5,4},{6,7},{7,6},{8,9},{9,8},{10,11... | collective-permute-start | bytes 5308424 | tf_op jit(solution)/shard_map/ppermute | solution.py:918
  76.5 141.2 %reduce-scatter.3.cloned.1.call-start = ((), (), s32[]{:S(2)}) async-start(), calls=%async_computation.4 | async-start | bytes 1843200 | tf_op jit(solution)/shard_map/reduce_scatter | solution.py:1125
  76.6 18.4 %collective-permute-start.8 = (bf16[384,640]{1,0:T(8,128)(2,1)}, bf16[384,640]{1,0:T(8,128)(2,1)S(1)}, u32[]{:S(2)}, u32[]{:S(2)}) collective-permute-start(bf16[384,640]{1,0:T(8,128)(2,1)} %copy-done.41), channel_id=1, source_target_pairs={{0,8},{8,0},{16,24},{24,16},{1,9},{9,1},{17,25},{25,17},{2,10},{10... | collective-permute-start | bytes 1474568 | tf_op jit(solution)/shard_map/ppermute | solution.py:918
  79.7 17.5 %collective-permute-start.9 = (bf16[384,640]{1,0:T(8,128)(2,1)}, bf16[384,640]{1,0:T(8,128)(2,1)S(1)}, u32[]{:S(2)}, u32[]{:S(2)}) collective-permute-start(bf16[384,640]{1,0:T(8,128)(2,1)} %copy-done.40), channel_id=1, source_target_pairs={{0,16},{8,24},{16,0},{24,8},{1,17},{9,25},{17,1},{25,9},{2,18},{10... | collective-permute-start | bytes 1474568 | tf_op jit(solution)/shard_map/ppermute | solution.py:918
  95.0 12.1 %copy-start.16 = (bf16[384,640]{1,0:T(8,128)(2,1)}, bf16[384,640]{1,0:T(8,128)(2,1)S(1)}, u32[]{:S(2)}) copy-start(bf16[384,640]{1,0:T(8,128)(2,1)S(1)} %collective-permute-done.8.refs_4_) | copy-start | bytes 1474564
  98.0 9.1 %collective-permute-start.10 = (f32[384,1152]{1,0:T(8,128)}, f32[384,1152]{1,0:T(8,128)}, u32[]{:S(2)}, u32[]{:S(2)}) collective-permute-start(f32[384,1152]{1,0:T(8,128)} %get-tuple-element.153.term_ref), channel_id=1, source_target_pairs={{0,1},{1,0},{2,3},{3,2},{4,5},{5,4},{6,7},{7,6},{8,9},{9,8},{10,11... | collective-permute-start | bytes 5308424 | tf_op jit(solution)/shard_map/ppermute | solution.py:918
  98.0 32.3 %collective-permute-start.13 = (bf16[384,640]{1,0:T(8,128)(2,1)}, bf16[384,640]{1,0:T(8,128)(2,1)}, u32[]{:S(2)}, u32[]{:S(2)}) collective-permute-start(bf16[384,640]{1,0:T(8,128)(2,1)} %get-tuple-element.171), channel_id=1, source_target_pairs={{0,24},{8,16},{16,8},{24,0},{1,25},{9,17},{17,9},{25,1},{2,26},{10... | collective-permute-start | bytes 1474568 | tf_op jit(solution)/shard_map/ppermute | solution.py:918
  107.1 19.3 %copy-start.11 = (bf16[384,576]{1,0:T(8,128)(2,1)S(1)}, bf16[384,576]{1,0:T(8,128)(2,1)}, u32[]{:S(2)}) copy-start(bf16[384,576]{1,0:T(8,128)(2,1)} %copy-done.10) | copy-start | bytes 1327108
  107.1 19.3 %copy-start.34 = (s32[23]{0:T(128)S(1)}, s32[23]{0:T(128)}, u32[]{:S(2)}) copy-start(s32[23]{0:T(128)} %copy-done.33) | copy-start | bytes 280
  107.1 23.1 %copy-start.15 = (bf16[384,640]{1,0:T(8,128)(2,1)S(1)}, bf16[384,640]{1,0:T(8,128)(2,1)}, u32[]{:S(2)}) copy-start(bf16[384,640]{1,0:T(8,128)(2,1)} %copy-done.14) | copy-start | bytes 1474564
  107.1 23.1 %copy-start.17 = (bf16[384,640]{1,0:T(8,128)(2,1)S(1)}, bf16[384,640]{1,0:T(8,128)(2,1)}, u32[]{:S(2)}) copy-start(bf16[384,640]{1,0:T(8,128)(2,1)} %copy-done.16) | copy-start | bytes 1474564
  107.2 23.1 %copy-start.19 = (bf16[384,640]{1,0:T(8,128)(2,1)S(1)}, bf16[384,640]{1,0:T(8,128)(2,1)}, u32[]{:S(2)}) copy-start(bf16[384,640]{1,0:T(8,128)(2,1)} %copy-done.18) | copy-start | bytes 1474564
  114.9 21.4 %collective-permute-start.12 = (bf16[384,576]{1,0:T(8,128)(2,1)}, bf16[384,576]{1,0:T(8,128)(2,1)S(1)}, u32[]{:S(2)}, u32[]{:S(2)}) collective-permute-start(bf16[384,576]{1,0:T(8,128)(2,1)} %get-tuple-element.166.refs_2_), channel_id=1, source_target_pairs={{2,0},{4,2},{6,4},{3,1},{5,3},{7,5},{10,8},{12,10},{14,12},{11,9},... | collective-permute-start | bytes 1327112 | tf_op jit(solution)/shard_map/ppermute | solution.py:928
  116.6 20.5 %collective-permute-start.11 = (bf16[384,576]{1,0:T(8,128)(2,1)}, bf16[384,576]{1,0:T(8,128)(2,1)}, u32[]{:S(2)}, u32[]{:S(2)}) collective-permute-start(bf16[384,576]{1,0:T(8,128)(2,1)} %get-tuple-element.166.refs_2_), channel_id=1, source_target_pairs={{0,2},{2,4},{4,6},{1,3},{3,5},{5,7},{8,10},{10,12},{12,14},{9,11},... | collective-permute-start | bytes 1327112 | tf_op jit(solution)/shard_map/ppermute | solution.py:928
  124.1 14.1 %collective-permute-start.14 = (bf16[384,640]{1,0:T(8,128)(2,1)}, bf16[384,640]{1,0:T(8,128)(2,1)}, u32[]{:S(2)}, u32[]{:S(2)}) collective-permute-start(bf16[384,640]{1,0:T(8,128)(2,1)} %get-tuple-element.178), channel_id=1, source_target_pairs={{0,8},{8,0},{16,24},{24,16},{1,9},{9,1},{17,25},{25,17},{2,10},{10... | collective-permute-start | bytes 1474568 | tf_op jit(solution)/shard_map/ppermute | solution.py:918
  125.9 13.1 %collective-permute-start.15 = (bf16[384,640]{1,0:T(8,128)(2,1)}, bf16[384,640]{1,0:T(8,128)(2,1)}, u32[]{:S(2)}, u32[]{:S(2)}) collective-permute-start(bf16[384,640]{1,0:T(8,128)(2,1)} %get-tuple-element.179), channel_id=1, source_target_pairs={{0,16},{8,24},{16,0},{24,8},{1,17},{9,25},{17,1},{25,9},{2,18},{10... | collective-permute-start | bytes 1474568 | tf_op jit(solution)/shard_map/ppermute | solution.py:918
  139.1 114.5 %reduce-scatter.5.cloned.1.call-start = ((), (), s32[]{:S(2)}) async-start(), calls=%async_computation.5 | async-start | bytes 1843200 | tf_op jit(solution)/shard_map/reduce_scatter | solution.py:1139
  139.1 19.7 %collective-permute-start.18 = (bf16[384,640]{1,0:T(8,128)(2,1)}, bf16[384,640]{1,0:T(8,128)(2,1)S(1)}, u32[]{:S(2)}, u32[]{:S(2)}) collective-permute-start(bf16[384,640]{1,0:T(8,128)(2,1)} %get-tuple-element.191), channel_id=1, source_target_pairs={{0,24},{8,16},{16,8},{24,0},{1,25},{9,17},{17,9},{25,1},{2,26},{10... | collective-permute-start | bytes 1474568 | tf_op jit(solution)/shard_map/ppermute | solution.py:918
  139.6 20.0 %collective-permute-start.16 = (bf16[144,1152]{1,0:T(8,128)(2,1)}, bf16[144,1152]{1,0:T(8,128)(2,1)S(1)}, u32[]{:S(2)}, u32[]{:S(2)}) collective-permute-start(bf16[144,1152]{1,0:T(8,128)(2,1)} %get-tuple-element.186), channel_id=1, source_target_pairs={{0,8},{8,0},{16,24},{24,16},{1,9},{9,1},{17,25},{25,17},{2,10},{10... | collective-permute-start | bytes 995336 | tf_op jit(solution)/shard_map/ppermute | solution.py:918
  141.4 19.0 %collective-permute-start.17 = (bf16[144,1152]{1,0:T(8,128)(2,1)}, bf16[144,1152]{1,0:T(8,128)(2,1)S(1)}, u32[]{:S(2)}, u32[]{:S(2)}) collective-permute-start(bf16[144,1152]{1,0:T(8,128)(2,1)} %get-tuple-element.187), channel_id=1, source_target_pairs={{0,16},{8,24},{16,0},{24,8},{1,17},{9,25},{17,1},{25,9},{2,18},{10... | collective-permute-start | bytes 995336 | tf_op jit(solution)/shard_map/ppermute | solution.py:918
  161.1 38.6 %collective-permute-start.19 = (bf16[384,1152]{1,0:T(8,128)(2,1)S(1)}, bf16[384,1152]{1,0:T(8,128)(2,1)}, u32[]{:S(2)}, u32[]{:S(2)}) collective-permute-start(bf16[384,1152]{1,0:T(8,128)(2,1)S(1)} %get-tuple-element.193.term_ref), channel_id=1, source_target_pairs={{0,1},{1,0},{2,3},{3,2},{4,5},{5,4},{6,7},{7,6},{8,9},{9,8},{10,11... | collective-permute-start | bytes 2654216 | tf_op jit(solution)/shard_map/ppermute | solution.py:918
  169.8 17.9 %copy-start.43 = (bf16[384,432]{1,0:T(8,128)(2,1)S(1)}, bf16[384,432]{1,0:T(8,128)(2,1)}, u32[]{:S(2)}) copy-start(bf16[384,432]{1,0:T(8,128)(2,1)} %copy-done.42) | copy-start | bytes 995332
  169.8 18.6 %copy-start.57 = (bf16[1152]{0:T(1024)(128)(2,1)S(1)}, bf16[1152]{0:T(1024)(128)(2,1)}, u32[]{:S(2)}) copy-start(bf16[1152]{0:T(1024)(128)(2,1)} %param.27) | copy-start | bytes 6916
  169.8 121.0 %all-gather.8.cloned.1.call-start = ((), (), s32[]{:S(2)}) async-start(), calls=%async_computation.6 | async-start | bytes 1843200 | tf_op jit(solution)/shard_map/all_gather | solution.py:1196
  169.9 12.7 %copy-start.45 = (bf16[384,432]{1,0:T(8,128)(2,1)S(1)}, bf16[384,432]{1,0:T(8,128)(2,1)}, u32[]{:S(2)}) copy-start(bf16[384,432]{1,0:T(8,128)(2,1)} %copy-done.44) | copy-start | bytes 995332
  169.9 29.8 %copy-start.4 = (f32[384,1152]{1,0:T(8,128)S(1)}, f32[384,1152]{1,0:T(8,128)}, u32[]{:S(2)}) copy-start(f32[384,1152]{1,0:T(8,128)} %copy-done.3) | copy-start | bytes 5308420
  175.5 28.2 %collective-permute-start.24 = (bf16[384,1152]{1,0:T(8,128)(2,1)S(1)}, bf16[384,1152]{1,0:T(8,128)(2,1)S(1)}, u32[]{:S(2)}, u32[]{:S(2)}) collective-permute-start(bf16[384,1152]{1,0:T(8,128)(2,1)S(1)} %convolution_convert_fusion.2.term_ref), channel_id=1, source_target_pairs={{0,1},{1,0},{2,3},{3,2},{4,5},{5,4},{6,7},{7,6},{8,9},{9,8},{10,11... | collective-permute-start | bytes 2654216 | tf_op jit(solution)/shard_map/ppermute | solution.py:918
  176.1 11.6 %collective-permute-start.22 = (bf16[144,1152]{1,0:T(8,128)(2,1)S(1)}, bf16[144,1152]{1,0:T(8,128)(2,1)S(1)}, u32[]{:S(2)}, u32[]{:S(2)}) collective-permute-start(bf16[144,1152]{1,0:T(8,128)(2,1)S(1)} %copy-done.49), channel_id=1, source_target_pairs={{0,24},{8,16},{16,8},{24,0},{1,25},{9,17},{17,9},{25,1},{2,26},{10... | collective-permute-start | bytes 995336 | tf_op jit(solution)/shard_map/ppermute | solution.py:918
  176.8 22.9 %collective-permute-start.20 = (bf16[384,432]{1,0:T(8,128)(2,1)S(1)}, bf16[384,432]{1,0:T(8,128)(2,1)S(1)}, u32[]{:S(2)}, u32[]{:S(2)}) collective-permute-start(bf16[384,432]{1,0:T(8,128)(2,1)S(1)} %copy-done.47), channel_id=1, source_target_pairs={{0,8},{8,0},{16,24},{24,16},{1,9},{9,1},{17,25},{25,17},{2,10},{10... | collective-permute-start | bytes 995336 | tf_op jit(solution)/shard_map/ppermute | solution.py:918
  182.6 17.1 %collective-permute-start.21 = (bf16[384,432]{1,0:T(8,128)(2,1)S(1)}, bf16[384,432]{1,0:T(8,128)(2,1)S(1)}, u32[]{:S(2)}, u32[]{:S(2)}) collective-permute-start(bf16[384,432]{1,0:T(8,128)(2,1)S(1)} %copy-done.45), channel_id=1, source_target_pairs={{0,16},{8,24},{16,0},{24,8},{1,17},{9,25},{17,1},{25,9},{2,18},{10... | collective-permute-start | bytes 995336 | tf_op jit(solution)/shard_map/ppermute | solution.py:918
  187.6 19.8 %collective-permute-start.23 = (bf16[384,432]{1,0:T(8,128)(2,1)S(1)}, bf16[384,432]{1,0:T(8,128)(2,1)S(1)}, u32[]{:S(2)}, u32[]{:S(2)}) collective-permute-start(bf16[384,432]{1,0:T(8,128)(2,1)S(1)} %copy-done.43), channel_id=1, source_target_pairs={{0,24},{8,16},{16,8},{24,0},{1,25},{9,17},{17,9},{25,1},{2,26},{10... | collective-permute-start | bytes 995336 | tf_op jit(solution)/shard_map/ppermute | solution.py:918
  206.7 11.0 %copy-start.39 = (bf16[384,1152]{1,0:T(8,128)(2,1)}, bf16[384,1152]{1,0:T(8,128)(2,1)S(1)}, u32[]{:S(2)}) copy-start(bf16[384,1152]{1,0:T(8,128)(2,1)S(1)} %get-tuple-element.236) | copy-start | bytes 2654212
  207.4 10.3 %collective-permute-start.27 = (bf16[48,576]{1,0:T(8,128)(2,1)S(1)}, bf16[48,576]{1,0:T(8,128)(2,1)S(1)}, u32[]{:S(2)}, u32[]{:S(2)}) collective-permute-start(bf16[48,576]{1,0:T(8,128)(2,1)S(1)} %collect.1), channel_id=1, source_target_pairs={{0,6},{2,4},{4,2},{6,0},{1,7},{3,5},{5,3},{7,1},{8,14},{10,12},{12... | collective-permute-start | bytes 165896 | tf_op jit(solution)/shard_map/ppermute | solution.py:918
  207.5 10.2 %collective-permute-start.26 = (bf16[48,576]{1,0:T(8,128)(2,1)S(1)}, bf16[48,576]{1,0:T(8,128)(2,1)S(1)}, u32[]{:S(2)}, u32[]{:S(2)}) collective-permute-start(bf16[48,576]{1,0:T(8,128)(2,1)S(1)} %collect.1), channel_id=1, source_target_pairs={{0,4},{2,6},{4,0},{6,2},{1,5},{3,7},{5,1},{7,3},{8,12},{10,14},{12... | collective-permute-start | bytes 165896 | tf_op jit(solution)/shard_map/ppermute | solution.py:918
  211.4 6.3 %collective-permute-start.25 = (bf16[48,576]{1,0:T(8,128)(2,1)S(1)}, bf16[48,576]{1,0:T(8,128)(2,1)S(1)}, u32[]{:S(2)}, u32[]{:S(2)}) collective-permute-start(bf16[48,576]{1,0:T(8,128)(2,1)S(1)} %collect.1), channel_id=1, source_target_pairs={{0,2},{2,0},{4,6},{6,4},{1,3},{3,1},{5,7},{7,5},{8,10},{10,8},{12,... | collective-permute-start | bytes 165896 | tf_op jit(solution)/shard_map/ppermute | solution.py:918
  217.8 25.8 %collective-permute-start.28 = (bf16[288,576]{1,0:T(8,128)(2,1)}, bf16[288,576]{1,0:T(8,128)(2,1)S(1)}, u32[]{:S(2)}, u32[]{:S(2)}) collective-permute-start(bf16[288,576]{1,0:T(8,128)(2,1)} %get-tuple-element.229), channel_id=1, source_target_pairs={{0,2},{2,4},{4,6},{6,0},{1,3},{3,5},{5,7},{7,1},{8,10},{10,12},{12... | collective-permute-start | bytes 995336 | tf_op jit(solution)/shard_map/ppermute | solution.py:973
  219.4 9.9 %collective-permute-start.33 = (bf16[192,576]{1,0:T(8,128)(2,1)S(1)}, bf16[192,576]{1,0:T(8,128)(2,1)S(1)}, u32[]{:S(2)}, u32[]{:S(2)}) collective-permute-start(bf16[192,576]{1,0:T(8,128)(2,1)S(1)} %constant_dynamic-update-slice_fusion.refs_2_), channel_id=1, source_target_pairs={{0,24},{8,16},{16,8},{24,0},{1,25},{9,17},{17,9},{25,1},{2,26},{10... | collective-permute-start | bytes 663560 | tf_op jit(solution)/shard_map/ppermute | solution.py:918
  220.3 16.6 %collective-permute-start.32 = (bf16[192,576]{1,0:T(8,128)(2,1)S(1)}, bf16[192,576]{1,0:T(8,128)(2,1)S(1)}, u32[]{:S(2)}, u32[]{:S(2)}) collective-permute-start(bf16[192,576]{1,0:T(8,128)(2,1)S(1)} %constant_dynamic-update-slice_fusion.refs_2_), channel_id=1, source_target_pairs={{0,16},{8,24},{16,0},{24,8},{1,17},{9,25},{17,1},{25,9},{2,18},{10... | collective-permute-start | bytes 663560 | tf_op jit(solution)/shard_map/ppermute | solution.py:918
  222.0 20.5 %collective-permute-start.31 = (bf16[192,576]{1,0:T(8,128)(2,1)S(1)}, bf16[192,576]{1,0:T(8,128)(2,1)S(1)}, u32[]{:S(2)}, u32[]{:S(2)}) collective-permute-start(bf16[192,576]{1,0:T(8,128)(2,1)S(1)} %constant_dynamic-update-slice_fusion.refs_2_), channel_id=1, source_target_pairs={{0,8},{8,0},{16,24},{24,16},{1,9},{9,1},{17,25},{25,17},{2,10},{10... | collective-permute-start | bytes 663560 | tf_op jit(solution)/shard_map/ppermute | solution.py:918
  223.4 27.6 %copy-start.38 = (bf16[384,1152]{1,0:T(8,128)(2,1)S(1)}, bf16[384,1152]{1,0:T(8,128)(2,1)}, u32[]{:S(2)}) copy-start(bf16[384,1152]{1,0:T(8,128)(2,1)} %copy-done.37) | copy-start | bytes 2654212
  223.4 27.6 %copy-start.59 = (bf16[1,768,1152]{2,1,0:T(8,128)(2,1)S(1)}, bf16[1,768,1152]{2,1,0:T(8,128)(2,1)}, u32[]{:S(2)}) copy-start(bf16[1,768,1152]{2,1,0:T(8,128)(2,1)} %param.19) | copy-start | bytes 5308420
  223.4 34.2 %collective-permute-start.36 = (bf16[288,640]{1,0:T(8,128)(2,1)}, bf16[288,640]{1,0:T(8,128)(2,1)S(1)}, u32[]{:S(2)}, u32[]{:S(2)}) collective-permute-start(bf16[288,640]{1,0:T(8,128)(2,1)} %reduce-scatter.3.cloned.1.call-done.refs_1_), channel_id=1, source_target_pairs={{0,24},{8,16},{16,8},{24,0},{1,25},{9,17},{17,9},{25,1},{2,26},{10... | collective-permute-start | bytes 1105928 | tf_op jit(solution)/shard_map/ppermute | solution.py:918
  229.3 28.3 %collective-permute-start.35 = (bf16[288,640]{1,0:T(8,128)(2,1)}, bf16[288,640]{1,0:T(8,128)(2,1)S(1)}, u32[]{:S(2)}, u32[]{:S(2)}) collective-permute-start(bf16[288,640]{1,0:T(8,128)(2,1)} %reduce-scatter.3.cloned.1.call-done.refs_1_), channel_id=1, source_target_pairs={{0,16},{8,24},{16,0},{24,8},{1,17},{9,25},{17,1},{25,9},{2,18},{10... | collective-permute-start | bytes 1105928 | tf_op jit(solution)/shard_map/ppermute | solution.py:918
  237.6 19.9 %collective-permute-start.34 = (bf16[288,640]{1,0:T(8,128)(2,1)}, bf16[288,640]{1,0:T(8,128)(2,1)S(1)}, u32[]{:S(2)}, u32[]{:S(2)}) collective-permute-start(bf16[288,640]{1,0:T(8,128)(2,1)} %reduce-scatter.3.cloned.1.call-done.refs_1_), channel_id=1, source_target_pairs={{0,8},{8,0},{16,24},{24,16},{1,9},{9,1},{17,25},{25,17},{2,10},{10... | collective-permute-start | bytes 1105928 | tf_op jit(solution)/shard_map/ppermute | solution.py:918
  242.5 15.0 %collective-permute-start.29 = (bf16[288,576]{1,0:T(8,128)(2,1)S(1)}, bf16[288,576]{1,0:T(8,128)(2,1)}, u32[]{:S(2)}, u32[]{:S(2)}) collective-permute-start(bf16[288,576]{1,0:T(8,128)(2,1)S(1)} %get-tuple-element.230), channel_id=1, source_target_pairs={{0,4},{2,6},{4,0},{6,2},{1,5},{3,7},{5,1},{7,3},{8,12},{10,14},{12... | collective-permute-start | bytes 995336 | tf_op jit(solution)/shard_map/ppermute | solution.py:973
  243.6 14.0 %collective-permute-start.30 = (bf16[288,576]{1,0:T(8,128)(2,1)S(1)}, bf16[288,576]{1,0:T(8,128)(2,1)}, u32[]{:S(2)}, u32[]{:S(2)}) collective-permute-start(bf16[288,576]{1,0:T(8,128)(2,1)S(1)} %get-tuple-element.231), channel_id=1, source_target_pairs={{0,6},{2,0},{4,2},{6,4},{1,7},{3,1},{5,3},{7,5},{8,14},{10,8},{12,... | collective-permute-start | bytes 995336 | tf_op jit(solution)/shard_map/ppermute | solution.py:973
  258.9 19.0 %collective-permute-start.40 = (bf16[288,576]{1,0:T(8,128)(2,1)S(1)}, bf16[288,576]{1,0:T(8,128)(2,1)S(1)}, u32[]{:S(2)}, u32[]{:S(2)}) collective-permute-start(bf16[288,576]{1,0:T(8,128)(2,1)S(1)} %add_convert_fusion.1.refs_1_), channel_id=1, source_target_pairs={{0,24},{8,16},{16,8},{24,0},{1,25},{9,17},{17,9},{25,1},{2,26},{10... | collective-permute-start | bytes 995336 | tf_op jit(solution)/shard_map/ppermute | solution.py:918
  260.0 17.9 %collective-permute-start.39 = (bf16[288,576]{1,0:T(8,128)(2,1)S(1)}, bf16[288,576]{1,0:T(8,128)(2,1)S(1)}, u32[]{:S(2)}, u32[]{:S(2)}) collective-permute-start(bf16[288,576]{1,0:T(8,128)(2,1)S(1)} %add_convert_fusion.1.refs_1_), channel_id=1, source_target_pairs={{0,16},{8,24},{16,0},{24,8},{1,17},{9,25},{17,1},{25,9},{2,18},{10... | collective-permute-start | bytes 995336 | tf_op jit(solution)/shard_map/ppermute | solution.py:918
  262.0 15.9 %collective-permute-start.38 = (bf16[288,576]{1,0:T(8,128)(2,1)S(1)}, bf16[288,576]{1,0:T(8,128)(2,1)S(1)}, u32[]{:S(2)}, u32[]{:S(2)}) collective-permute-start(bf16[288,576]{1,0:T(8,128)(2,1)S(1)} %add_convert_fusion.1.refs_1_), channel_id=1, source_target_pairs={{0,8},{8,0},{16,24},{24,16},{1,9},{9,1},{17,25},{25,17},{2,10},{10... | collective-permute-start | bytes 995336 | tf_op jit(solution)/shard_map/ppermute | solution.py:918
  272.0 5.2 %collective-permute-start.37 = (f32[9,1152]{1,0:T(8,128)S(1)}, f32[9,1152]{1,0:T(8,128)S(1)}, u32[]{:S(2)}, u32[]{:S(2)}) collective-permute-start(f32[9,1152]{1,0:T(8,128)S(1)} %slice_add_fusion), channel_id=1, source_target_pairs={{0,1},{1,0},{2,3},{3,2},{4,5},{5,4},{6,7},{7,6},{8,9},{9,8},{10,11... | collective-permute-start | bytes 124424 | tf_op jit(solution)/shard_map/ppermute | solution.py:918
  (42 other events, 127.9 us)
Sparse Core Ops, SparseCore 0:
  16.4 51.5 all-gather.3
  76.7 48.2 all-gather.5
  139.2 30.9 reduce-scatter.2
  173.1 34.2 reduce-scatter.4
  253.7 36.9 all-gather.7
